TPU v7x, 512 devices: a whole 4x4x16 slice. The times are simulated.
512 devices in a mesh: seq: 16 (over y, x), mp: 32 (over z, core).
Axes of the slice: x: 4, y: 4, z: 16, core: 2. Of those that a mesh axis runs over, the one named last changes fastest.
Arguments:
- queries: bfloat16 [2048, 8192], P('seq', 'mp'), may hold values from -3 to 3
- key_rows: bfloat16 [2048, 8192], P('seq', 'mp'), may hold values from -1.25 to 1.25
- value_rows: bfloat16 [2048, 8192], P('seq', 'mp'), may hold values from -4 to 4
- decay_rates: float32 [64], P('mp'), may hold values from 5e-05 to 0.001
- w_out: bfloat16 [8192, 3072], P('mp'), may hold values from -0.125 to 0.125
- inputs: bfloat16 [2048, 3072], P(('seq', 'mp')), may hold values from -4 to 4
- cotangent: bfloat16 [2048, 3072], P(('seq', 'mp')), may hold values from -6 to 6
- norm_gain: float32 [3072], replicated, may hold values from 0.5 to 1.5
- expert_ids: int32 [2048, 2], P('seq'), may hold values from 0 to 15, all different within a row; in each aligned block of 128 rows (0 to 127, 128 to 255, ...) at most 32 rows name the same one
- gate_weights: float32 [2048, 2], P('seq'), may hold values from 0.1 to 0.9
- w_gate: bfloat16 [16, 3072, 4608], P('seq', None, 'mp'), may hold values from -0.109375 to 0.109375
- w_up: bfloat16 [16, 3072, 4608], P('seq', None, 'mp'), may hold values from -0.109375 to 0.109375
- w_down: bfloat16 [16, 4608, 3072], P('seq', 'mp'), may hold values from -0.09375 to 0.09375
Outputs:
- query_grad: bfloat16 [2048, 8192], P('seq', 'mp')
- key_grad: bfloat16 [2048, 8192], P('seq', 'mp')
- value_grad: bfloat16 [2048, 8192], P('seq', 'mp')
- input_grad: bfloat16 [2048, 3072], P(('seq', 'mp'))
Inputs may be any that keep to these rules, and one draw needn't show every extreme that they name: `expert_ids`: A token's two experts differ. Among the 128 tokens of one index of seq no expert is named by more than 32 tokens, a bound that some block reaches.
All inputs are finite; a program needn't handle non-finite values.
Results may differ from a plain program's by a relative error of at most 0.025.
Values may be sent and summed in bfloat16 or wider, within the bound.
No kernel may reach another device: no remote copies, remote signals or barrier semaphores. Data moves between devices by JAX's collectives and lax.ppermute only.
A program may use at most 64 MiB of HBM per device.

v0:
```python
import jax
import jax.numpy as jnp
from jax import lax
from jax.sharding import PartitionSpec as P

EPSILON = 1e-06
HIGHEST_PRECISION = lax.Precision.HIGHEST


def carried_in(x, axis, combine, identity, reverse):
    peers, mine = (lax.axis_size(axis), lax.axis_index(axis))
    everything = jax.tree.map(lambda part: lax.all_gather(part, axis), x)
    start = jax.tree.map(
        lambda part, zero: jnp.broadcast_to(jnp.asarray(zero, part.dtype), part.shape), x, identity
    )

    def lap(k, before):
        at = peers - 1 - k if reverse else k
        reached = at > mine if reverse else at < mine
        new = combine(before, jax.tree.map(lambda part: part[at], everything))
        return jax.tree.map(lambda a, b: jnp.where(reached, a, b), new, before)

    return lax.fori_loop(0, peers, lap, start)


def decay_tables(decay_rates, length):
    places = jnp.arange(length).astype(jnp.float32)
    offset = places[:, None] - places[None, :]
    causal = offset >= 0
    clipped = jnp.where(causal, offset, 0.0)
    decay_band = jnp.where(causal[None], jnp.exp(-decay_rates[:, None, None] * clipped[None]), 0.0)
    head_decay = jnp.exp(-decay_rates[:, None] * places[None, :])
    tail_decay = jnp.exp(-decay_rates[:, None] * (length - 1.0 - places)[None, :])
    return (decay_band, head_decay, tail_decay)


def combine_states(earlier, later):
    return (earlier[0] * later[0], later[0][:, None, None] * earlier[1] + later[1])


def body(
    queries,
    key_rows,
    value_rows,
    decay_rates,
    w_out,
    inputs,
    cotangent,
    norm_gain,
    expert_ids,
    gate_weights,
    w_gate,
    w_up,
    w_down,
):
    length = queries.shape[0]
    head_count = decay_rates.shape[0]
    head_size = queries.shape[1] // head_count
    model_width = w_out.shape[1]
    tok_share = inputs.shape[0]
    seq_count = lax.axis_size("seq")
    mp_count = lax.axis_size("mp")
    mp_place = lax.axis_index("mp")

    def to_heads(matrix):
        return matrix.astype(jnp.float32).reshape(length, head_count, head_size).transpose(1, 0, 2)

    def from_heads(blocks):
        return blocks.transpose(1, 0, 2).reshape(length, head_count * head_size)

    query_heads = to_heads(queries)
    key_heads = to_heads(key_rows)
    value_heads = to_heads(value_rows)
    decay_band, head_decay, tail_decay = decay_tables(decay_rates, length)
    block_decay = jnp.exp(-decay_rates * length)
    step_decay = jnp.exp(-decay_rates)
    local_state = jnp.einsum(
        "ht,htd,hte->hde",
        step_decay[:, None] * tail_decay,
        key_heads,
        value_heads,
        precision=HIGHEST_PRECISION,
    )
    zero_state = jnp.zeros_like(local_state)
    identity = (jnp.ones_like(block_decay), zero_state)
    _, entering = carried_in((block_decay, local_state), "seq", combine_states, identity, False)
    scores = (
        jnp.einsum("htd,hsd->hts", query_heads, key_heads, precision=HIGHEST_PRECISION) * decay_band
    )
    attended = jnp.einsum("hts,hse->hte", scores, value_heads, precision=HIGHEST_PRECISION)
    attended = attended + head_decay[:, :, None] * jnp.einsum(
        "htd,hde->hte", query_heads, entering, precision=HIGHEST_PRECISION
    )
    attended_b = from_heads(attended).astype(jnp.bfloat16)
    mixed = lax.psum_scatter(
        jnp.dot(attended_b, w_out, preferred_element_type=jnp.float32).astype(jnp.bfloat16),
        "mp",
        scatter_dimension=0,
        tiled=True,
    ).astype(jnp.float32)
    stream = inputs.astype(jnp.float32) + mixed
    inverse = lax.rsqrt(jnp.mean(stream * stream, axis=1, keepdims=True) + EPSILON)
    normed = stream * inverse
    expert_in = (normed * norm_gain).astype(jnp.bfloat16)
    group_in, group_cot = (
        lax.all_gather(expert_in, "mp", axis=0, tiled=True),
        lax.all_gather(cotangent, "mp", axis=0, tiled=True),
    )
    capacity = mp_count * max(1, 4 * length // (seq_count * mp_count))
    slot_share = capacity // mp_count
    labels = jnp.arange(seq_count, dtype=jnp.int32)
    first_pick = expert_ids[:, 0:1] == labels[None, :]
    second_pick = expert_ids[:, 1:2] == labels[None, :]
    chosen = (first_pick | second_pick).astype(jnp.int32)
    weight = jnp.where(first_pick, gate_weights[:, 0:1], 0.0) + jnp.where(
        second_pick, gate_weights[:, 1:2], 0.0
    )
    ranking = jnp.cumsum(chosen, axis=0) - 1
    slot_ids = jnp.arange(capacity, dtype=jnp.int32)
    placed = (chosen.T[:, None, :] == 1) & (ranking.T[:, None, :] == slot_ids[None, :, None])
    token_places = jnp.arange(length, dtype=jnp.int32)
    slot_token = jnp.sum(jnp.where(placed, token_places[None, None, :], 0), axis=2)
    slot_weight = jnp.sum(jnp.where(placed, weight.T[:, None, :], 0.0), axis=2)
    gate_block = w_gate[0]
    up_block = w_up[0]
    down_block = w_down[0]
    slot_start = mp_place * slot_share
    own_token = lax.dynamic_slice_in_dim(slot_token, slot_start, slot_share, 1)
    own_weight = lax.dynamic_slice_in_dim(slot_weight, slot_start, slot_share, 1)
    taken_in = jnp.take(group_in, own_token, axis=0)
    taken_cot = jnp.take(group_cot, own_token, axis=0).astype(jnp.float32)
    weighted = (own_weight[:, :, None] * taken_cot).astype(jnp.bfloat16)
    outgoing = jnp.stack([taken_in, weighted], axis=2)
    arrived = lax.all_to_all(outgoing, "seq", split_axis=0, concat_axis=0, tiled=True)
    slot_data = lax.all_gather(arrived[None], "mp", axis=0, tiled=True)
    leading = slot_data.shape[:-2]
    flattened = slot_data.reshape(-1, 2, model_width)
    rows_in = flattened[:, 0, :]
    rows_cot = flattened[:, 1, :]
    gate_pre = jnp.dot(rows_in, gate_block, preferred_element_type=jnp.float32)
    up_pre = jnp.dot(rows_in, up_block, preferred_element_type=jnp.float32)
    hidden_grad = lax.dot_general(
        rows_cot, down_block, (((1,), (1,)), ((), ())), preferred_element_type=jnp.float32
    )
    sigma = jax.nn.sigmoid(gate_pre)
    gate_grad = (hidden_grad * up_pre * sigma * (1.0 + gate_pre * (1.0 - sigma))).astype(
        jnp.bfloat16
    )
    up_grad = (hidden_grad * gate_pre * sigma).astype(jnp.bfloat16)
    result = lax.dot_general(
        gate_grad, gate_block, (((1,), (1,)), ((), ())), preferred_element_type=jnp.float32
    )
    result = result + lax.dot_general(
        up_grad, up_block, (((1,), (1,)), ((), ())), preferred_element_type=jnp.float32
    )
    partial_value = result.reshape(leading + (model_width,))
    summed = lax.psum_scatter(
        partial_value.astype(jnp.bfloat16), "mp", scatter_dimension=0, tiled=True
    ).astype(jnp.float32)[0]
    returned = lax.all_to_all(
        summed.astype(jnp.bfloat16), "seq", split_axis=0, concat_axis=0, tiled=True
    )
    all_slots = lax.all_gather(returned, "mp", axis=1, tiled=True)
    own_slots = lax.dynamic_slice_in_dim(placed, mp_place * tok_share, tok_share, 2)
    expert_grad = jnp.einsum(
        "ect,ecd->td", own_slots.astype(jnp.bfloat16), all_slots, preferred_element_type=jnp.float32
    )
    scaled = expert_grad * norm_gain
    stream_grad = inverse * (
        scaled - normed * jnp.mean(scaled * normed, axis=1, keepdims=True)
    ) + cotangent.astype(jnp.float32)
    input_grad = stream_grad.astype(jnp.bfloat16)
    attended_grad = lax.dot_general(
        lax.all_gather(input_grad, "mp", axis=0, tiled=True),
        w_out,
        (((1,), (1,)), ((), ())),
        preferred_element_type=jnp.float32,
    )
    grad_heads = to_heads(attended_grad)
    local_adjoint = jnp.einsum(
        "ht,htd,hte->hde",
        step_decay[:, None] * head_decay,
        query_heads,
        grad_heads,
        precision=HIGHEST_PRECISION,
    )
    _, leaving = carried_in((block_decay, local_adjoint), "seq", combine_states, identity, True)
    grad_scores = (
        jnp.einsum("hte,hse->hts", grad_heads, value_heads, precision=HIGHEST_PRECISION)
        * decay_band
    )
    query_part = jnp.einsum("hts,hsd->htd", grad_scores, key_heads, precision=HIGHEST_PRECISION)
    query_part = query_part + head_decay[:, :, None] * jnp.einsum(
        "hte,hde->htd", grad_heads, entering, precision=HIGHEST_PRECISION
    )
    key_part = jnp.einsum("hts,htd->hsd", grad_scores, query_heads, precision=HIGHEST_PRECISION)
    key_part = key_part + tail_decay[:, :, None] * jnp.einsum(
        "hse,hde->hsd", value_heads, leaving, precision=HIGHEST_PRECISION
    )
    value_part = jnp.einsum("hts,hte->hse", scores, grad_heads, precision=HIGHEST_PRECISION)
    value_part = value_part + tail_decay[:, :, None] * jnp.einsum(
        "hsd,hde->hse", key_heads, leaving, precision=HIGHEST_PRECISION
    )
    query_grad = from_heads(query_part).astype(jnp.bfloat16)
    key_grad = from_heads(key_part).astype(jnp.bfloat16)
    value_grad = from_heads(value_part).astype(jnp.bfloat16)
    return (query_grad, key_grad, value_grad, input_grad)


def solution(mesh):
    placed = (
        P("seq", "mp"),
        P("seq", "mp"),
        P("seq", "mp"),
        P("mp"),
        P("mp", None),
        P(("seq", "mp"), None),
        P(("seq", "mp"), None),
        P(),
        P("seq", None),
        P("seq", None),
        P("seq", None, "mp"),
        P("seq", None, "mp"),
        P("seq", "mp", None),
    )
    return jax.shard_map(
        body,
        mesh=mesh,
        in_specs=placed,
        out_specs=(P("seq", "mp"), P("seq", "mp"), P("seq", "mp"), P(("seq", "mp"), None)),
        check_vma=False,
    )
```

profile of v0, /device:TPU:1, one launch (start us, length us, event | category | flops | bytes accessed | tf_op | source)
XLA Modules:
  0.0 785.2 jit_solution(13098843725600787549)
XLA Ops:
  7.3 1.4 dynamic-slice
  10.7 1.9 fusion.39
  12.7 34.4 %all-reduce = f32[32]{0:T(128)S(1)} all-reduce(f32[32]{0:T(128)S(1)} %get-tuple-element.318), channel_id=2, replica_groups=mesh['seq'=16,'mp'=32] {'seq'}, use_global_device_ids=true, to_apply=%add | all-reduce | flops 32 | bytes 256
  49.2 46.4 %all-gather.5 = bf16[32,4,3072]{2,1,0:T(4,128)(2,1)S(1)} all-gather(bf16[1,4,3072]{2,1,0:T(4,128)(2,1)} %bitcast.235), channel_id=1, replica_groups=mesh['seq'=16,'mp'=32] {'mp'}, dimensions={0}, use_global_device_ids=true | all-gather | bytes 811008 | tf_op jit(solution)/shard_map/all_gather | solution.py:107
  95.8 1.3 dynamic-slice.1
  99.3 1.2 select_reduce_fusion
  102.0 16.5 %while.30 = (s32[]{:T(128)}, f32[2,128,128]{2,1,0:T(8,128)S(1)}, s32[]{:T(128)}, f32[16,2]{1,0:T(8,128)S(1)}, f32[16,2,128,128]{3,2,1,0:T(8,128)}, /*index=5*/s32[]{:T(128)}, s32[]{:T(128)}) while((s32[]{:T(128)}, f32[2,128,128]{2,1,0:T(8,128)S(1)}, s32[]{:T(128)}, f32[16,2]{1,0:T(8,128)S(1)}, f32[16,2,128,128]{3,2,1,0:T(8,128)}, ...), condition=%wide.region_1.2_spmd.clone, body=%wide.region_0.1_spmd.clone.sunk | while | flops 131076 | bytes 393345 | solution.py:23
  102.0 1.0 fusion.95
  103.1 1.0 fusion.95
  104.1 1.0 fusion.95
  105.1 1.0 fusion.95
  106.2 1.0 fusion.95
  107.2 1.0 fusion.95
  108.2 1.0 fusion.95
  109.3 1.0 fusion.95
  110.3 1.0 fusion.95
  111.3 1.0 fusion.95
  112.4 1.0 fusion.95
  113.4 1.0 fusion.95
  114.4 1.0 fusion.95
  115.5 1.0 fusion.95
  116.5 1.0 fusion.95
  117.5 1.0 fusion.95
  119.1 1.3 convolution_convert_fusion
  120.6 200.2 %all-reduce.4.cloned.1.call-done = bf16[128,3072]{1,0:T(8,128)(2,1)} async-done(((bf16[128,3072]{1,0:T(8,128)(2,1)}), bf16[128,3072]{1,0:T(8,128)(2,1)}) %all-reduce.4.cloned.1.call-update) | async-done | bytes 786448
  322.7 30.4 %all-gather.4 = bf16[32,4,3072]{2,1,0:T(4,128)(2,1)S(1)} all-gather(bf16[1,4,3072]{2,1,0:T(4,128)(2,1)S(1)} %fusion.58), channel_id=1, replica_groups=mesh['seq'=16,'mp'=32] {'mp'}, dimensions={0}, use_global_device_ids=true | all-gather | bytes 811008 | tf_op jit(solution)/shard_map/all_gather | solution.py:106
  354.3 14.0 %all_to_all.10 = bf16[16,1,2,3072]{3,2,1,0:T(2,128)(2,1)S(1)} all-to-all(bf16[16,1,2,3072]{3,2,1,0:T(2,128)(2,1)S(1)} %copy.108), channel_id=1, replica_groups=mesh['seq'=16,'mp'=32] {'seq'}, dimensions={0} | all-to-all | bytes 393216 | tf_op jit(solution)/shard_map/all_to_all | solution.py:134
  369.0 73.7 %all-gather.16.cloned.1.call-done = bf16[512,1,2,3072]{3,0,2,1:T(8,128)(2,1)} async-done(((bf16[16,1,2,3072]{3,0,2,1:T(8,128)(2,1)}), bf16[512,1,2,3072]{3,0,2,1:T(8,128)(2,1)}) %all-gather.16.cloned.1.call-update) | async-done | bytes 6291472 | tf_op jit(solution)/shard_map/all_gather | solution.py:135
  442.7 3.5 fusion.3
  446.9 1.2 fusion.5
  448.1 7.0 fusion.11
  455.1 5.5 add_convert_fusion
  460.6 105.4 %reduce-scatter.2.cloned.1.call-done = bf16[1,16,1,3072]{3,1,2,0:T(8,128)(2,1)} async-done(((bf16[32,16,1,3072]{3,1,2,0:T(8,128)(2,1)}), bf16[1,16,1,3072]{3,1,2,0:T(8,128)(2,1)}) %reduce-scatter.2.cloned.1.call-update) | async-done | bytes 98320 | tf_op jit(solution)/shard_map/reduce_scatter | solution.py:157
  566.6 1.6 reduce.6
  568.2 13.0 %all_to_all.11 = bf16[16,2,1536]{2,1,0:T(2,128)(2,1)S(1)} all-to-all(bf16[16,2,1536]{2,1,0:T(2,128)(2,1)S(1)} %reshape.401), channel_id=1, replica_groups=mesh['seq'=16,'mp'=32] {'seq'}, dimensions={0} | all-to-all | bytes 196608 | tf_op jit(solution)/shard_map/all_to_all | solution.py:160
  582.9 71.3 %all-gather.12.cloned.1.call-done = bf16[16,32,3072]{2,0,1:T(8,128)(2,1)} async-done(((bf16[16,1,3072]{2,0,1:T(8,128)(2,1)}), bf16[16,32,3072]{2,0,1:T(8,128)(2,1)}) %all-gather.12.cloned.1.call-update) | async-done | bytes 3145744 | tf_op jit(solution)/shard_map/all_gather | solution.py:163
  654.2 3.8 multiply_reduce_fusion
  659.6 31.6 %all-gather.6 = bf16[32,4,3072]{2,1,0:T(4,128)(2,1)S(1)} all-gather(bf16[1,4,3072]{2,1,0:T(4,128)(2,1)S(1)} %bitcast.236), channel_id=1, replica_groups=mesh['seq'=16,'mp'=32] {'mp'}, dimensions={0}, use_global_device_ids=true | all-gather | bytes 811008 | tf_op jit(solution)/shard_map/all_gather | solution.py:174
  692.0 1.8 fusion.36
  694.7 1.2 convolution_multiply_fusion
  695.9 1.1 fusion.22
  697.7 50.8 %all-gather.18.cloned.1.call-done = f32[32,128,128]{2,1,0:T(8,128)} async-done(((f32[2,128,128]{2,1,0:T(8,128)}), f32[32,128,128]{2,1,0:T(8,128)}) %all-gather.18.cloned.1.call-update) | async-done | bytes 2097168 | tf_op jit(solution)/shard_map/all_gather | solution.py:12
  748.5 27.2 %while.31 = (s32[]{:T(128)}, f32[2,128,128]{2,1,0:T(8,128)S(1)}, s32[]{:T(128)}, f32[16,2]{1,0:T(8,128)}, f32[16,2,128,128]{3,2,1,0:T(8,128)}, /*index=5*/s32[]{:T(128)}, s32[]{:T(128)}, s32[]{:T(128)}, s32[]{:T(128)}) while((s32[]{:T(128)}, f32[2,128,128]{2,1,0:T(8,128)S(1)}, s32[]{:T(128)}, f32[16,2]{1,0:T(8,128)}, ...), condition=%wide.region_10.12_spmd.clone, body=%wide.region_9.11_spmd.clone.sunk | while | flops 131080 | bytes 393407 | solution.py:23
  749.2 1.0 fusion.96
  750.9 1.0 fusion.96
  752.6 1.0 fusion.96
  754.3 1.0 fusion.96
  756.0 1.0 fusion.96
  (159 shorter events, 42.8 us)
Async XLA Ops:
  7.2 112.0 %copy-start = (bf16[256,3072]{1,0:T(8,128)(2,1)S(1)}, bf16[256,3072]{1,0:T(8,128)(2,1)}, u32[]{:S(2)}) copy-start(bf16[256,3072]{1,0:T(8,128)(2,1)} %param.23) | copy-start | bytes 4718596
  7.2 94.5 %copy-start.10 = (bf16[128,256]{1,0:T(8,128)(2,1)S(1)}, bf16[128,256]{1,0:T(8,128)(2,1)}, u32[]{:S(2)}) copy-start(bf16[128,256]{1,0:T(8,128)(2,1)} %param.20) | copy-start | bytes 196612
  7.2 92.1 %copy-start.22 = (f32[128,2]{0,1:T(2,128)S(1)}, f32[128,2]{0,1:T(2,128)}, u32[]{:S(2)}) copy-start(f32[128,2]{0,1:T(2,128)} %param.28) | copy-start | bytes 3076
  7.2 94.7 %all-gather.14.cloned.1.call-start = ((), (), s32[]{:S(2)}) async-start(), calls=%async_computation.5 | async-start | bytes 2228224 | tf_op jit(solution)/shard_map/all_gather | solution.py:12
  10.1 91.9 %copy-start.17 = (f32[2]{0:T(128)}, f32[2]{0:T(128)S(1)}, u32[]{:S(2)}) copy-start(f32[2]{0:T(128)S(1)} %get-tuple-element.317) | copy-start | bytes 28
  12.6 308.2 %all-reduce.4.cloned.1.call-start = ((), (), s32[]{:S(2)}) async-start(), calls=%async_computation.8 | async-start | bytes 1572864
  48.1 70.5 %copy-start.2 = (bf16[128,256]{0,1:T(8,128)(2,1)}, bf16[128,256]{0,1:T(8,128)(2,1)S(1)}, u32[]{:S(2)}) copy-start(bf16[128,256]{0,1:T(8,128)(2,1)S(1)} %copy.133) | copy-start | bytes 196612
  49.2 69.7 %copy-start.8 = (bf16[128,256]{1,0:T(8,128)(2,1)S(1)}, bf16[128,256]{1,0:T(8,128)(2,1)}, u32[]{:S(2)}) copy-start(bf16[128,256]{1,0:T(8,128)(2,1)} %param.21) | copy-start | bytes 196612
  101.5 19.0 %copy-start.20 = (f32[128,2]{0,1:T(2,128)}, f32[128,2]{0,1:T(2,128)S(1)}, u32[]{:S(2)}) copy-start(f32[128,2]{0,1:T(2,128)S(1)} %get-tuple-element.316) | copy-start | bytes 3076
  101.7 18.8 %copy-start.13 = (f32[128,128]{1,0:T(8,128)}, f32[128,128]{1,0:T(8,128)S(1)}, u32[]{:S(2)}) copy-start(f32[128,128]{1,0:T(8,128)S(1)} %subtract_select_fusion) | copy-start | bytes 196612
  101.9 219.9 %copy-start.6 = (f32[2,128,128]{2,1,0:T(8,128)}, f32[2,128,128]{2,1,0:T(8,128)S(1)}, u32[]{:S(2)}) copy-start(f32[2,128,128]{2,1,0:T(8,128)S(1)} %convolution_multiply_fusion.1) | copy-start | bytes 393220
  101.9 218.9 %copy-start.14 = (bf16[4,3072]{1,0:T(4,128)(2,1)S(1)}, bf16[4,3072]{1,0:T(4,128)(2,1)}, u32[]{:S(2)}) copy-start(bf16[4,3072]{1,0:T(4,128)(2,1)} %param.24) | copy-start | bytes 73732
  102.0 219.9 %copy-start.18 = (f32[3072]{0:T(1024)S(1)}, f32[3072]{0:T(1024)}, u32[]{:S(2)}) copy-start(f32[3072]{0:T(1024)} %param.26) | copy-start | bytes 36868
  118.5 234.8 %copy-start.21 = (f32[16,2]{1,0:T(8,128)}, f32[16,2]{1,0:T(8,128)S(1)}, u32[]{:S(2)}) copy-start(f32[16,2]{1,0:T(8,128)S(1)} %get-tuple-element.454) | copy-start | bytes 388
  120.5 322.2 %all-gather.16.cloned.1.call-start = ((), (), s32[]{:S(2)}) async-start(), calls=%async_computation.6 | async-start | bytes 6488064 | tf_op jit(solution)/shard_map/all_gather | solution.py:135
  369.0 197.1 %reduce-scatter.2.cloned.1.call-start = ((), (), s32[]{:S(2)}) async-start(), calls=%async_computation.3 | async-start | bytes 3244032 | tf_op jit(solution)/shard_map/reduce_scatter | solution.py:157
  442.7 4.0 copy-start.5
  442.7 4.2 copy-start.12
  446.9 1.2 copy-start.1
  460.6 197.4 %copy-start.15 = (bf16[4,3072]{1,0:T(4,128)(2,1)S(1)}, bf16[4,3072]{1,0:T(4,128)(2,1)}, u32[]{:S(2)}) copy-start(bf16[4,3072]{1,0:T(4,128)(2,1)} %param.25) | copy-start | bytes 73732
  460.6 193.6 %all-gather.12.cloned.1.call-start = ((), (), s32[]{:S(2)}) async-start(), calls=%async_computation.4 | async-start | bytes 3244032 | tf_op jit(solution)/shard_map/all_gather | solution.py:163
  582.0 166.6 %all-gather.18.cloned.1.call-start = ((), (), s32[]{:S(2)}) async-start(), calls=%async_computation.7 | async-start | bytes 2228224 | tf_op jit(solution)/shard_map/all_gather | solution.py:12
  658.0 34.0 %copy-start.3 = (bf16[128,256]{0,1:T(8,128)(2,1)S(1)}, bf16[128,256]{0,1:T(8,128)(2,1)}, u32[]{:S(2)}) copy-start(bf16[128,256]{0,1:T(8,128)(2,1)} %copy-done.2) | copy-start | bytes 196612
  659.0 0.6 copy-start.16
  691.4 84.4 %copy-start.11 = (bf16[128,256]{1,0:T(8,128)(2,1)S(1)}, bf16[128,256]{1,0:T(8,128)(2,1)}, u32[]{:S(2)}) copy-start(bf16[128,256]{1,0:T(8,128)(2,1)} %param.20) | copy-start | bytes 196612
  691.4 84.4 %copy-start.19 = (f32[128,2]{0,1:T(2,128)S(1)}, f32[128,2]{0,1:T(2,128)}, u32[]{:S(2)}) copy-start(f32[128,2]{0,1:T(2,128)} %get-tuple-element.315) | copy-start | bytes 3076
  691.4 84.7 %copy-start.9 = (bf16[128,256]{1,0:T(8,128)(2,1)S(1)}, bf16[128,256]{1,0:T(8,128)(2,1)}, u32[]{:S(2)}) copy-start(bf16[128,256]{1,0:T(8,128)(2,1)} %param.21) | copy-start | bytes 196612
  691.4 84.9 %copy-start.7 = (f32[2,128,128]{2,1,0:T(8,128)S(1)}, f32[2,128,128]{2,1,0:T(8,128)}, u32[]{:S(2)}) copy-start(f32[2,128,128]{2,1,0:T(8,128)} %copy-done.6) | copy-start | bytes 393220
  692.0 85.4 %copy-start.4 = (bf16[128,256]{0,1:T(8,128)(2,1)S(1)}, bf16[128,256]{0,1:T(8,128)(2,1)}, u32[]{:S(2)}) copy-start(bf16[128,256]{0,1:T(8,128)(2,1)} %copy-done.2) | copy-start | bytes 196612
Sparse Core Ops, SparseCore 0:
  12.7 64.6 all-gather.13
  120.6 200.2 all-reduce.3
  369.1 73.5 all-gather.15
  460.7 105.3 reduce-scatter.1
  582.1 72.0 all-gather.11
  693.9 54.5 all-gather.17
where the time goes:
time: 787 us; the launch traced here: 785 us
  waiting for transfers between devices  501 us (64%)
  blocking collectives  170 us (22%)
  other arithmetic  41.7 us (5%)
  matrix products  31.4 us (4%)
  local copies, waits for them, and re-layouts  23.5 us (3%)
  between operations  16 us (2%)
    unnamed x7, waiting for transfers between devices  200 us
    reduce_scatter x1, waiting for transfers between devices, body(): lax.psum_scatter(partial_value.astype(jnp.bfloat16), 'mp', scatter_dimens...  105 us
    all_gather x1, waiting for transfers between devices, body(): slot_data = lax.all_gather(arrived[None], 'mp', axis=0, tiled=True)  73.7 us
    all_gather x1, waiting for transfers between devices, body(): all_slots = lax.all_gather(returned, 'mp', axis=1, tiled=True)  71.3 us
    all_gather x2, waiting for transfers between devices, carried_in(): everything = jax.tree.map(lambda part: lax.all_gather(part, axis), x)  50.8 us
    all_gather x1, blocking collectives, body(): lax.all_gather(cotangent, 'mp', axis=0, tiled=True)  46.4 us
    unnamed x1, blocking collectives  34.4 us
    select_n x32, other arithmetic, lap(): return jax.tree.map(lambda a, b: jnp.where(reached, a, b), new, before)  31.7 us
  transfers between devices with their start and end apart: 6, of which 5 were waited for; matrix products, arithmetic and copies ran while one was open for 2% of the time, Pallas kernels for 0%

commit v1 on v0

v1 whole, which is shorter than its diff:
```python
import jax
import jax.numpy as jnp
from jax import lax
from jax.sharding import PartitionSpec as P

EPSILON = 1e-06
F32 = jnp.float32
BF16 = jnp.bfloat16


def mm(a, b):
    return jnp.dot(a, b, preferred_element_type=F32)


def mm_t(a, b):
    return lax.dot_general(a, b, (((1,), (1,)), ((), ())), preferred_element_type=F32)


def heads_dot(spec, a, b):
    return jnp.einsum(spec, a, b, preferred_element_type=F32)


def body(
    queries,
    key_rows,
    value_rows,
    decay_rates,
    w_out,
    inputs,
    cotangent,
    norm_gain,
    expert_ids,
    gate_weights,
    w_gate,
    w_up,
    w_down,
):
    length = queries.shape[0]
    head_count = decay_rates.shape[0]
    head_size = queries.shape[1] // head_count
    width = w_out.shape[1]
    half = width // 2
    tok_share = inputs.shape[0]
    pair_share = 2 * tok_share
    seq_count = lax.axis_size("seq")
    mp_count = lax.axis_size("mp")
    z_count = mp_count // 2
    seq_place = lax.axis_index("seq")
    core = lax.rem(lax.axis_index("mp"), 2)
    z_groups = [[2 * k + c for k in range(z_count)] for c in range(2)]
    core_groups = [[2 * k, 2 * k + 1] for k in range(z_count)]
    swap_pairs = [(i, i ^ 1) for i in range(mp_count)]

    def swap(x):
        return lax.ppermute(x, "mp", swap_pairs)

    def own_half(x, axis):
        return lax.dynamic_slice_in_dim(x, core * half, half, axis)

    def other_half(x, axis):
        return lax.dynamic_slice_in_dim(x, (1 - core) * half, half, axis)

    def by_core(mine, theirs, axis):
        return jnp.where(
            core == 0,
            jnp.concatenate([mine, theirs], axis=axis),
            jnp.concatenate([theirs, mine], axis=axis),
        )

    def spread_z(x):
        copies = jnp.broadcast_to(x[None], (z_count,) + x.shape)
        out = lax.all_to_all(copies, "mp", 0, 0, axis_index_groups=z_groups, tiled=True)
        return out.reshape((z_count * x.shape[0],) + x.shape[1:])

    def sum_z(x):
        parts = x.reshape(z_count, pair_share, half)
        out = lax.all_to_all(parts, "mp", 0, 0, axis_index_groups=z_groups, tiled=True)
        return jnp.sum(out.astype(F32), axis=0)

    def to_heads(matrix):
        return matrix.reshape(length, head_count, head_size).transpose(1, 0, 2)

    def from_heads(blocks):
        return blocks.transpose(1, 0, 2).reshape(length, head_count * head_size)

    cot_all = lax.all_gather(cotangent, ("seq", "mp"), axis=0, tiled=True)

    capacity = 4 * length // seq_count
    labels = jnp.arange(seq_count, dtype=jnp.int32)
    first_pick = expert_ids[:, 0:1] == labels[None, :]
    second_pick = expert_ids[:, 1:2] == labels[None, :]
    chosen = (first_pick | second_pick).astype(jnp.int32)
    weight = jnp.where(first_pick, gate_weights[:, 0:1], 0.0) + jnp.where(
        second_pick, gate_weights[:, 1:2], 0.0
    )
    ranking = jnp.cumsum(chosen, axis=0) - 1
    slot_ids = jnp.arange(capacity, dtype=jnp.int32)
    placed = (chosen.T[:, None, :] == 1) & (ranking.T[:, None, :] == slot_ids[None, :, None])
    token_places = jnp.arange(length, dtype=jnp.int32)
    slot_token = jnp.sum(jnp.where(placed, token_places[None, None, :], 0), axis=2)
    slot_weight = jnp.sum(jnp.where(placed, weight.T[:, None, :], 0.0), axis=2)
    placing = placed.astype(BF16).reshape(seq_count * capacity, length)
    weight_top = slot_weight.astype(BF16)
    weight_low = (slot_weight - weight_top.astype(F32)).astype(BF16)
    notes = jnp.stack([slot_token.astype(BF16), weight_top, weight_low], axis=1)
    notes = jnp.pad(notes, ((0, 0), (0, 13), (0, head_size - capacity)))

    both = jnp.concatenate([inputs, cotangent], axis=0)
    both_kept, both_got = own_half(both, 1), swap(other_half(both, 1))
    pair_inputs = by_core(both_kept[:tok_share], both_got[:tok_share], 0).astype(F32)
    pair_cot = by_core(both_kept[tok_share:], both_got[tok_share:], 0).astype(F32)
    gain = own_half(norm_gain, 0)[None, :]

    query_heads, key_heads, value_heads = map(to_heads, (queries, key_rows, value_rows))
    places = jnp.arange(length).astype(F32)
    offset = places[:, None] - places[None, :]
    causal = offset >= 0
    clipped = jnp.where(causal, offset, 0.0)
    decay_band = jnp.where(causal[None], jnp.exp(-decay_rates[:, None, None] * clipped[None]), 0.0)
    head_decay = jnp.exp(-decay_rates[:, None] * places[None, :])[:, :, None]
    tail_decay = jnp.exp(-decay_rates[:, None] * (length - 1.0 - places)[None, :])[:, :, None]
    step_decay = jnp.exp(-decay_rates)[:, None, None]

    def exchange_states(states, extra):
        sent = states.astype(BF16).reshape(head_count * head_size, head_size)
        sent = jnp.broadcast_to(sent[None], (seq_count,) + sent.shape)
        if extra is not None:
            sent = jnp.concatenate([sent, extra], axis=1)
        return lax.all_to_all(sent, "seq", 0, 0, tiled=True)

    def combine_states(states, ahead):
        rate = decay_rates[:, None] * length * jnp.maximum(ahead, 0).astype(F32)[None, :]
        share = jnp.where(ahead[None, :] >= 0, jnp.exp(-rate), 0.0)
        states = states.reshape(seq_count, head_count, head_size, head_size).astype(F32)
        return jnp.sum(share.T[:, :, None, None] * states, axis=0)

    peers = jnp.arange(seq_count, dtype=jnp.int32)
    local_state = heads_dot(
        "htd,hte->hde",
        (step_decay * tail_decay * key_heads.astype(F32)).astype(BF16),
        value_heads,
    )
    arrived = exchange_states(local_state, notes)
    entering = combine_states(arrived[:, : head_count * head_size], seq_place - 1 - peers)
    entering_b = entering.astype(BF16)
    arrived_notes = arrived[:, head_count * head_size :, :capacity]
    scores = heads_dot("htd,hsd->hts", query_heads, key_heads) * decay_band
    scores_b = scores.astype(BF16)
    attended = heads_dot("hts,hse->hte", scores_b, value_heads)
    attended = attended + head_decay * heads_dot("htd,hde->hte", query_heads, entering_b)
    attended_b = from_heads(attended).astype(BF16)

    out_own, out_other = own_half(w_out, 1), other_half(w_out, 1)
    got = swap(mm(attended_b, out_other).astype(BF16))
    chip_mixed = (mm(attended_b, out_own) + got.astype(F32)).astype(BF16)
    stream = pair_inputs + sum_z(chip_mixed)

    def over_features(x):
        total = jnp.sum(x, axis=1, keepdims=True)
        return lax.psum(total, "mp", axis_index_groups=core_groups) / width

    inverse = lax.rsqrt(over_features(stream * stream) + EPSILON)
    normed = stream * inverse
    expert_in = (normed * gain).astype(BF16)

    group_in = spread_z(expert_in)
    outgoing = mm(placing, group_in).astype(BF16).reshape(seq_count, capacity, half)
    rows_own = lax.all_to_all(outgoing, "seq", 0, 0, tiled=True).reshape(-1, half)
    rows_other = swap(rows_own)
    gate_own, gate_other = own_half(w_gate[0], 0), other_half(w_gate[0], 0)
    up_own, up_other = own_half(w_up[0], 0), other_half(w_up[0], 0)

    hidden_all = mm_t(cot_all, w_down[0]).reshape(seq_count, length, -1)
    note_token = arrived_notes[:, 0, :].astype(jnp.int32)
    note_weight = arrived_notes[:, 1, :].astype(F32) + arrived_notes[:, 2, :].astype(F32)
    taken = (note_token[:, :, None] == token_places[None, None, :]).astype(F32)
    hidden_grad = jnp.einsum("bkt,bth->bkh", taken, hidden_all, precision=lax.Precision.HIGHEST)
    hidden_grad = (hidden_grad * note_weight[:, :, None]).reshape(seq_count * capacity, -1)

    gate_pre = mm(rows_own, gate_own) + mm(rows_other, gate_other)
    up_pre = mm(rows_own, up_own) + mm(rows_other, up_other)
    sigma = jax.nn.sigmoid(gate_pre)
    gate_grad = (hidden_grad * up_pre * sigma * (1.0 + gate_pre * (1.0 - sigma))).astype(BF16)
    up_grad = (hidden_grad * gate_pre * sigma).astype(BF16)
    got = swap((mm_t(gate_grad, gate_other) + mm_t(up_grad, up_other)).astype(BF16))
    slots = mm_t(gate_grad, gate_own) + mm_t(up_grad, up_own) + got.astype(F32)
    slots = slots.astype(BF16).reshape(seq_count, capacity, half)

    returned = lax.all_to_all(slots, "seq", 0, 0, tiled=True).reshape(-1, half)
    token_part = lax.dot_general(
        placing, returned, (((0,), (0,)), ((), ())), preferred_element_type=F32
    )
    expert_grad = sum_z(token_part.astype(BF16))
    scaled = expert_grad * gain
    stream_grad = inverse * (scaled - normed * over_features(scaled * normed)) + pair_cot
    pair_grad = stream_grad.astype(BF16)

    pair_kept = lax.dynamic_slice_in_dim(pair_grad, core * tok_share, tok_share, 0)
    pair_sent = lax.dynamic_slice_in_dim(pair_grad, (1 - core) * tok_share, tok_share, 0)
    input_grad = by_core(pair_kept, swap(pair_sent), 1)

    block_own = spread_z(pair_grad)
    block_other = swap(block_own)
    attended_grad = mm_t(block_own, out_own) + mm_t(block_other, out_other)
    grad_heads = to_heads(attended_grad)
    grad_b = grad_heads.astype(BF16)
    local_adjoint = heads_dot(
        "htd,hte->hde",
        query_heads,
        (step_decay * head_decay * grad_heads).astype(BF16),
    )
    leaving = combine_states(exchange_states(local_adjoint, None), peers - 1 - seq_place)
    leaving_b = leaving.astype(BF16)
    grad_scores = (heads_dot("hte,hse->hts", grad_b, value_heads) * decay_band).astype(BF16)
    query_part = heads_dot("hts,hsd->htd", grad_scores, key_heads)
    query_part = query_part + head_decay * heads_dot("hte,hde->htd", grad_b, entering_b)
    key_part = heads_dot("hts,htd->hsd", grad_scores, query_heads)
    key_part = key_part + tail_decay * heads_dot("hse,hde->hsd", value_heads, leaving_b)
    value_part = heads_dot("hts,hte->hse", scores_b, grad_b)
    value_part = value_part + tail_decay * heads_dot("hsd,hde->hse", key_heads, leaving_b)
    query_grad = from_heads(query_part).astype(BF16)
    key_grad = from_heads(key_part).astype(BF16)
    value_grad = from_heads(value_part).astype(BF16)
    return (query_grad, key_grad, value_grad, input_grad)


def solution(mesh):
    placed = (
        P("seq", "mp"),
        P("seq", "mp"),
        P("seq", "mp"),
        P("mp"),
        P("mp", None),
        P(("seq", "mp"), None),
        P(("seq", "mp"), None),
        P(),
        P("seq", None),
        P("seq", None),
        P("seq", None, "mp"),
        P("seq", None, "mp"),
        P("seq", "mp", None),
    )
    return jax.shard_map(
        body,
        mesh=mesh,
        in_specs=placed,
        out_specs=(P("seq", "mp"), P("seq", "mp"), P("seq", "mp"), P(("seq", "mp"), None)),
        check_vma=False,
    )
```

time: 787 us -> 413 us (0.52)
  waiting for transfers between devices: 501 us -> 181 us
  blocking collectives: 170 us -> 70.4 us
  starting transfers between devices: 0.43 us -> 74.8 us
  other arithmetic: 41.7 us -> 10.4 us
  local copies, waits for them, and re-layouts: 23.5 us -> 31.4 us
    unnamed x7 -> x1, waiting for transfers between devices: 200 us -> 0.68 us
    all_gather x4 -> x1, waiting for transfers between devices: 196 us -> 85.5 us  [body(): cot_all = lax.all_gather(cotangent, ('seq', 'mp'), axis=0, tiled=True)]
    all_gather x3 -> x0, blocking collectives: 108 us -> none  [the longest x1 46.4 us: body(): lax.all_gather(cotangent, 'mp', axis=0, tiled=True)]
    reduce_scatter x1 -> x0, waiting for transfers between devices: 105 us -> none  [body(): lax.psum_scatter(partial_value.astype(jnp.bfloat16), 'mp', scatter_dimens...]
    all_to_all x0 -> x6, waiting for transfers between devices: none -> 90.4 us  [the longest x2 34.2 us: spread_z(): lax.all_to_all(copies, 'mp', 0, 0, axis_index_groups=z_groups, tiled=True)]
    all_to_all x0 -> x6, starting transfers between devices: none -> 41.9 us  [the longest x1 15.1 us: sum_z(): lax.all_to_all(parts, 'mp', 0, 0, axis_index_groups=z_groups, tiled=True)]
    unnamed x1 -> x0, blocking collectives: 34.4 us -> none
    ppermute x0 -> x6, starting transfers between devices: none -> 32.8 us  [swap(): return lax.ppermute(x, 'mp', swap_pairs)]
  transfers between devices with their start and end apart: 6 -> 13, of which waited for: 5 -> 9; matrix products, arithmetic and copies ran while one was open for 2% -> 14% of each run, Pallas kernels for 0% -> 0%
where the time goes in v1:
time: 413 us; the launch traced here: 411 us
  waiting for transfers between devices  181 us (44%)
  starting transfers between devices  74.8 us (18%)
  blocking collectives  70.4 us (17%)
  local copies, waits for them, and re-layouts  31.4 us (8%)
  matrix products  28.8 us (7%)
  between operations  14.8 us (4%)
  other arithmetic  10.4 us (3%)
    all_gather x1, waiting for transfers between devices, body(): cot_all = lax.all_gather(cotangent, ('seq', 'mp'), axis=0, tiled=True)  85.5 us
    all_to_all x2, waiting for transfers between devices, spread_z(): lax.all_to_all(copies, 'mp', 0, 0, axis_index_groups=z_groups, tiled=True)  34.2 us
    ppermute x6, starting transfers between devices, swap(): return lax.ppermute(x, 'mp', swap_pairs)  32.8 us
    all_to_all x2, waiting for transfers between devices, exchange_states(): return lax.all_to_all(sent, 'seq', 0, 0, tiled=True)  27.6 us
    all_to_all x1, blocking collectives, body(): returned = lax.all_to_all(slots, 'seq', 0, 0, tiled=True).reshape(-1, half)  26.9 us
    all_to_all x1, blocking collectives, sum_z(): lax.all_to_all(parts, 'mp', 0, 0, axis_index_groups=z_groups, tiled=True)  23.5 us
    dot_general x1, local copies, waits for them, and re-layouts, mm_t(): lax.dot_general(a, b, (((1,), (1,)), ((), ())), preferred_element_type=F32)  20.2 us
    psum x2, blocking collectives, over_features(): return lax.psum(total, 'mp', axis_index_groups=core_groups) / width  20 us
  transfers between devices with their start and end apart: 13, of which 9 were waited for; matrix products, arithmetic and copies ran while one was open for 14% of the time, Pallas kernels for 0%

profile of v1, /device:TPU:1, one launch (start us, length us, event | category | flops | bytes accessed | tf_op | source)
XLA Modules:
  0.0 411.2 jit_solution(17643634173562279131)
XLA Ops:
  7.9 0.8 slice_bitcast_fusion.3
  9.4 0.8 slice_bitcast_fusion.1
  11.7 1.1 convolution_convert_fusion.3
  13.1 1.1 fusion.22
  14.2 7.7 %all-to-all-start = ((bf16[16,272,128]{2,1,0:T(8,128)(2,1)}), bf16[16,272,128]{2,1,0:T(8,128)(2,1)S(1)}, u32[]{:S(2)}, u32[]{:S(2)}) async-start(bf16[16,272,128]{2,1,0:T(8,128)(2,1)} %fusion.22), calls=%async_computation | async-start | bytes 2228224 | tf_op jit(solution)/shard_map/all_to_all | solution.py:129
  24.0 13.1 %all-to-all-done = bf16[16,272,128]{2,1,0:T(8,128)(2,1)S(1)} async-done(((bf16[16,272,128]{2,1,0:T(8,128)(2,1)}), bf16[16,272,128]{2,1,0:T(8,128)(2,1)S(1)}, u32[]{:S(2)}, u32[]{:S(2)}) %all-to-all-start) | async-done | bytes 1114144 | tf_op jit(solution)/shard_map/all_to_all | solution.py:129
  38.3 1.1 convolution_convert_fusion.1
  39.4 6.0 %collective-permute-start.1 = (bf16[128,1536]{1,0:T(8,128)(2,1)}, bf16[128,1536]{1,0:T(8,128)(2,1)S(1)}, u32[]{:S(2)}, u32[]{:S(2)}) collective-permute-start(bf16[128,1536]{1,0:T(8,128)(2,1)} %convolution_convert_fusion.1), channel_id=1, source_target_pairs={{0,1},{1,0},{2,3},{3,2},{4,5},{5,4},{6,7},{7,6},{8,9},{9,8},{10,11... | collective-permute-start | bytes 1179656 | tf_op jit(solution)/shard_map/ppermute | solution.py:55
  45.5 1.5 collective-permute-done.1
  47.0 1.1 fusion.33
  48.1 15.1 %all-to-all-start.1 = ((bf16[16,8,1536]{2,1,0:T(8,128)(2,1)}), bf16[16,8,1536]{2,1,0:T(8,128)(2,1)S(1)}, u32[]{:S(2)}, u32[]{:S(2)}) async-start(bf16[16,8,1536]{2,1,0:T(8,128)(2,1)} %fusion.33), calls=%async_computation.1 | async-start | bytes 786432 | tf_op jit(solution)/shard_map/all_to_all | solution.py:77
  63.4 2.6 collective-permute-start
  66.6 0.8 dynamic_slice.45
  68.0 12.8 %all-to-all-done.1 = bf16[16,8,1536]{2,1,0:T(8,128)(2,1)S(1)} async-done(((bf16[16,8,1536]{2,1,0:T(8,128)(2,1)}), bf16[16,8,1536]{2,1,0:T(8,128)(2,1)S(1)}, u32[]{:S(2)}, u32[]{:S(2)}) %all-to-all-start.1) | async-done | bytes 393248 | tf_op jit(solution)/shard_map/all_to_all | solution.py:77
  81.0 9.9 %psum.14 = f32[8,1]{0,1:T(1,128)S(1)} all-reduce(f32[8,1]{0,1:T(1,128)S(1)} %bitcast.259), channel_id=1, replica_groups={{0,1},{2,3},{4,5},{6,7},{8,9},{10,11},{12,13},{14,15},{16,17},{18,19},{..., use_global_device_ids=true, to_apply=%region_6.7 | all-reduce | flops 8 | bytes 64 | tf_op jit(solution)/shard_map/psum | solution.py:160
  91.0 0.8 broadcast_in_dim.160
  91.8 5.6 %all-to-all-start.2 = ((bf16[16,8,1536]{2,1,0:T(8,128)(2,1)}), bf16[16,8,1536]{2,1,0:T(8,128)(2,1)S(1)}, u32[]{:S(2)}, u32[]{:S(2)}) async-start(bf16[16,8,1536]{2,1,0:T(8,128)(2,1)} %broadcast_in_dim.160), calls=%async_computation.2 | async-start | bytes 786432 | tf_op jit(solution)/shard_map/all_to_all | solution.py:72
  97.4 17.1 %all-to-all-done.2 = bf16[16,8,1536]{2,1,0:T(8,128)(2,1)S(1)} async-done(((bf16[16,8,1536]{2,1,0:T(8,128)(2,1)}), bf16[16,8,1536]{2,1,0:T(8,128)(2,1)S(1)}, u32[]{:S(2)}, u32[]{:S(2)}) %all-to-all-start.2) | async-done | bytes 393248 | tf_op jit(solution)/shard_map/all_to_all | solution.py:72
  114.6 1.7 convolution_convert_fusion
  116.3 3.7 all-to-all-start.3
  120.0 1.4 fusion.75
  121.4 1.4 slice_convert_fusion.2
  122.8 15.8 %all-to-all-done.3 = bf16[16,32,1536]{2,1,0:T(8,128)(2,1)S(1)} async-done(((bf16[16,32,1536]{2,1,0:T(8,128)(2,1)}), bf16[16,32,1536]{2,1,0:T(8,128)(2,1)S(1)}, u32[]{:S(2)}, u32[]{:S(2)}) %all-to-all-start.3) | async-done | bytes 1572896 | tf_op jit(solution)/shard_map/all_to_all | solution.py:168
  138.6 10.5 %collective-permute-start.2 = (bf16[512,1536]{1,0:T(8,128)(2,1)S(1)}, bf16[512,1536]{1,0:T(8,128)(2,1)}, u32[]{:S(2)}, u32[]{:S(2)}) collective-permute-start(bf16[512,1536]{1,0:T(8,128)(2,1)S(1)} %bitcast.225), channel_id=1, source_target_pairs={{0,1},{1,0},{2,3},{3,2},{4,5},{5,4},{6,7},{7,6},{8,9},{9,8},{10,11... | collective-permute-start | bytes 4718600 | tf_op jit(solution)/shard_map/ppermute | solution.py:55
  149.0 2.4 fusion.41
  151.4 1.4 fusion.46
  152.8 85.5 %all-gather.3.cloned.1.call-done = bf16[512,4,3072]{2,1,0:T(4,128)(2,1)} async-done(((bf16[1,4,3072]{2,1,0:T(4,128)(2,1)}), bf16[512,4,3072]{2,1,0:T(4,128)(2,1)}) %all-gather.3.cloned.1.call-update) | async-done | bytes 12582928 | tf_op jit(solution)/shard_map/all_gather | solution.py:86
  238.3 20.2 %dot_general.110 = bf16[16,128,3072]{2,1,0:T(8,128)(2,1)} reshape(bf16[512,4,3072]{2,1,0:T(4,128)(2,1)} %all-gather.3.cloned.1.call-done) | data formatting | bytes 25165824 | tf_op jit(solution)/shard_map/dot_general | solution.py:16
  258.5 7.4 %fusion.23 = f32[16,128,144]{1,2,0:T(8,128)S(1)} fusion(bf16[16,128,3072]{2,1,0:T(8,128)(2,1)} %dot_general.110, bf16[1,144,3072]{2,1,0:T(8,128)(2,1)} %param.25), kind=kOutput, calls=%fused_computation.48 | convolution fusion | flops 1811939328 | bytes 14647296 | tf_op jit(solution)/shard_map/dot_general | solution.py:16
  266.0 2.0 convolution_multiply_fusion
  268.0 1.9 copy.110
  270.0 2.5 multiply_convert_fusion
  272.5 2.2 fusion.7
  275.9 2.2 collective-permute-start.3
  278.7 2.5 collective-permute-done.3
  281.9 26.9 %all_to_all.40 = bf16[16,32,1536]{2,1,0:T(8,128)(2,1)S(1)} all-to-all(bf16[16,32,1536]{2,1,0:T(8,128)(2,1)S(1)} %bitcast.229), channel_id=1, replica_groups=mesh['seq'=16,'mp'=32] {'seq'}, dimensions={0} | all-to-all | bytes 3145728 | tf_op jit(solution)/shard_map/all_to_all | solution.py:189
  309.2 23.5 %all_to_all.41 = bf16[16,8,1536]{2,1,0:T(8,128)(2,1)S(1)} all-to-all(bf16[16,8,1536]{2,1,0:T(8,128)(2,1)S(1)} %fusion.2), channel_id=1, replica_groups={{0,2,4,6,8,10,12,14,16,18,20,22,24,26,28,30},{1,3,5,7,9,11,13,15,17,19,..., dimensions={0} | all-to-all | bytes 786432 | tf_op jit(solution)/shard_map/all_to_all | solution.py:77
  333.0 10.1 %psum.15 = f32[8,1]{0,1:T(1,128)S(1)} all-reduce(f32[8,1]{0,1:T(1,128)S(1)} %bitcast.260), channel_id=1, replica_groups={{0,1},{2,3},{4,5},{6,7},{8,9},{10,11},{12,13},{14,15},{16,17},{18,19},{..., use_global_device_ids=true, to_apply=%region_9.10 | all-reduce | flops 8 | bytes 64 | tf_op jit(solution)/shard_map/psum | solution.py:160
  343.3 0.8 broadcast_in_dim.162
  344.0 6.1 %all-to-all-start.6 = ((bf16[16,8,1536]{2,1,0:T(8,128)(2,1)}), bf16[16,8,1536]{2,1,0:T(8,128)(2,1)S(1)}, u32[]{:S(2)}, u32[]{:S(2)}) async-start(bf16[16,8,1536]{2,1,0:T(8,128)(2,1)} %broadcast_in_dim.162), calls=%async_computation.6 | async-start | bytes 786432 | tf_op jit(solution)/shard_map/all_to_all | solution.py:72
  350.3 17.1 %all-to-all-done.6 = bf16[16,8,1536]{2,1,0:T(8,128)(2,1)S(1)} async-done(((bf16[16,8,1536]{2,1,0:T(8,128)(2,1)}), bf16[16,8,1536]{2,1,0:T(8,128)(2,1)S(1)}, u32[]{:S(2)}, u32[]{:S(2)}) %all-to-all-start.6) | async-done | bytes 393248 | tf_op jit(solution)/shard_map/all_to_all | solution.py:72
  367.3 9.7 %collective-permute-start.4 = (bf16[128,1536]{1,0:T(8,128)(2,1)S(1)}, bf16[128,1536]{1,0:T(8,128)(2,1)S(1)}, u32[]{:S(2)}, u32[]{:S(2)}) collective-permute-start(bf16[128,1536]{1,0:T(8,128)(2,1)S(1)} %bitcast.235), channel_id=1, source_target_pairs={{0,1},{1,0},{2,3},{3,2},{4,5},{5,4},{6,7},{7,6},{8,9},{9,8},{10,11... | collective-permute-start | bytes 1179656 | tf_op jit(solution)/shard_map/ppermute | solution.py:55
  377.0 1.9 collective-permute-start.5
  380.1 1.2 broadcast_in_dim.165
  381.3 3.7 all-to-all-start.7
  387.0 14.5 %all-to-all-done.7 = bf16[16,256,128]{2,1,0:T(8,128)(2,1)S(1)} async-done(((bf16[16,256,128]{2,1,0:T(8,128)(2,1)}), bf16[16,256,128]{2,1,0:T(8,128)(2,1)S(1)}, u32[]{:S(2)}, u32[]{:S(2)}) %all-to-all-start.7) | async-done | bytes 1048608 | tf_op jit(solution)/shard_map/all_to_all | solution.py:129
  402.7 0.7 copy.120
  403.6 0.7 copy.119
  (138 shorter events, 15.8 us)
Async XLA Ops:
  7.2 31.1 %copy-start = (bf16[256,3072]{1,0:T(8,128)(2,1)S(1)}, bf16[256,3072]{1,0:T(8,128)(2,1)}, u32[]{:S(2)}) copy-start(bf16[256,3072]{1,0:T(8,128)(2,1)} %param.17) | copy-start | bytes 4718596
  7.2 231.1 %all-gather.3.cloned.1.call-start = ((), (), s32[]{:S(2)}) async-start(), calls=%async_computation.8 | async-start | bytes 12607488 | tf_op jit(solution)/shard_map/all_gather | solution.py:86
  9.0 3.9 copy-start.17
  11.1 12.6 %copy-start.29 = (f32[2]{0:T(128)}, f32[2]{0:T(128)S(1)}, u32[]{:S(2)}) copy-start(f32[2]{0:T(128)S(1)} %get-tuple-element.46) | copy-start | bytes 28
  14.2 8.5 %copy-start.14 = (bf16[128,256]{1,0:T(8,128)(2,1)S(1)}, bf16[128,256]{1,0:T(8,128)(2,1)}, u32[]{:S(2)}) copy-start(bf16[128,256]{1,0:T(8,128)(2,1)} %param.13) | copy-start | bytes 196612
  14.2 9.5 %copy-start.8 = (bf16[128,256]{1,0:T(8,128)(2,1)S(1)}, bf16[128,256]{1,0:T(8,128)(2,1)}, u32[]{:S(2)}) copy-start(bf16[128,256]{1,0:T(8,128)(2,1)} %param.14) | copy-start | bytes 196612
  14.2 22.9 %all-to-all-start = ((bf16[16,272,128]{2,1,0:T(8,128)(2,1)}), bf16[16,272,128]{2,1,0:T(8,128)(2,1)S(1)}, u32[]{:S(2)}, u32[]{:S(2)}) async-start(bf16[16,272,128]{2,1,0:T(8,128)(2,1)} %fusion.22), calls=%async_computation | async-start | bytes 2228224 | tf_op jit(solution)/shard_map/all_to_all | solution.py:129
  21.9 16.1 %copy-start.5 = (bf16[128,256]{1,0:T(8,128)(2,1)S(1)}, bf16[128,256]{1,0:T(8,128)(2,1)}, u32[]{:S(2)}) copy-start(bf16[128,256]{1,0:T(8,128)(2,1)} %param.15) | copy-start | bytes 196612
  23.5 14.8 %copy-start.27 = (f32[128,2]{0,1:T(2,128)}, f32[128,2]{0,1:T(2,128)S(1)}, u32[]{:S(2)}) copy-start(f32[128,2]{0,1:T(2,128)S(1)} %get-tuple-element.41) | copy-start | bytes 3076
  23.6 14.2 %copy-start.15 = (pred[128,128]{1,0:T(8,128)(4,1)}, pred[128,128]{1,0:T(8,128)(4,1)S(1)}, u32[]{:S(2)}) copy-start(pred[128,128]{1,0:T(8,128)(4,1)S(1)} %subtract_compare_fusion) | copy-start | bytes 49156
  23.7 13.4 %copy-start.9 = (f32[128,128]{1,0:T(8,128)}, f32[128,128]{1,0:T(8,128)S(1)}, u32[]{:S(2)}) copy-start(f32[128,128]{1,0:T(8,128)S(1)} %subtract_select_fusion) | copy-start | bytes 196612
  37.1 11.0 %copy-start.1 = (bf16[16,272,128]{2,1,0:T(8,128)(2,1)}, bf16[16,272,128]{2,1,0:T(8,128)(2,1)S(1)}, u32[]{:S(2)}) copy-start(bf16[16,272,128]{2,1,0:T(8,128)(2,1)S(1)} %all-to-all-done) | copy-start | bytes 3342340
  38.3 25.0 %copy-start.13 = (bf16[4,3072]{1,0:T(4,128)(2,1)S(1)}, bf16[4,3072]{1,0:T(4,128)(2,1)}, u32[]{:S(2)}) copy-start(bf16[4,3072]{1,0:T(4,128)(2,1)} %param.19) | copy-start | bytes 73732
  38.3 25.0 %copy-start.25 = (bf16[4,3072]{1,0:T(4,128)(2,1)S(1)}, bf16[4,3072]{1,0:T(4,128)(2,1)}, u32[]{:S(2)}) copy-start(bf16[4,3072]{1,0:T(4,128)(2,1)} %param.18) | copy-start | bytes 73732
  39.4 7.6 %collective-permute-start.1 = (bf16[128,1536]{1,0:T(8,128)(2,1)}, bf16[128,1536]{1,0:T(8,128)(2,1)S(1)}, u32[]{:S(2)}, u32[]{:S(2)}) collective-permute-start(bf16[128,1536]{1,0:T(8,128)(2,1)} %convolution_convert_fusion.1), channel_id=1, source_target_pairs={{0,1},{1,0},{2,3},{3,2},{4,5},{5,4},{6,7},{7,6},{8,9},{9,8},{10,11... | collective-permute-start | bytes 1179656 | tf_op jit(solution)/shard_map/ppermute | solution.py:55
  48.1 49.3 %copy-start.18 = (pred[16,128]{1,0:T(8,128)(4,1)S(1)}, pred[16,128]{1,0:T(8,128)(4,1)}, u32[]{:S(2)}) copy-start(pred[16,128]{1,0:T(8,128)(4,1)} %copy-done.17) | copy-start | bytes 6148
  48.1 32.7 %all-to-all-start.1 = ((bf16[16,8,1536]{2,1,0:T(8,128)(2,1)}), bf16[16,8,1536]{2,1,0:T(8,128)(2,1)S(1)}, u32[]{:S(2)}, u32[]{:S(2)}) async-start(bf16[16,8,1536]{2,1,0:T(8,128)(2,1)} %fusion.33), calls=%async_computation.1 | async-start | bytes 786432 | tf_op jit(solution)/shard_map/all_to_all | solution.py:77
  63.4 4.0 collective-permute-start
  67.3 24.5 %copy-start.11 = (f32[1536]{0:T(1024)}, f32[1536]{0:T(1024)S(1)}, u32[]{:S(2)}) copy-start(f32[1536]{0:T(1024)S(1)} %dynamic_slice.45) | copy-start | bytes 18436
  90.9 25.4 %copy-start.31 = (f32[8]{0:T(128)}, f32[8]{0:T(128)S(1)}, u32[]{:S(2)}) copy-start(f32[8]{0:T(128)S(1)} %rsqrt_bitcast_fusion) | copy-start | bytes 100
  91.8 22.7 %all-to-all-start.2 = ((bf16[16,8,1536]{2,1,0:T(8,128)(2,1)}), bf16[16,8,1536]{2,1,0:T(8,128)(2,1)S(1)}, u32[]{:S(2)}, u32[]{:S(2)}) async-start(bf16[16,8,1536]{2,1,0:T(8,128)(2,1)} %broadcast_in_dim.160), calls=%async_computation.2 | async-start | bytes 786432 | tf_op jit(solution)/shard_map/all_to_all | solution.py:72
  116.3 22.3 %all-to-all-start.3 = ((bf16[16,32,1536]{2,1,0:T(8,128)(2,1)}), bf16[16,32,1536]{2,1,0:T(8,128)(2,1)S(1)}, u32[]{:S(2)}, u32[]{:S(2)}) async-start(bf16[16,32,1536]{2,1,0:T(8,128)(2,1)} %bitcast.228), calls=%async_computation.3 | async-start | bytes 3145728 | tf_op jit(solution)/shard_map/all_to_all | solution.py:168
  138.6 12.8 %copy-start.3 = (bf16[1,3072,144]{1,2,0:T(8,128)(2,1)S(1)}, bf16[1,3072,144]{1,2,0:T(8,128)(2,1)}, u32[]{:S(2)}) copy-start(bf16[1,3072,144]{1,2,0:T(8,128)(2,1)} %param.24) | copy-start | bytes 2654212
  138.6 131.4 %collective-permute-start.2 = (bf16[512,1536]{1,0:T(8,128)(2,1)S(1)}, bf16[512,1536]{1,0:T(8,128)(2,1)}, u32[]{:S(2)}, u32[]{:S(2)}) collective-permute-start(bf16[512,1536]{1,0:T(8,128)(2,1)S(1)} %bitcast.225), channel_id=1, source_target_pairs={{0,1},{1,0},{2,3},{3,2},{4,5},{5,4},{6,7},{7,6},{8,9},{9,8},{10,11... | collective-permute-start | bytes 4718600 | tf_op jit(solution)/shard_map/ppermute | solution.py:55
  258.5 7.5 %copy-start.22 = (f32[16,1,32]{2,1,0:T(1,128)S(1)}, f32[16,1,32]{2,1,0:T(1,128)}, u32[]{:S(2)}) copy-start(f32[16,1,32]{2,1,0:T(1,128)} %fusion.75) | copy-start | bytes 6148
  258.5 7.5 %copy-start.23 = (s32[16,1,32]{2,1,0:T(1,128)S(1)}, s32[16,1,32]{2,1,0:T(1,128)}, u32[]{:S(2)}) copy-start(s32[16,1,32]{2,1,0:T(1,128)} %slice_convert_fusion.2) | copy-start | bytes 6148
  269.9 2.5 copy-start.4
  269.9 2.5 copy-start.6
  269.9 2.5 copy-start.7
  272.5 2.2 copy-start.2
  275.9 5.3 %collective-permute-start.3 = (bf16[512,1536]{1,0:T(8,128)(2,1)S(1)}, bf16[512,1536]{1,0:T(8,128)(2,1)S(1)}, u32[]{:S(2)}, u32[]{:S(2)}) collective-permute-start(bf16[512,1536]{1,0:T(8,128)(2,1)S(1)} %fusion), channel_id=1, source_target_pairs={{0,1},{1,0},{2,3},{3,2},{4,5},{5,4},{6,7},{7,6},{8,9},{9,8},{10,11... | collective-permute-start | bytes 4718600 | tf_op jit(solution)/shard_map/ppermute | solution.py:55
  281.9 26.9 %copy-start.19 = (pred[16,128]{1,0:T(8,128)(4,1)S(1)}, pred[16,128]{1,0:T(8,128)(4,1)}, u32[]{:S(2)}) copy-start(pred[16,128]{1,0:T(8,128)(4,1)} %copy-done.17) | copy-start | bytes 6148
  308.7 24.1 %copy-start.12 = (f32[1536]{0:T(1024)S(1)}, f32[1536]{0:T(1024)}, u32[]{:S(2)}) copy-start(f32[1536]{0:T(1024)} %copy-done.11) | copy-start | bytes 18436
  308.7 24.1 %copy-start.32 = (f32[8]{0:T(128)S(1)}, f32[8]{0:T(128)}, u32[]{:S(2)}) copy-start(f32[8]{0:T(128)} %copy-done.31) | copy-start | bytes 100
  308.7 34.4 %copy-start.20 = (bf16[4,1536]{1,0:T(4,128)(2,1)S(1)}, bf16[4,1536]{1,0:T(4,128)(2,1)}, u32[]{:S(2)}) copy-start(bf16[4,1536]{1,0:T(4,128)(2,1)} %get-tuple-element.30) | copy-start | bytes 36868
  308.8 34.4 %copy-start.21 = (bf16[4,1536]{1,0:T(4,128)(2,1)S(1)}, bf16[4,1536]{1,0:T(4,128)(2,1)}, u32[]{:S(2)}) copy-start(bf16[4,1536]{1,0:T(4,128)(2,1)} %get-tuple-element.32) | copy-start | bytes 36868
  309.2 41.0 %copy-start.24 = (f32[16,2]{1,0:T(8,128)S(1)}, f32[16,2]{1,0:T(8,128)}, u32[]{:S(2)}) copy-start(f32[16,2]{1,0:T(8,128)} %get-tuple-element.42) | copy-start | bytes 388
  344.0 23.3 %all-to-all-start.6 = ((bf16[16,8,1536]{2,1,0:T(8,128)(2,1)}), bf16[16,8,1536]{2,1,0:T(8,128)(2,1)S(1)}, u32[]{:S(2)}, u32[]{:S(2)}) async-start(bf16[16,8,1536]{2,1,0:T(8,128)(2,1)} %broadcast_in_dim.162), calls=%async_computation.6 | async-start | bytes 786432 | tf_op jit(solution)/shard_map/all_to_all | solution.py:72
  350.2 29.7 %copy-start.33 = (f32[2,128]{1,0:T(2,128)S(1)}, f32[2,128]{1,0:T(2,128)}, u32[]{:S(2)}) copy-start(f32[2,128]{1,0:T(2,128)} %get-tuple-element.34) | copy-start | bytes 3076
  367.3 12.0 %collective-permute-start.4 = (bf16[128,1536]{1,0:T(8,128)(2,1)S(1)}, bf16[128,1536]{1,0:T(8,128)(2,1)S(1)}, u32[]{:S(2)}, u32[]{:S(2)}) collective-permute-start(bf16[128,1536]{1,0:T(8,128)(2,1)S(1)} %bitcast.235), channel_id=1, source_target_pairs={{0,1},{1,0},{2,3},{3,2},{4,5},{5,4},{6,7},{7,6},{8,9},{9,8},{10,11... | collective-permute-start | bytes 1179656 | tf_op jit(solution)/shard_map/ppermute | solution.py:55
  377.0 7.9 %collective-permute-start.5 = (bf16[4,1536]{1,0:T(4,128)(2,1)S(1)}, bf16[4,1536]{1,0:T(4,128)(2,1)S(1)}, u32[]{:S(2)}, u32[]{:S(2)}) collective-permute-start(bf16[4,1536]{1,0:T(4,128)(2,1)S(1)} %get-tuple-element.29), channel_id=1, source_target_pairs={{0,1},{1,0},{2,3},{3,2},{4,5},{5,4},{6,7},{7,6},{8,9},{9,8},{10,11... | collective-permute-start | bytes 36872 | tf_op jit(solution)/shard_map/ppermute | solution.py:55
  380.1 5.5 %copy-start.28 = (f32[128,2]{0,1:T(2,128)S(1)}, f32[128,2]{0,1:T(2,128)}, u32[]{:S(2)}) copy-start(f32[128,2]{0,1:T(2,128)} %copy-done.27) | copy-start | bytes 3076
  380.1 5.7 %copy-start.10 = (f32[128,128]{1,0:T(8,128)S(1)}, f32[128,128]{1,0:T(8,128)}, u32[]{:S(2)}) copy-start(f32[128,128]{1,0:T(8,128)} %copy-done.9) | copy-start | bytes 196612
  380.1 5.7 %copy-start.16 = (pred[128,128]{1,0:T(8,128)(4,1)S(1)}, pred[128,128]{1,0:T(8,128)(4,1)}, u32[]{:S(2)}) copy-start(pred[128,128]{1,0:T(8,128)(4,1)} %copy-done.15) | copy-start | bytes 49156
  380.1 5.7 %copy-start.30 = (f32[2]{0:T(128)S(1)}, f32[2]{0:T(128)}, u32[]{:S(2)}) copy-start(f32[2]{0:T(128)} %copy-done.29) | copy-start | bytes 28
  381.3 20.2 %all-to-all-start.7 = ((bf16[16,256,128]{2,1,0:T(8,128)(2,1)}), bf16[16,256,128]{2,1,0:T(8,128)(2,1)S(1)}, u32[]{:S(2)}, u32[]{:S(2)}) async-start(bf16[16,256,128]{2,1,0:T(8,128)(2,1)} %broadcast_in_dim.165), calls=%async_computation.7 | async-start | bytes 2097152 | tf_op jit(solution)/shard_map/all_to_all | solution.py:129
  385.0 17.2 %copy-start.26 = (f32[128,2]{0,1:T(2,128)S(1)}, f32[128,2]{0,1:T(2,128)}, u32[]{:S(2)}) copy-start(f32[128,2]{0,1:T(2,128)} %get-tuple-element.40) | copy-start | bytes 3076
Sparse Core Ops, SparseCore 0:
  12.7 225.5 all-gather.2

commit v2 on v1

--- a/solution.py
+++ b/solution.py
@@ -72,6 +72,15 @@
         out = lax.all_to_all(copies, "mp", 0, 0, axis_index_groups=z_groups, tiled=True)
         return out.reshape((z_count * x.shape[0],) + x.shape[1:])
 
+    z_bits = z_count.bit_length() - 1
+
+    def double_z(x, level):
+        bit = 2 << (z_bits - 1 - level)
+        theirs = lax.ppermute(x, "mp", [(i, i ^ bit) for i in range(mp_count)])
+        upper = lax.rem(lax.axis_index("mp") // bit, 2) == 1
+        first, second = jnp.where(upper, theirs, x), jnp.where(upper, x, theirs)
+        return jnp.stack([first, second], axis=level)
+
     def sum_z(x):
         parts = x.reshape(z_count, pair_share, half)
         out = lax.all_to_all(parts, "mp", 0, 0, axis_index_groups=z_groups, tiled=True)
@@ -82,8 +91,6 @@
 
     def from_heads(blocks):
         return blocks.transpose(1, 0, 2).reshape(length, head_count * head_size)
-
-    cot_all = lax.all_gather(cotangent, ("seq", "mp"), axis=0, tiled=True)
 
     capacity = 4 * length // seq_count
     labels = jnp.arange(seq_count, dtype=jnp.int32)
@@ -96,19 +103,14 @@
     ranking = jnp.cumsum(chosen, axis=0) - 1
     slot_ids = jnp.arange(capacity, dtype=jnp.int32)
     placed = (chosen.T[:, None, :] == 1) & (ranking.T[:, None, :] == slot_ids[None, :, None])
-    token_places = jnp.arange(length, dtype=jnp.int32)
-    slot_token = jnp.sum(jnp.where(placed, token_places[None, None, :], 0), axis=2)
+    placing = placed.astype(BF16).reshape(seq_count * capacity, length)
     slot_weight = jnp.sum(jnp.where(placed, weight.T[:, None, :], 0.0), axis=2)
-    placing = placed.astype(BF16).reshape(seq_count * capacity, length)
-    weight_top = slot_weight.astype(BF16)
-    weight_low = (slot_weight - weight_top.astype(F32)).astype(BF16)
-    notes = jnp.stack([slot_token.astype(BF16), weight_top, weight_low], axis=1)
-    notes = jnp.pad(notes, ((0, 0), (0, 13), (0, head_size - capacity)))
 
     both = jnp.concatenate([inputs, cotangent], axis=0)
     both_kept, both_got = own_half(both, 1), swap(other_half(both, 1))
     pair_inputs = by_core(both_kept[:tok_share], both_got[:tok_share], 0).astype(F32)
-    pair_cot = by_core(both_kept[tok_share:], both_got[tok_share:], 0).astype(F32)
+    pair_cot_b = by_core(both_kept[tok_share:], both_got[tok_share:], 0)
+    pair_cot = pair_cot_b.astype(F32)
     gain = own_half(norm_gain, 0)[None, :]
 
     query_heads, key_heads, value_heads = map(to_heads, (queries, key_rows, value_rows))
@@ -121,11 +123,9 @@
     tail_decay = jnp.exp(-decay_rates[:, None] * (length - 1.0 - places)[None, :])[:, :, None]
     step_decay = jnp.exp(-decay_rates)[:, None, None]
 
-    def exchange_states(states, extra):
+    def exchange_states(states):
         sent = states.astype(BF16).reshape(head_count * head_size, head_size)
         sent = jnp.broadcast_to(sent[None], (seq_count,) + sent.shape)
-        if extra is not None:
-            sent = jnp.concatenate([sent, extra], axis=1)
         return lax.all_to_all(sent, "seq", 0, 0, tiled=True)
 
     def combine_states(states, ahead):
@@ -140,10 +140,8 @@
         (step_decay * tail_decay * key_heads.astype(F32)).astype(BF16),
         value_heads,
     )
-    arrived = exchange_states(local_state, notes)
-    entering = combine_states(arrived[:, : head_count * head_size], seq_place - 1 - peers)
+    entering = combine_states(exchange_states(local_state), seq_place - 1 - peers)
     entering_b = entering.astype(BF16)
-    arrived_notes = arrived[:, head_count * head_size :, :capacity]
     scores = heads_dot("htd,hsd->hts", query_heads, key_heads) * decay_band
     scores_b = scores.astype(BF16)
     attended = heads_dot("hts,hse->hte", scores_b, value_heads)
@@ -153,6 +151,13 @@
     out_own, out_other = own_half(w_out, 1), other_half(w_out, 1)
     got = swap(mm(attended_b, out_other).astype(BF16))
     chip_mixed = (mm(attended_b, out_own) + got.astype(F32)).astype(BF16)
+    block_cot = pair_cot_b
+    for level in range(z_bits // 2):
+        block_cot = double_z(block_cot, level)
+    block_cot, chip_mixed = lax.optimization_barrier((block_cot, chip_mixed))
+    for level in range(z_bits // 2, z_bits):
+        block_cot = double_z(block_cot, level)
+    block_cot = block_cot.reshape(length, half)
     stream = pair_inputs + sum_z(chip_mixed)
 
     def over_features(x):
@@ -162,21 +167,22 @@
     inverse = lax.rsqrt(over_features(stream * stream) + EPSILON)
     normed = stream * inverse
     expert_in = (normed * gain).astype(BF16)
+    block_cot, expert_in = lax.optimization_barrier((block_cot, expert_in))
 
     group_in = spread_z(expert_in)
     outgoing = mm(placing, group_in).astype(BF16).reshape(seq_count, capacity, half)
+    weighted = (slot_weight.reshape(-1, 1) * mm(placing, block_cot)).astype(BF16)
+    weighted = weighted.reshape(seq_count, capacity, half)
+    cot_own = lax.all_to_all(weighted, "seq", 0, 0, tiled=True).reshape(-1, half)
+    cot_own, outgoing = lax.optimization_barrier((cot_own, outgoing))
+    cot_other = swap(cot_own)
     rows_own = lax.all_to_all(outgoing, "seq", 0, 0, tiled=True).reshape(-1, half)
     rows_other = swap(rows_own)
     gate_own, gate_other = own_half(w_gate[0], 0), other_half(w_gate[0], 0)
     up_own, up_other = own_half(w_up[0], 0), other_half(w_up[0], 0)
 
-    hidden_all = mm_t(cot_all, w_down[0]).reshape(seq_count, length, -1)
-    note_token = arrived_notes[:, 0, :].astype(jnp.int32)
-    note_weight = arrived_notes[:, 1, :].astype(F32) + arrived_notes[:, 2, :].astype(F32)
-    taken = (note_token[:, :, None] == token_places[None, None, :]).astype(F32)
-    hidden_grad = jnp.einsum("bkt,bth->bkh", taken, hidden_all, precision=lax.Precision.HIGHEST)
-    hidden_grad = (hidden_grad * note_weight[:, :, None]).reshape(seq_count * capacity, -1)
-
+    down_own, down_other = own_half(w_down[0], 1), other_half(w_down[0], 1)
+    hidden_grad = mm_t(cot_own, down_own) + mm_t(cot_other, down_other)
     gate_pre = mm(rows_own, gate_own) + mm(rows_other, gate_other)
     up_pre = mm(rows_own, up_own) + mm(rows_other, up_other)
     sigma = jax.nn.sigmoid(gate_pre)
@@ -209,7 +215,7 @@
         query_heads,
         (step_decay * head_decay * grad_heads).astype(BF16),
     )
-    leaving = combine_states(exchange_states(local_adjoint, None), peers - 1 - seq_place)
+    leaving = combine_states(exchange_states(local_adjoint), peers - 1 - seq_place)
     leaving_b = leaving.astype(BF16)
     grad_scores = (heads_dot("hte,hse->hts", grad_b, value_heads) * decay_band).astype(BF16)
     query_part = heads_dot("hts,hsd->htd", grad_scores, key_heads)

time: 413 us -> 318 us (0.77)
  waiting for transfers between devices: 181 us -> 85.9 us
  starting transfers between devices: 74.8 us -> 105 us
  local copies, waits for them, and re-layouts: 31.4 us -> 8.21 us
  blocking collectives: 70.4 us -> 92 us
  matrix products: 28.8 us -> 15.7 us
  between operations: 14.8 us -> 1.75 us
    all_gather x1 -> x0, waiting for transfers between devices: 85.5 us -> none  [body(): cot_all = lax.all_gather(cotangent, ('seq', 'mp'), axis=0, tiled=True)]
    ppermute x0 -> x4, starting transfers between devices: none -> 26.9 us  [double_z(): theirs = lax.ppermute(x, 'mp', [(i, i ^ bit) for i in range(mp_count)])]
    dot_general x1 -> x0, local copies, waits for them, and re-layouts: 20.2 us -> none  [mm_t(): lax.dot_general(a, b, (((1,), (1,)), ((), ())), preferred_element_type=F32)]
    ppermute x0 -> x4, waiting for transfers between devices: none -> 20 us  [double_z(): theirs = lax.ppermute(x, 'mp', [(i, i ^ bit) for i in range(mp_count)])]
    all_to_all x0 -> x1, blocking collectives: none -> 19 us  [body(): lax.all_to_all(outgoing, 'seq', 0, 0, tiled=True).reshape(-1, half)]
    all_to_all x2, waiting for transfers between devices: 27.6 us -> 14.3 us  [exchange_states(): return lax.all_to_all(sent, 'seq', 0, 0, tiled=True)]
    all_to_all x1, waiting for transfers between devices: 12.8 us -> 0.01 us  [sum_z(): lax.all_to_all(parts, 'mp', 0, 0, axis_index_groups=z_groups, tiled=True)]
    all_to_all x1, blocking collectives: 23.5 us -> 34.3 us  [sum_z(): lax.all_to_all(parts, 'mp', 0, 0, axis_index_groups=z_groups, tiled=True)]
  transfers between devices with their start and end apart: 13 -> 17, of which waited for: 9 -> 9; matrix products, arithmetic and copies ran while one was open for 14% -> 6% of each run, Pallas kernels for 0% -> 0%
where the time goes in v2:
time: 318 us; the launch traced here: 316 us
  starting transfers between devices  105 us (33%)
  blocking collectives  92 us (29%)
  waiting for transfers between devices  85.9 us (27%)
  matrix products  15.7 us (5%)
  local copies, waits for them, and re-layouts  8.21 us (3%)
  other arithmetic  7.94 us (2%)
    ppermute x7, starting transfers between devices, swap(): return lax.ppermute(x, 'mp', swap_pairs)  39.4 us
    all_to_all x1, blocking collectives, sum_z(): lax.all_to_all(parts, 'mp', 0, 0, axis_index_groups=z_groups, tiled=True)  34.3 us
    all_to_all x2, waiting for transfers between devices, spread_z(): lax.all_to_all(copies, 'mp', 0, 0, axis_index_groups=z_groups, tiled=True)  31.7 us
    ppermute x4, starting transfers between devices, double_z(): theirs = lax.ppermute(x, 'mp', [(i, i ^ bit) for i in range(mp_count)])  26.9 us
    all_to_all x1, blocking collectives, body(): returned = lax.all_to_all(slots, 'seq', 0, 0, tiled=True).reshape(-1, half)  24.7 us
    ppermute x4, waiting for transfers between devices, double_z(): theirs = lax.ppermute(x, 'mp', [(i, i ^ bit) for i in range(mp_count)])  20 us
    all_to_all x1, blocking collectives, body(): lax.all_to_all(outgoing, 'seq', 0, 0, tiled=True).reshape(-1, half)  19 us
    all_to_all x2, starting transfers between devices, spread_z(): lax.all_to_all(copies, 'mp', 0, 0, axis_index_groups=z_groups, tiled=True)  16.2 us
  transfers between devices with their start and end apart: 17, of which 9 were waited for; matrix products, arithmetic and copies ran while one was open for 6% of the time, Pallas kernels for 0%

profile of v2, /device:TPU:1, one launch (start us, length us, event | category | flops | bytes accessed | tf_op | source)
XLA Modules:
  0.0 316.2 jit_solution(13460703812521659739)
XLA Ops:
  0.7 1.0 fusion.73
  1.6 8.8 %collective-permute-start = (bf16[8,1536]{1,0:T(8,128)(2,1)S(1)}, bf16[8,1536]{1,0:T(8,128)(2,1)S(1)}, u32[]{:S(2)}, u32[]{:S(2)}) collective-permute-start(bf16[8,1536]{1,0:T(8,128)(2,1)S(1)} %get-tuple-element.37), channel_id=1, source_target_pairs={{0,1},{1,0},{2,3},{3,2},{4,5},{5,4},{6,7},{7,6},{8,9},{9,8},{10,11... | collective-permute-start | bytes 73736 | tf_op jit(solution)/shard_map/ppermute | solution.py:55
  10.4 0.7 broadcast_multiply_fusion
  11.8 1.1 convolution_convert_fusion.3
  12.9 1.2 broadcast_in_dim.130
  14.1 3.7 %all-to-all-start = ((bf16[16,256,128]{2,1,0:T(8,128)(2,1)}), bf16[16,256,128]{2,1,0:T(8,128)(2,1)S(1)}, u32[]{:S(2)}, u32[]{:S(2)}) async-start(bf16[16,256,128]{2,1,0:T(8,128)(2,1)} %broadcast_in_dim.130), calls=%async_computation | async-start | bytes 2097152 | tf_op jit(solution)/shard_map/all_to_all | solution.py:129
  18.4 0.7 exponential_select_fusion.1
  19.2 13.2 %collective-permute-start.1 = (bf16[8,1536]{1,0:T(8,128)(2,1)S(1)}, bf16[8,1536]{1,0:T(8,128)(2,1)S(1)}, u32[]{:S(2)}, u32[]{:S(2)}) collective-permute-start(bf16[8,1536]{1,0:T(8,128)(2,1)S(1)} %maximum_select_fusion.1), channel_id=1, source_target_pairs={{0,16},{1,17},{2,18},{3,19},{4,20},{5,21},{6,22},{7,23},{8,24},{9,... | collective-permute-start | bytes 73736 | tf_op jit(solution)/shard_map/ppermute | solution.py:79
  33.6 5.5 %collective-permute-start.2 = (bf16[2,8,1536]{2,1,0:T(8,128)(2,1)S(1)}, bf16[2,8,1536]{2,1,0:T(8,128)(2,1)S(1)}, u32[]{:S(2)}, u32[]{:S(2)}) collective-permute-start(bf16[2,8,1536]{2,1,0:T(8,128)(2,1)S(1)} %pad_maximum_fusion.3), channel_id=1, source_target_pairs={{0,8},{1,9},{2,10},{3,11},{4,12},{5,13},{6,14},{7,15},{8,0},{9,1},... | collective-permute-start | bytes 147464 | tf_op jit(solution)/shard_map/ppermute | solution.py:79
  39.1 0.7 multiply_reduce_fusion.1
  41.3 4.1 %collective-permute-start.3 = (bf16[128,1536]{1,0:T(8,128)(2,1)S(1)}, bf16[128,1536]{1,0:T(8,128)(2,1)S(1)}, u32[]{:S(2)}, u32[]{:S(2)}) collective-permute-start(bf16[128,1536]{1,0:T(8,128)(2,1)S(1)} %convolution_convert_fusion.1), channel_id=1, source_target_pairs={{0,1},{1,0},{2,3},{3,2},{4,5},{5,4},{6,7},{7,6},{8,9},{9,8},{10,11... | collective-permute-start | bytes 1179656 | tf_op jit(solution)/shard_map/ppermute | solution.py:55
  45.4 1.3 collective-permute-done.3
  46.7 1.0 add_convert_fusion.1
  47.8 5.0 %collective-permute-start.4 = (bf16[2,2,8,1536]{3,2,1,0:T(8,128)(2,1)S(1)}, bf16[2,2,8,1536]{3,2,1,0:T(8,128)(2,1)S(1)}, u32[]{:S(2)}, u32[]{:S(2)}) collective-permute-start(bf16[2,2,8,1536]{3,2,1,0:T(8,128)(2,1)S(1)} %pad_maximum_fusion.2), channel_id=1, source_target_pairs={{0,4},{1,5},{2,6},{3,7},{4,0},{5,1},{6,2},{7,3},{8,12},{9,13},{10,... | collective-permute-start | bytes 294920 | tf_op jit(solution)/shard_map/ppermute | solution.py:79
  53.0 8.0 %all-to-all-start.1 = ((bf16[16,8,1536]{2,1,0:T(8,128)(2,1)}), bf16[16,8,1536]{2,1,0:T(8,128)(2,1)S(1)}, u32[]{:S(2)}, u32[]{:S(2)}) async-start(bf16[16,8,1536]{2,1,0:T(8,128)(2,1)} %bitcast.17), calls=%async_computation.1 | async-start | bytes 786432 | tf_op jit(solution)/shard_map/all_to_all | solution.py:86
  61.0 3.3 %collective-permute-start.5 = (bf16[2,2,2,8,1536]{4,3,2,1,0:T(8,128)(2,1)S(1)}, bf16[2,2,2,8,1536]{4,3,2,1,0:T(8,128)(2,1)S(1)}, u32[]{:S(2)}, u32[]{:S(2)}) collective-permute-start(bf16[2,2,2,8,1536]{4,3,2,1,0:T(8,128)(2,1)S(1)} %pad_maximum_fusion.1), channel_id=1, source_target_pairs={{0,2},{1,3},{2,0},{3,1},{4,6},{5,7},{6,4},{7,5},{8,10},{9,11},{10,... | collective-permute-start | bytes 589832 | tf_op jit(solution)/shard_map/ppermute | solution.py:79
  64.3 19.5 %collective-permute-done.5 = bf16[2,2,2,8,1536]{4,3,2,1,0:T(8,128)(2,1)S(1)} collective-permute-done((bf16[2,2,2,8,1536]{4,3,2,1,0:T(8,128)(2,1)S(1)}, bf16[2,2,2,8,1536]{4,3,2,1,0:T(8,128)(2,1)S(1)}, u32[]{:S(2)}, u32[]{:S(2)}) %collective-permute-start.5) | collective-permute-done | bytes 196640 | tf_op jit(solution)/shard_map/ppermute | solution.py:79
  84.1 3.9 %psum.14 = f32[8,1]{0,1:T(1,128)S(1)} all-reduce(f32[8,1]{0,1:T(1,128)S(1)} %bitcast.281), channel_id=1, replica_groups={{0,1},{2,3},{4,5},{6,7},{8,9},{10,11},{12,13},{14,15},{16,17},{18,19},{..., use_global_device_ids=true, to_apply=%region_3.4 | all-reduce | flops 8 | bytes 64 | tf_op jit(solution)/shard_map/psum | solution.py:165
  88.2 0.8 broadcast_in_dim.139
  88.9 10.0 %all-to-all-start.3 = ((bf16[16,8,1536]{2,1,0:T(8,128)(2,1)}), bf16[16,8,1536]{2,1,0:T(8,128)(2,1)S(1)}, u32[]{:S(2)}, u32[]{:S(2)}) async-start(bf16[16,8,1536]{2,1,0:T(8,128)(2,1)} %broadcast_in_dim.139), calls=%async_computation.3 | async-start | bytes 786432 | tf_op jit(solution)/shard_map/all_to_all | solution.py:72
  99.7 1.7 fusion
  101.5 14.6 %all-to-all-done.3 = bf16[16,8,1536]{2,1,0:T(8,128)(2,1)S(1)} async-done(((bf16[16,8,1536]{2,1,0:T(8,128)(2,1)}), bf16[16,8,1536]{2,1,0:T(8,128)(2,1)S(1)}, u32[]{:S(2)}, u32[]{:S(2)}) %all-to-all-start.3) | async-done | bytes 393248 | tf_op jit(solution)/shard_map/all_to_all | solution.py:72
  116.1 6.8 %all-to-all-start.2 = ((bf16[16,32,1536]{2,1,0:T(8,128)(2,1)}), bf16[16,32,1536]{2,1,0:T(8,128)(2,1)S(1)}, u32[]{:S(2)}, u32[]{:S(2)}) async-start(bf16[16,32,1536]{2,1,0:T(8,128)(2,1)} %bitcast.252), calls=%async_computation.2 | async-start | bytes 3145728 | tf_op jit(solution)/shard_map/all_to_all | solution.py:176
  122.9 0.7 fusion.58
  123.7 1.7 convolution_convert_fusion
  125.4 16.0 %all-to-all-done.2 = bf16[16,32,1536]{2,1,0:T(8,128)(2,1)S(1)} async-done(((bf16[16,32,1536]{2,1,0:T(8,128)(2,1)}), bf16[16,32,1536]{2,1,0:T(8,128)(2,1)S(1)}, u32[]{:S(2)}, u32[]{:S(2)}) %all-to-all-start.2) | async-done | bytes 1572896 | tf_op jit(solution)/shard_map/all_to_all | solution.py:176
  141.4 19.0 %all_to_all.45 = bf16[16,32,1536]{2,1,0:T(8,128)(2,1)S(1)} all-to-all(bf16[16,32,1536]{2,1,0:T(8,128)(2,1)} %bitcast.253), channel_id=1, replica_groups=mesh['seq'=16,'mp'=32] {'seq'}, dimensions={0} | all-to-all | bytes 3145728 | tf_op jit(solution)/shard_map/all_to_all | solution.py:179
  160.4 10.8 %collective-permute-start.7 = (bf16[512,1536]{1,0:T(8,128)(2,1)S(1)}, bf16[512,1536]{1,0:T(8,128)(2,1)S(1)}, u32[]{:S(2)}, u32[]{:S(2)}) collective-permute-start(bf16[512,1536]{1,0:T(8,128)(2,1)S(1)} %bitcast.247), channel_id=1, source_target_pairs={{0,1},{1,0},{2,3},{3,2},{4,5},{5,4},{6,7},{7,6},{8,9},{9,8},{10,11... | collective-permute-start | bytes 4718600 | tf_op jit(solution)/shard_map/ppermute | solution.py:55
  171.2 1.9 collective-permute-start.6
  176.5 0.7 multiply_convert_fusion
  177.2 0.7 fusion.7
  179.1 2.2 collective-permute-start.8
  182.0 2.4 collective-permute-done.8
  185.1 24.7 %all_to_all.46 = bf16[16,32,1536]{2,1,0:T(8,128)(2,1)S(1)} all-to-all(bf16[16,32,1536]{2,1,0:T(8,128)(2,1)S(1)} %bitcast.254), channel_id=1, replica_groups=mesh['seq'=16,'mp'=32] {'seq'}, dimensions={0} | all-to-all | bytes 3145728 | tf_op jit(solution)/shard_map/all_to_all | solution.py:195
  210.2 34.3 %all_to_all.47 = bf16[16,8,1536]{2,1,0:T(8,128)(2,1)S(1)} all-to-all(bf16[16,8,1536]{2,1,0:T(8,128)(2,1)S(1)} %fusion.3), channel_id=1, replica_groups={{0,2,4,6,8,10,12,14,16,18,20,22,24,26,28,30},{1,3,5,7,9,11,13,15,17,19,..., dimensions={0} | all-to-all | bytes 786432 | tf_op jit(solution)/shard_map/all_to_all | solution.py:86
  244.9 10.0 %psum.15 = f32[8,1]{0,1:T(1,128)S(1)} all-reduce(f32[8,1]{0,1:T(1,128)S(1)} %bitcast.282), channel_id=1, replica_groups={{0,1},{2,3},{4,5},{6,7},{8,9},{10,11},{12,13},{14,15},{16,17},{18,19},{..., use_global_device_ids=true, to_apply=%region_8.9 | all-reduce | flops 8 | bytes 64 | tf_op jit(solution)/shard_map/psum | solution.py:165
  255.0 0.8 broadcast_in_dim.141
  255.7 6.2 %all-to-all-start.7 = ((bf16[16,8,1536]{2,1,0:T(8,128)(2,1)}), bf16[16,8,1536]{2,1,0:T(8,128)(2,1)S(1)}, u32[]{:S(2)}, u32[]{:S(2)}) async-start(bf16[16,8,1536]{2,1,0:T(8,128)(2,1)} %broadcast_in_dim.141), calls=%async_computation.7 | async-start | bytes 786432 | tf_op jit(solution)/shard_map/all_to_all | solution.py:72
  262.1 17.0 %all-to-all-done.7 = bf16[16,8,1536]{2,1,0:T(8,128)(2,1)S(1)} async-done(((bf16[16,8,1536]{2,1,0:T(8,128)(2,1)}), bf16[16,8,1536]{2,1,0:T(8,128)(2,1)S(1)}, u32[]{:S(2)}, u32[]{:S(2)}) %all-to-all-start.7) | async-done | bytes 393248 | tf_op jit(solution)/shard_map/all_to_all | solution.py:72
  279.1 9.7 %collective-permute-start.9 = (bf16[128,1536]{1,0:T(8,128)(2,1)S(1)}, bf16[128,1536]{1,0:T(8,128)(2,1)S(1)}, u32[]{:S(2)}, u32[]{:S(2)}) collective-permute-start(bf16[128,1536]{1,0:T(8,128)(2,1)S(1)} %bitcast.260), channel_id=1, source_target_pairs={{0,1},{1,0},{2,3},{3,2},{4,5},{5,4},{6,7},{7,6},{8,9},{9,8},{10,11... | collective-permute-start | bytes 1179656 | tf_op jit(solution)/shard_map/ppermute | solution.py:55
  288.8 1.9 collective-permute-start.10
  291.9 1.2 broadcast_in_dim.144
  293.1 3.8 %all-to-all-start.8 = ((bf16[16,256,128]{2,1,0:T(8,128)(2,1)}), bf16[16,256,128]{2,1,0:T(8,128)(2,1)S(1)}, u32[]{:S(2)}, u32[]{:S(2)}) async-start(bf16[16,256,128]{2,1,0:T(8,128)(2,1)} %broadcast_in_dim.144), calls=%async_computation.8 | async-start | bytes 2097152 | tf_op jit(solution)/shard_map/all_to_all | solution.py:129
  298.2 0.7 copy.74
  299.0 14.3 %all-to-all-done.8 = bf16[16,256,128]{2,1,0:T(8,128)(2,1)S(1)} async-done(((bf16[16,256,128]{2,1,0:T(8,128)(2,1)}), bf16[16,256,128]{2,1,0:T(8,128)(2,1)S(1)}, u32[]{:S(2)}, u32[]{:S(2)}) %all-to-all-start.8) | async-done | bytes 1048608 | tf_op jit(solution)/shard_map/all_to_all | solution.py:129
  313.3 0.7 multiply_reduce_fusion
  314.6 0.7 copy.76
  315.5 0.7 copy.75
  (164 shorter events, 15.0 us)
Async XLA Ops:
  0.6 40.3 %copy-start = (bf16[256,3072]{1,0:T(8,128)(2,1)S(1)}, bf16[256,3072]{1,0:T(8,128)(2,1)}, u32[]{:S(2)}) copy-start(bf16[256,3072]{1,0:T(8,128)(2,1)} %param.17) | copy-start | bytes 4718596
  1.6 17.5 %collective-permute-start = (bf16[8,1536]{1,0:T(8,128)(2,1)S(1)}, bf16[8,1536]{1,0:T(8,128)(2,1)S(1)}, u32[]{:S(2)}, u32[]{:S(2)}) collective-permute-start(bf16[8,1536]{1,0:T(8,128)(2,1)S(1)} %get-tuple-element.37), channel_id=1, source_target_pairs={{0,1},{1,0},{2,3},{3,2},{4,5},{5,4},{6,7},{7,6},{8,9},{9,8},{10,11... | collective-permute-start | bytes 73736 | tf_op jit(solution)/shard_map/ppermute | solution.py:55
  11.1 21.3 %copy-start.33 = (f32[2]{0:T(128)}, f32[2]{0:T(128)S(1)}, u32[]{:S(2)}) copy-start(f32[2]{0:T(128)S(1)} %get-tuple-element.56) | copy-start | bytes 28
  14.1 24.9 %all-to-all-start = ((bf16[16,256,128]{2,1,0:T(8,128)(2,1)}), bf16[16,256,128]{2,1,0:T(8,128)(2,1)S(1)}, u32[]{:S(2)}, u32[]{:S(2)}) async-start(bf16[16,256,128]{2,1,0:T(8,128)(2,1)} %broadcast_in_dim.130), calls=%async_computation | async-start | bytes 2097152 | tf_op jit(solution)/shard_map/all_to_all | solution.py:129
  17.8 22.9 %copy-start.9 = (bf16[128,256]{1,0:T(8,128)(2,1)S(1)}, bf16[128,256]{1,0:T(8,128)(2,1)}, u32[]{:S(2)}) copy-start(bf16[128,256]{1,0:T(8,128)(2,1)} %param.15) | copy-start | bytes 196612
  18.0 23.2 %copy-start.17 = (f32[128,128]{1,0:T(8,128)}, f32[128,128]{1,0:T(8,128)S(1)}, u32[]{:S(2)}) copy-start(f32[128,128]{1,0:T(8,128)S(1)} %subtract_select_fusion) | copy-start | bytes 196612
  18.2 23.0 %copy-start.5 = (bf16[128,256]{0,1:T(8,128)(2,1)}, bf16[128,256]{0,1:T(8,128)(2,1)S(1)}, u32[]{:S(2)}) copy-start(bf16[128,256]{0,1:T(8,128)(2,1)S(1)} %copy.87) | copy-start | bytes 196612
  18.4 22.8 %copy-start.15 = (bf16[2,128,128]{2,1,0:T(8,128)(2,1)}, bf16[2,128,128]{2,1,0:T(8,128)(2,1)S(1)}, u32[]{:S(2)}) copy-start(bf16[2,128,128]{2,1,0:T(8,128)(2,1)S(1)} %fusion.16) | copy-start | bytes 196612
  19.1 68.9 %copy-start.11 = (bf16[4,1536]{1,0:T(4,128)(2,1)}, bf16[4,1536]{1,0:T(4,128)(2,1)S(1)}, u32[]{:S(2)}) copy-start(bf16[4,1536]{1,0:T(4,128)(2,1)S(1)} %get-tuple-element.40) | copy-start | bytes 36868
  19.2 22.0 %copy-start.20 = (bf16[8,1536]{1,0:T(8,128)(2,1)}, bf16[8,1536]{1,0:T(8,128)(2,1)S(1)}, u32[]{:S(2)}) copy-start(bf16[8,1536]{1,0:T(8,128)(2,1)S(1)} %maximum_select_fusion.1) | copy-start | bytes 73732
  19.2 14.4 %collective-permute-start.1 = (bf16[8,1536]{1,0:T(8,128)(2,1)S(1)}, bf16[8,1536]{1,0:T(8,128)(2,1)S(1)}, u32[]{:S(2)}, u32[]{:S(2)}) collective-permute-start(bf16[8,1536]{1,0:T(8,128)(2,1)S(1)} %maximum_select_fusion.1), channel_id=1, source_target_pairs={{0,16},{1,17},{2,18},{3,19},{4,20},{5,21},{6,22},{7,23},{8,24},{9,... | collective-permute-start | bytes 73736 | tf_op jit(solution)/shard_map/ppermute | solution.py:79
  33.0 8.2 %copy-start.31 = (f32[128,2]{0,1:T(2,128)}, f32[128,2]{0,1:T(2,128)S(1)}, u32[]{:S(2)}) copy-start(f32[128,2]{0,1:T(2,128)S(1)} %get-tuple-element.51) | copy-start | bytes 3076
  33.6 11.8 %collective-permute-start.2 = (bf16[2,8,1536]{2,1,0:T(8,128)(2,1)S(1)}, bf16[2,8,1536]{2,1,0:T(8,128)(2,1)S(1)}, u32[]{:S(2)}, u32[]{:S(2)}) collective-permute-start(bf16[2,8,1536]{2,1,0:T(8,128)(2,1)S(1)} %pad_maximum_fusion.3), channel_id=1, source_target_pairs={{0,8},{1,9},{2,10},{3,11},{4,12},{5,13},{6,14},{7,15},{8,0},{9,1},... | collective-permute-start | bytes 147464 | tf_op jit(solution)/shard_map/ppermute | solution.py:79
  40.9 11.9 %copy-start.35 = (f32[3072]{0:T(1024)S(1)}, f32[3072]{0:T(1024)}, u32[]{:S(2)}) copy-start(f32[3072]{0:T(1024)} %param.20) | copy-start | bytes 36868
  41.3 5.5 %collective-permute-start.3 = (bf16[128,1536]{1,0:T(8,128)(2,1)S(1)}, bf16[128,1536]{1,0:T(8,128)(2,1)S(1)}, u32[]{:S(2)}, u32[]{:S(2)}) collective-permute-start(bf16[128,1536]{1,0:T(8,128)(2,1)S(1)} %convolution_convert_fusion.1), channel_id=1, source_target_pairs={{0,1},{1,0},{2,3},{3,2},{4,5},{5,4},{6,7},{7,6},{8,9},{9,8},{10,11... | collective-permute-start | bytes 1179656 | tf_op jit(solution)/shard_map/ppermute | solution.py:55
  45.4 18.9 %copy-start.39 = (s32[128,2]{0,1:T(2,128)S(1)}, s32[128,2]{0,1:T(2,128)}, u32[]{:S(2)}) copy-start(s32[128,2]{0,1:T(2,128)} %param.21) | copy-start | bytes 3076
  47.8 13.2 %collective-permute-start.4 = (bf16[2,2,8,1536]{3,2,1,0:T(8,128)(2,1)S(1)}, bf16[2,2,8,1536]{3,2,1,0:T(8,128)(2,1)S(1)}, u32[]{:S(2)}, u32[]{:S(2)}) collective-permute-start(bf16[2,2,8,1536]{3,2,1,0:T(8,128)(2,1)S(1)} %pad_maximum_fusion.2), channel_id=1, source_target_pairs={{0,4},{1,5},{2,6},{3,7},{4,0},{5,1},{6,2},{7,3},{8,12},{9,13},{10,... | collective-permute-start | bytes 294920 | tf_op jit(solution)/shard_map/ppermute | solution.py:79
  52.9 35.2 %copy-start.24 = (f32[1536]{0:T(1024)}, f32[1536]{0:T(1024)S(1)}, u32[]{:S(2)}) copy-start(f32[1536]{0:T(1024)S(1)} %dynamic_slice.55) | copy-start | bytes 18436
  53.0 31.0 %all-to-all-start.1 = ((bf16[16,8,1536]{2,1,0:T(8,128)(2,1)}), bf16[16,8,1536]{2,1,0:T(8,128)(2,1)S(1)}, u32[]{:S(2)}, u32[]{:S(2)}) async-start(bf16[16,8,1536]{2,1,0:T(8,128)(2,1)} %bitcast.17), calls=%async_computation.1 | async-start | bytes 786432 | tf_op jit(solution)/shard_map/all_to_all | solution.py:86
  61.0 22.8 %collective-permute-start.5 = (bf16[2,2,2,8,1536]{4,3,2,1,0:T(8,128)(2,1)S(1)}, bf16[2,2,2,8,1536]{4,3,2,1,0:T(8,128)(2,1)S(1)}, u32[]{:S(2)}, u32[]{:S(2)}) collective-permute-start(bf16[2,2,2,8,1536]{4,3,2,1,0:T(8,128)(2,1)S(1)} %pad_maximum_fusion.1), channel_id=1, source_target_pairs={{0,2},{1,3},{2,0},{3,1},{4,6},{5,7},{6,4},{7,5},{8,10},{9,11},{10,... | collective-permute-start | bytes 589832 | tf_op jit(solution)/shard_map/ppermute | solution.py:79
  83.9 15.4 %copy-start.40 = (f32[128,2]{0,1:T(2,128)S(1)}, f32[128,2]{0,1:T(2,128)}, u32[]{:S(2)}) copy-start(f32[128,2]{0,1:T(2,128)} %param.22) | copy-start | bytes 3076
  84.0 17.5 %copy-start.3 = (f32[8,1536]{1,0:T(8,128)}, f32[8,1536]{1,0:T(8,128)S(1)}, u32[]{:S(2)}) copy-start(f32[8,1536]{1,0:T(8,128)S(1)} %convert_reduce_fusion.1) | copy-start | bytes 147460
  88.1 13.4 %copy-start.36 = (f32[8]{0:T(128)}, f32[8]{0:T(128)S(1)}, u32[]{:S(2)}) copy-start(f32[8]{0:T(128)S(1)} %rsqrt_bitcast_fusion) | copy-start | bytes 100
  88.9 27.2 %all-to-all-start.3 = ((bf16[16,8,1536]{2,1,0:T(8,128)(2,1)}), bf16[16,8,1536]{2,1,0:T(8,128)(2,1)S(1)}, u32[]{:S(2)}, u32[]{:S(2)}) async-start(bf16[16,8,1536]{2,1,0:T(8,128)(2,1)} %broadcast_in_dim.139), calls=%async_computation.3 | async-start | bytes 786432 | tf_op jit(solution)/shard_map/all_to_all | solution.py:72
  99.3 16.8 %copy-start.22 = (s32[16,128]{1,0:T(8,128)}, s32[16,128]{1,0:T(8,128)S(1)}, u32[]{:S(2)}) copy-start(s32[16,128]{1,0:T(8,128)S(1)} %copy.65) | copy-start | bytes 24580
  116.1 25.3 %all-to-all-start.2 = ((bf16[16,32,1536]{2,1,0:T(8,128)(2,1)}), bf16[16,32,1536]{2,1,0:T(8,128)(2,1)S(1)}, u32[]{:S(2)}, u32[]{:S(2)}) async-start(bf16[16,32,1536]{2,1,0:T(8,128)(2,1)} %bitcast.252), calls=%async_computation.2 | async-start | bytes 3145728 | tf_op jit(solution)/shard_map/all_to_all | solution.py:176
  141.4 31.8 %copy-start.19 = (bf16[1,144,3072]{2,1,0:T(8,128)(2,1)S(1)}, bf16[1,144,3072]{2,1,0:T(8,128)(2,1)}, u32[]{:S(2)}) copy-start(bf16[1,144,3072]{2,1,0:T(8,128)(2,1)} %param.25) | copy-start | bytes 2654212
  160.4 13.4 %copy-start.1 = (bf16[1,3072,144]{1,2,0:T(8,128)(2,1)S(1)}, bf16[1,3072,144]{1,2,0:T(8,128)(2,1)}, u32[]{:S(2)}) copy-start(bf16[1,3072,144]{1,2,0:T(8,128)(2,1)} %param.23) | copy-start | bytes 2654212
  160.4 15.2 %collective-permute-start.7 = (bf16[512,1536]{1,0:T(8,128)(2,1)S(1)}, bf16[512,1536]{1,0:T(8,128)(2,1)S(1)}, u32[]{:S(2)}, u32[]{:S(2)}) collective-permute-start(bf16[512,1536]{1,0:T(8,128)(2,1)S(1)} %bitcast.247), channel_id=1, source_target_pairs={{0,1},{1,0},{2,3},{3,2},{4,5},{5,4},{6,7},{7,6},{8,9},{9,8},{10,11... | collective-permute-start | bytes 4718600 | tf_op jit(solution)/shard_map/ppermute | solution.py:55
  171.2 5.3 %collective-permute-start.6 = (bf16[512,1536]{1,0:T(8,128)(2,1)S(1)}, bf16[512,1536]{1,0:T(8,128)(2,1)S(1)}, u32[]{:S(2)}, u32[]{:S(2)}) collective-permute-start(bf16[512,1536]{1,0:T(8,128)(2,1)S(1)} %bitcast.250), channel_id=1, source_target_pairs={{0,1},{1,0},{2,3},{3,2},{4,5},{5,4},{6,7},{7,6},{8,9},{9,8},{10,11... | collective-permute-start | bytes 4718600 | tf_op jit(solution)/shard_map/ppermute | solution.py:55
  179.1 5.3 %collective-permute-start.8 = (bf16[512,1536]{1,0:T(8,128)(2,1)S(1)}, bf16[512,1536]{1,0:T(8,128)(2,1)S(1)}, u32[]{:S(2)}, u32[]{:S(2)}) collective-permute-start(bf16[512,1536]{1,0:T(8,128)(2,1)S(1)} %fusion.1), channel_id=1, source_target_pairs={{0,1},{1,0},{2,3},{3,2},{4,5},{5,4},{6,7},{7,6},{8,9},{9,8},{10,11... | collective-permute-start | bytes 4718600 | tf_op jit(solution)/shard_map/ppermute | solution.py:55
  185.1 24.7 %copy-start.23 = (s32[16,128]{1,0:T(8,128)S(1)}, s32[16,128]{1,0:T(8,128)}, u32[]{:S(2)}) copy-start(s32[16,128]{1,0:T(8,128)} %copy-done.22) | copy-start | bytes 24580
  209.8 34.8 %copy-start.4 = (f32[8,1536]{1,0:T(8,128)S(1)}, f32[8,1536]{1,0:T(8,128)}, u32[]{:S(2)}) copy-start(f32[8,1536]{1,0:T(8,128)} %copy-done.3) | copy-start | bytes 147460
  209.8 34.8 %copy-start.12 = (bf16[4,1536]{1,0:T(4,128)(2,1)S(1)}, bf16[4,1536]{1,0:T(4,128)(2,1)}, u32[]{:S(2)}) copy-start(bf16[4,1536]{1,0:T(4,128)(2,1)} %copy-done.11) | copy-start | bytes 36868
  209.8 34.9 %copy-start.25 = (f32[1536]{0:T(1024)S(1)}, f32[1536]{0:T(1024)}, u32[]{:S(2)}) copy-start(f32[1536]{0:T(1024)} %copy-done.24) | copy-start | bytes 18436
  209.8 34.9 %copy-start.37 = (f32[8]{0:T(128)S(1)}, f32[8]{0:T(128)}, u32[]{:S(2)}) copy-start(f32[8]{0:T(128)} %copy-done.36) | copy-start | bytes 100
  209.8 45.1 %copy-start.21 = (bf16[8,1536]{1,0:T(8,128)(2,1)S(1)}, bf16[8,1536]{1,0:T(8,128)(2,1)}, u32[]{:S(2)}) copy-start(bf16[8,1536]{1,0:T(8,128)(2,1)} %copy-done.20) | copy-start | bytes 73732
  210.2 51.7 %copy-start.29 = (f32[16,2]{1,0:T(8,128)S(1)}, f32[16,2]{1,0:T(8,128)}, u32[]{:S(2)}) copy-start(f32[16,2]{1,0:T(8,128)} %get-tuple-element.52) | copy-start | bytes 388
  255.7 23.4 %all-to-all-start.7 = ((bf16[16,8,1536]{2,1,0:T(8,128)(2,1)}), bf16[16,8,1536]{2,1,0:T(8,128)(2,1)S(1)}, u32[]{:S(2)}, u32[]{:S(2)}) async-start(bf16[16,8,1536]{2,1,0:T(8,128)(2,1)} %broadcast_in_dim.141), calls=%async_computation.7 | async-start | bytes 786432 | tf_op jit(solution)/shard_map/all_to_all | solution.py:72
  261.9 29.7 %copy-start.6 = (bf16[128,256]{0,1:T(8,128)(2,1)S(1)}, bf16[128,256]{0,1:T(8,128)(2,1)}, u32[]{:S(2)}) copy-start(bf16[128,256]{0,1:T(8,128)(2,1)} %copy-done.5) | copy-start | bytes 196612
  262.0 29.7 %copy-start.38 = (f32[2,128]{1,0:T(2,128)S(1)}, f32[2,128]{1,0:T(2,128)}, u32[]{:S(2)}) copy-start(f32[2,128]{1,0:T(2,128)} %get-tuple-element.44) | copy-start | bytes 3076
  279.1 12.0 %collective-permute-start.9 = (bf16[128,1536]{1,0:T(8,128)(2,1)S(1)}, bf16[128,1536]{1,0:T(8,128)(2,1)S(1)}, u32[]{:S(2)}, u32[]{:S(2)}) collective-permute-start(bf16[128,1536]{1,0:T(8,128)(2,1)S(1)} %bitcast.260), channel_id=1, source_target_pairs={{0,1},{1,0},{2,3},{3,2},{4,5},{5,4},{6,7},{7,6},{8,9},{9,8},{10,11... | collective-permute-start | bytes 1179656 | tf_op jit(solution)/shard_map/ppermute | solution.py:55
  288.8 8.1 %collective-permute-start.10 = (bf16[4,1536]{1,0:T(4,128)(2,1)S(1)}, bf16[4,1536]{1,0:T(4,128)(2,1)S(1)}, u32[]{:S(2)}, u32[]{:S(2)}) collective-permute-start(bf16[4,1536]{1,0:T(4,128)(2,1)S(1)} %get-tuple-element.39), channel_id=1, source_target_pairs={{0,1},{1,0},{2,3},{3,2},{4,5},{5,4},{6,7},{7,6},{8,9},{9,8},{10,11... | collective-permute-start | bytes 36872 | tf_op jit(solution)/shard_map/ppermute | solution.py:55
  291.9 5.9 %copy-start.10 = (bf16[128,256]{1,0:T(8,128)(2,1)S(1)}, bf16[128,256]{1,0:T(8,128)(2,1)}, u32[]{:S(2)}) copy-start(bf16[128,256]{1,0:T(8,128)(2,1)} %param.15) | copy-start | bytes 196612
  291.9 5.8 %copy-start.18 = (f32[128,128]{1,0:T(8,128)S(1)}, f32[128,128]{1,0:T(8,128)}, u32[]{:S(2)}) copy-start(f32[128,128]{1,0:T(8,128)} %copy-done.17) | copy-start | bytes 196612
  293.1 20.2 %all-to-all-start.8 = ((bf16[16,256,128]{2,1,0:T(8,128)(2,1)}), bf16[16,256,128]{2,1,0:T(8,128)(2,1)S(1)}, u32[]{:S(2)}, u32[]{:S(2)}) async-start(bf16[16,256,128]{2,1,0:T(8,128)(2,1)} %broadcast_in_dim.144), calls=%async_computation.8 | async-start | bytes 2097152 | tf_op jit(solution)/shard_map/all_to_all | solution.py:129
  296.9 17.1 %copy-start.30 = (f32[128,2]{0,1:T(2,128)S(1)}, f32[128,2]{0,1:T(2,128)}, u32[]{:S(2)}) copy-start(f32[128,2]{0,1:T(2,128)} %get-tuple-element.50) | copy-start | bytes 3076
  296.9 17.5 %copy-start.16 = (bf16[2,128,128]{2,1,0:T(8,128)(2,1)S(1)}, bf16[2,128,128]{2,1,0:T(8,128)(2,1)}, u32[]{:S(2)}) copy-start(bf16[2,128,128]{2,1,0:T(8,128)(2,1)} %copy-done.15) | copy-start | bytes 196612
  (10 other events, 41.4 us)

commit v3 on v2

--- a/solution.py
+++ b/solution.py
@@ -72,14 +72,16 @@
         out = lax.all_to_all(copies, "mp", 0, 0, axis_index_groups=z_groups, tiled=True)
         return out.reshape((z_count * x.shape[0],) + x.shape[1:])
 
-    z_bits = z_count.bit_length() - 1
-
-    def double_z(x, level):
-        bit = 2 << (z_bits - 1 - level)
-        theirs = lax.ppermute(x, "mp", [(i, i ^ bit) for i in range(mp_count)])
-        upper = lax.rem(lax.axis_index("mp") // bit, 2) == 1
-        first, second = jnp.where(upper, theirs, x), jnp.where(upper, x, theirs)
-        return jnp.stack([first, second], axis=level)
+    z_odd = lax.rem(lax.axis_index("mp") // 2, 2)
+
+    def own_quarter(x):
+        return lax.dynamic_slice_in_dim(x, z_odd * (half // 2), half // 2, 1)
+
+    def other_quarter(x):
+        return lax.dynamic_slice_in_dim(x, (1 - z_odd) * (half // 2), half // 2, 1)
+
+    def across_z(x, offset):
+        return lax.ppermute(x, "mp", [(i, i ^ (2 * offset)) for i in range(mp_count)])
 
     def sum_z(x):
         parts = x.reshape(z_count, pair_share, half)
@@ -105,13 +107,6 @@
     placed = (chosen.T[:, None, :] == 1) & (ranking.T[:, None, :] == slot_ids[None, :, None])
     placing = placed.astype(BF16).reshape(seq_count * capacity, length)
     slot_weight = jnp.sum(jnp.where(placed, weight.T[:, None, :], 0.0), axis=2)
-
-    both = jnp.concatenate([inputs, cotangent], axis=0)
-    both_kept, both_got = own_half(both, 1), swap(other_half(both, 1))
-    pair_inputs = by_core(both_kept[:tok_share], both_got[:tok_share], 0).astype(F32)
-    pair_cot_b = by_core(both_kept[tok_share:], both_got[tok_share:], 0)
-    pair_cot = pair_cot_b.astype(F32)
-    gain = own_half(norm_gain, 0)[None, :]
 
     query_heads, key_heads, value_heads = map(to_heads, (queries, key_rows, value_rows))
     places = jnp.arange(length).astype(F32)
@@ -140,6 +135,23 @@
         (step_decay * tail_decay * key_heads.astype(F32)).astype(BF16),
         value_heads,
     )
+    local_state = local_state.astype(BF16)
+
+    both = jnp.concatenate([inputs, cotangent], axis=0)
+    hidden_units = w_down.shape[1]
+    both, gate_in, up_in, down_in, local_state = lax.optimization_barrier(
+        (both, w_gate[0], w_up[0], w_down[0], local_state)
+    )
+    weights = jnp.concatenate([gate_in.T, up_in.T, down_in], axis=0)
+    both_kept, both_got = own_half(both, 1), swap(other_half(both, 1))
+    weights_kept, weights_got = lax.optimization_barrier(
+        (own_half(weights, 1), swap(other_half(weights, 1)))
+    )
+    pair_inputs = by_core(both_kept[:tok_share], both_got[:tok_share], 0).astype(F32)
+    pair_cot_b = by_core(both_kept[tok_share:], both_got[tok_share:], 0)
+    pair_cot = pair_cot_b.astype(F32)
+    gain = own_half(norm_gain, 0)[None, :]
+
     entering = combine_states(exchange_states(local_state), seq_place - 1 - peers)
     entering_b = entering.astype(BF16)
     scores = heads_dot("htd,hsd->hts", query_heads, key_heads) * decay_band
@@ -151,14 +163,18 @@
     out_own, out_other = own_half(w_out, 1), other_half(w_out, 1)
     got = swap(mm(attended_b, out_other).astype(BF16))
     chip_mixed = (mm(attended_b, out_own) + got.astype(F32)).astype(BF16)
-    block_cot = pair_cot_b
-    for level in range(z_bits // 2):
-        block_cot = double_z(block_cot, level)
-    block_cot, chip_mixed = lax.optimization_barrier((block_cot, chip_mixed))
-    for level in range(z_bits // 2, z_bits):
-        block_cot = double_z(block_cot, level)
-    block_cot = block_cot.reshape(length, half)
-    stream = pair_inputs + sum_z(chip_mixed)
+    quarters = pair_cot_b.reshape(pair_share, 2, half // 2).transpose(1, 0, 2)
+    quarters = jnp.broadcast_to(quarters[None], (z_count // 2,) + quarters.shape)
+    sent = jnp.concatenate(
+        [
+            chip_mixed.reshape(z_count, pair_share, half),
+            quarters.reshape(z_count, pair_share, half // 2),
+        ],
+        axis=2,
+    )
+    arrived = lax.all_to_all(sent, "mp", 0, 0, axis_index_groups=z_groups, tiled=True)
+    stream = pair_inputs + jnp.sum(arrived[:, :, :half].astype(F32), axis=0)
+    block_cot = arrived[:, :, half:].reshape(length, half // 2)
 
     def over_features(x):
         total = jnp.sum(x, axis=1, keepdims=True)
@@ -167,29 +183,41 @@
     inverse = lax.rsqrt(over_features(stream * stream) + EPSILON)
     normed = stream * inverse
     expert_in = (normed * gain).astype(BF16)
-    block_cot, expert_in = lax.optimization_barrier((block_cot, expert_in))
+
 
     group_in = spread_z(expert_in)
     outgoing = mm(placing, group_in).astype(BF16).reshape(seq_count, capacity, half)
     weighted = (slot_weight.reshape(-1, 1) * mm(placing, block_cot)).astype(BF16)
-    weighted = weighted.reshape(seq_count, capacity, half)
-    cot_own = lax.all_to_all(weighted, "seq", 0, 0, tiled=True).reshape(-1, half)
+    cot_own = lax.all_to_all(
+        weighted.reshape(seq_count, capacity, half // 2), "seq", 0, 0, tiled=True
+    ).reshape(-1, half // 2)
     cot_own, outgoing = lax.optimization_barrier((cot_own, outgoing))
-    cot_other = swap(cot_own)
-    rows_own = lax.all_to_all(outgoing, "seq", 0, 0, tiled=True).reshape(-1, half)
-    rows_other = swap(rows_own)
-    gate_own, gate_other = own_half(w_gate[0], 0), other_half(w_gate[0], 0)
-    up_own, up_other = own_half(w_up[0], 0), other_half(w_up[0], 0)
-
-    down_own, down_other = own_half(w_down[0], 1), other_half(w_down[0], 1)
-    hidden_grad = mm_t(cot_own, down_own) + mm_t(cot_other, down_other)
-    gate_pre = mm(rows_own, gate_own) + mm(rows_other, gate_other)
-    up_pre = mm(rows_own, up_own) + mm(rows_other, up_other)
+    cot_pair = across_z(cot_own, 1)
+    rows = lax.all_to_all(outgoing, "seq", 0, 0, tiled=True).reshape(-1, half)
+
+    def features_part(part):
+        pre = mm_t(part[: 2 * hidden_units], rows)
+        down = part[2 * hidden_units :]
+        hidden = mm_t(own_quarter(down), cot_own) + mm_t(other_quarter(down), cot_pair)
+        return jnp.concatenate([pre, hidden], axis=0)
+
+    got = swap(features_part(weights_got))
+    pre = features_part(weights_kept) + got
+    gate_pre, up_pre = pre[:hidden_units], pre[hidden_units : 2 * hidden_units]
+    hidden_grad = pre[2 * hidden_units :]
     sigma = jax.nn.sigmoid(gate_pre)
     gate_grad = (hidden_grad * up_pre * sigma * (1.0 + gate_pre * (1.0 - sigma))).astype(BF16)
     up_grad = (hidden_grad * gate_pre * sigma).astype(BF16)
-    got = swap((mm_t(gate_grad, gate_other) + mm_t(up_grad, up_other)).astype(BF16))
-    slots = mm_t(gate_grad, gate_own) + mm_t(up_grad, up_own) + got.astype(F32)
+    grads = jnp.concatenate([gate_grad, up_grad], axis=0)
+    grads_got = swap(grads)
+
+    def units_part(units, part):
+        return lax.dot_general(
+            units, part, (((0,), (0,)), ((), ())), preferred_element_type=F32
+        )
+
+    slots = units_part(grads, weights_kept[: 2 * hidden_units])
+    slots = slots + units_part(grads_got, weights_got[: 2 * hidden_units])
     slots = slots.astype(BF16).reshape(seq_count, capacity, half)
 
     returned = lax.all_to_all(slots, "seq", 0, 0, tiled=True).reshape(-1, half)
@@ -200,10 +228,6 @@
     scaled = expert_grad * gain
     stream_grad = inverse * (scaled - normed * over_features(scaled * normed)) + pair_cot
     pair_grad = stream_grad.astype(BF16)
-
-    pair_kept = lax.dynamic_slice_in_dim(pair_grad, core * tok_share, tok_share, 0)
-    pair_sent = lax.dynamic_slice_in_dim(pair_grad, (1 - core) * tok_share, tok_share, 0)
-    input_grad = by_core(pair_kept, swap(pair_sent), 1)
 
     block_own = spread_z(pair_grad)
     block_other = swap(block_own)
@@ -227,6 +251,10 @@
     query_grad = from_heads(query_part).astype(BF16)
     key_grad = from_heads(key_part).astype(BF16)
     value_grad = from_heads(value_part).astype(BF16)
+    def own_tokens(x):
+        return lax.dynamic_slice_in_dim(x, lax.axis_index("mp") * tok_share, tok_share, 0)
+
+    input_grad = by_core(own_tokens(block_own), own_tokens(block_other), 1)
     return (query_grad, key_grad, value_grad, input_grad)
 
 

time: 318 us -> 303 us (0.953)
  blocking collectives: 92 us -> 69.8 us
  starting transfers between devices: 105 us -> 91 us
  waiting for transfers between devices: 85.9 us -> 97.1 us
  matrix products: 15.7 us -> 19.2 us
  local copies, waits for them, and re-layouts: 8.21 us -> 11.7 us
    ppermute x4 -> x1, starting transfers between devices: 26.9 us -> 2.84 us  [across_z(): return lax.ppermute(x, 'mp', [(i, i ^ 2 * offset) for i in range(mp_count)])]
    all_to_all x1 -> x0, blocking collectives: 19 us -> none  [body(): lax.all_to_all(outgoing, 'seq', 0, 0, tiled=True).reshape(-1, half)]
    all_to_all x2 -> x3, starting transfers between devices: 14.8 us -> 25.6 us  [the longest x1 15.1 us: body(): lax.all_to_all(sent, 'mp', 0, 0, axis_index_groups=z_groups, tiled=True)]
    all_to_all x2 -> x3, waiting for transfers between devices: 16 us -> 26.1 us  [the longest x1 24.9 us: body(): lax.all_to_all(sent, 'mp', 0, 0, axis_index_groups=z_groups, tiled=True)]
    all_to_all x1, blocking collectives: 34.3 us -> 24.9 us  [sum_z(): lax.all_to_all(parts, 'mp', 0, 0, axis_index_groups=z_groups, tiled=True)]
    all_to_all x2, waiting for transfers between devices: 14.3 us -> 20.5 us  [exchange_states(): return lax.all_to_all(sent, 'seq', 0, 0, tiled=True)]
    ppermute x4 -> x1, waiting for transfers between devices: 20 us -> 14.9 us  [across_z(): return lax.ppermute(x, 'mp', [(i, i ^ 2 * offset) for i in range(mp_count)])]
    psum x2, blocking collectives: 13.9 us -> 18.6 us  [over_features(): return lax.psum(total, 'mp', axis_index_groups=core_groups) / width]
  transfers between devices with their start and end apart: 17 -> 14, of which waited for: 9 -> 10; matrix products, arithmetic and copies ran while one was open for 6% -> 7% of each run, Pallas kernels for 0% -> 0%
where the time goes in v3:
time: 303 us; the launch traced here: 301 us
  waiting for transfers between devices  97.1 us (32%)
  starting transfers between devices  91 us (30%)
  blocking collectives  69.8 us (23%)
  matrix products  19.2 us (6%)
  local copies, waits for them, and re-layouts  11.7 us (4%)
  other arithmetic  10.9 us (4%)
    ppermute x6, starting transfers between devices, swap(): return lax.ppermute(x, 'mp', swap_pairs)  38 us
    all_to_all x2, waiting for transfers between devices, spread_z(): lax.all_to_all(copies, 'mp', 0, 0, axis_index_groups=z_groups, tiled=True)  32.5 us
    all_to_all x1, blocking collectives, body(): returned = lax.all_to_all(slots, 'seq', 0, 0, tiled=True).reshape(-1, half)  26.3 us
    all_to_all x1, waiting for transfers between devices, body(): lax.all_to_all(sent, 'mp', 0, 0, axis_index_groups=z_groups, tiled=True)  24.9 us
    all_to_all x1, blocking collectives, sum_z(): lax.all_to_all(parts, 'mp', 0, 0, axis_index_groups=z_groups, tiled=True)  24.9 us
    all_to_all x2, waiting for transfers between devices, exchange_states(): return lax.all_to_all(sent, 'seq', 0, 0, tiled=True)  20.5 us
    psum x2, blocking collectives, over_features(): return lax.psum(total, 'mp', axis_index_groups=core_groups) / width  18.6 us
    all_to_all x1, starting transfers between devices, body(): lax.all_to_all(sent, 'mp', 0, 0, axis_index_groups=z_groups, tiled=True)  15.1 us
  transfers between devices with their start and end apart: 14, of which 10 were waited for; matrix products, arithmetic and copies ran while one was open for 7% of the time, Pallas kernels for 0%

profile of v3, /device:TPU:1, one launch (start us, length us, event | category | flops | bytes accessed | tf_op | source)
XLA Modules:
  0.0 301.4 jit_solution(16462821883404873568)
XLA Ops:
  0.7 0.8 broadcast_multiply_fusion
  1.4 0.8 pad_maximum_fusion.4
  2.9 1.1 convolution_convert_fusion.3
  4.1 1.2 broadcast_in_dim.136
  5.3 7.6 %all-to-all-start = ((bf16[16,256,128]{2,1,0:T(8,128)(2,1)}), bf16[16,256,128]{2,1,0:T(8,128)(2,1)S(1)}, u32[]{:S(2)}, u32[]{:S(2)}) async-start(bf16[16,256,128]{2,1,0:T(8,128)(2,1)} %broadcast_in_dim.136), calls=%async_computation | async-start | bytes 2097152 | tf_op jit(solution)/shard_map/all_to_all | solution.py:124
  12.9 4.9 %collective-permute-start = (bf16[8,1536]{1,0:T(8,128)(2,1)S(1)}, bf16[8,1536]{1,0:T(8,128)(2,1)S(1)}, u32[]{:S(2)}, u32[]{:S(2)}) collective-permute-start(bf16[8,1536]{1,0:T(8,128)(2,1)S(1)} %constant_dynamic-slice_fusion.5), channel_id=1, source_target_pairs={{0,1},{1,0},{2,3},{3,2},{4,5},{5,4},{6,7},{7,6},{8,9},{9,8},{10,11... | collective-permute-start | bytes 73736 | tf_op jit(solution)/shard_map/ppermute | solution.py:55
  20.6 6.8 %all-to-all-done = bf16[16,256,128]{2,1,0:T(8,128)(2,1)S(1)} async-done(((bf16[16,256,128]{2,1,0:T(8,128)(2,1)}), bf16[16,256,128]{2,1,0:T(8,128)(2,1)S(1)}, u32[]{:S(2)}, u32[]{:S(2)}) %all-to-all-start) | async-done | bytes 1048608 | tf_op jit(solution)/shard_map/all_to_all | solution.py:124
  29.5 6.0 %collective-permute-start.1 = (bf16[128,1536]{1,0:T(8,128)(2,1)S(1)}, bf16[128,1536]{1,0:T(8,128)(2,1)S(1)}, u32[]{:S(2)}, u32[]{:S(2)}) collective-permute-start(bf16[128,1536]{1,0:T(8,128)(2,1)S(1)} %convolution_convert_fusion.1), channel_id=1, source_target_pairs={{0,1},{1,0},{2,3},{3,2},{4,5},{5,4},{6,7},{7,6},{8,9},{9,8},{10,11... | collective-permute-start | bytes 1179656 | tf_op jit(solution)/shard_map/ppermute | solution.py:55
  35.6 1.2 collective-permute-done.1
  37.1 0.9 pad_maximum_fusion.2
  38.0 15.1 %all-to-all-start.1 = ((bf16[16,8,2304]{2,1,0:T(8,128)(2,1)}), bf16[16,8,2304]{2,1,0:T(8,128)(2,1)S(1)}, u32[]{:S(2)}, u32[]{:S(2)}) async-start(bf16[16,8,2304]{2,1,0:T(8,128)(2,1)} %pad_maximum_fusion.2), calls=%async_computation.1 | async-start | bytes 1179648 | tf_op jit(solution)/shard_map/all_to_all | solution.py:175
  53.5 24.9 %all-to-all-done.1 = bf16[16,8,2304]{2,1,0:T(8,128)(2,1)S(1)} async-done(((bf16[16,8,2304]{2,1,0:T(8,128)(2,1)}), bf16[16,8,2304]{2,1,0:T(8,128)(2,1)S(1)}, u32[]{:S(2)}, u32[]{:S(2)}) %all-to-all-start.1) | async-done | bytes 589856 | tf_op jit(solution)/shard_map/all_to_all | solution.py:175
  78.6 8.5 %psum.14 = f32[8,1]{0,1:T(1,128)S(1)} all-reduce(f32[8,1]{0,1:T(1,128)S(1)} %bitcast.232), channel_id=1, replica_groups={{0,1},{2,3},{4,5},{6,7},{8,9},{10,11},{12,13},{14,15},{16,17},{18,19},{..., use_global_device_ids=true, to_apply=%region_3.4 | all-reduce | flops 8 | bytes 64 | tf_op jit(solution)/shard_map/psum | solution.py:181
  87.2 0.8 broadcast_in_dim.146
  88.0 7.2 %all-to-all-start.3 = ((bf16[16,8,1536]{2,1,0:T(8,128)(2,1)}), bf16[16,8,1536]{2,1,0:T(8,128)(2,1)S(1)}, u32[]{:S(2)}, u32[]{:S(2)}) async-start(bf16[16,8,1536]{2,1,0:T(8,128)(2,1)} %broadcast_in_dim.146), calls=%async_computation.3 | async-start | bytes 786432 | tf_op jit(solution)/shard_map/all_to_all | solution.py:72
  95.6 1.3 multiply_convert_fusion
  96.9 15.5 %all-to-all-done.3 = bf16[16,8,1536]{2,1,0:T(8,128)(2,1)S(1)} async-done(((bf16[16,8,1536]{2,1,0:T(8,128)(2,1)}), bf16[16,8,1536]{2,1,0:T(8,128)(2,1)S(1)}, u32[]{:S(2)}, u32[]{:S(2)}) %all-to-all-start.3) | async-done | bytes 393248 | tf_op jit(solution)/shard_map/all_to_all | solution.py:72
  112.4 3.6 %all-to-all-start.2 = ((bf16[16,32,768]{2,1,0:T(8,128)(2,1)}), bf16[16,32,768]{2,1,0:T(8,128)(2,1)S(1)}, u32[]{:S(2)}, u32[]{:S(2)}) async-start(bf16[16,32,768]{2,1,0:T(8,128)(2,1)} %bitcast.29), calls=%async_computation.2 | async-start | bytes 1572864 | tf_op jit(solution)/shard_map/all_to_all | solution.py:191
  116.0 1.9 pad_maximum_fusion
  117.9 1.7 constant_dynamic-slice_fusion.3
  119.6 9.7 %collective-permute-start.2 = (bf16[432,1536]{1,0:T(8,128)(2,1)}, bf16[432,1536]{1,0:T(8,128)(2,1)}, u32[]{:S(2)}, u32[]{:S(2)}) collective-permute-start(bf16[432,1536]{1,0:T(8,128)(2,1)} %get-tuple-element.34), channel_id=1, source_target_pairs={{0,1},{1,0},{2,3},{3,2},{4,5},{5,4},{6,7},{7,6},{8,9},{9,8},{10,11... | collective-permute-start | bytes 3981320 | tf_op jit(solution)/shard_map/ppermute | solution.py:55
  129.2 1.7 convolution_convert_fusion
  131.0 6.9 %all-to-all-start.4 = ((bf16[16,32,1536]{2,1,0:T(8,128)(2,1)}), bf16[16,32,1536]{2,1,0:T(8,128)(2,1)}, u32[]{:S(2)}, u32[]{:S(2)}) async-start(bf16[16,32,1536]{2,1,0:T(8,128)(2,1)} %bitcast.199), calls=%async_computation.4 | async-start | bytes 3145728 | tf_op jit(solution)/shard_map/all_to_all | solution.py:196
  137.9 2.8 collective-permute-start.3
  140.8 1.0 slice.66
  142.2 14.9 %collective-permute-done.3 = bf16[512,768]{1,0:T(8,128)(2,1)S(1)} collective-permute-done((bf16[512,768]{1,0:T(8,128)(2,1)S(1)}, bf16[512,768]{1,0:T(8,128)(2,1)S(1)}, u32[]{:S(2)}, u32[]{:S(2)}) %collective-permute-start.3) | collective-permute-done | bytes 786464 | tf_op jit(solution)/shard_map/ppermute | solution.py:84
  157.5 1.2 all-to-all-done.4
  158.7 2.3 fusion.19
  161.1 5.9 %collective-permute-start.4 = (f32[432,512]{1,0:T(8,128)S(1)}, f32[432,512]{1,0:T(8,128)S(1)}, u32[]{:S(2)}, u32[]{:S(2)}) collective-permute-start(f32[432,512]{1,0:T(8,128)S(1)} %pad_maximum_fusion.1), channel_id=1, source_target_pairs={{0,1},{1,0},{2,3},{3,2},{4,5},{5,4},{6,7},{7,6},{8,9},{9,8},{10,11... | collective-permute-start | bytes 2654216 | tf_op jit(solution)/shard_map/ppermute | solution.py:55
  167.9 2.1 fusion.22
  170.3 1.9 collective-permute-start.5
  172.3 1.5 collective-permute-done.5
  173.8 2.2 fusion.17
  176.0 1.0 fusion
  177.0 26.3 %all_to_all.45 = bf16[16,32,1536]{2,1,0:T(8,128)(2,1)S(1)} all-to-all(bf16[16,32,1536]{2,1,0:T(8,128)(2,1)S(1)} %bitcast.200), channel_id=1, replica_groups=mesh['seq'=16,'mp'=32] {'seq'}, dimensions={0} | all-to-all | bytes 3145728 | tf_op jit(solution)/shard_map/all_to_all | solution.py:223
  203.8 24.9 %all_to_all.46 = bf16[16,8,1536]{2,1,0:T(8,128)(2,1)S(1)} all-to-all(bf16[16,8,1536]{2,1,0:T(8,128)(2,1)S(1)} %fusion.2), channel_id=1, replica_groups={{0,2,4,6,8,10,12,14,16,18,20,22,24,26,28,30},{1,3,5,7,9,11,13,15,17,19,..., dimensions={0} | all-to-all | bytes 786432 | tf_op jit(solution)/shard_map/all_to_all | solution.py:88
  229.0 10.1 %psum.15 = f32[8,1]{0,1:T(1,128)S(1)} all-reduce(f32[8,1]{0,1:T(1,128)S(1)} %bitcast.233), channel_id=1, replica_groups={{0,1},{2,3},{4,5},{6,7},{8,9},{10,11},{12,13},{14,15},{16,17},{18,19},{..., use_global_device_ids=true, to_apply=%region_8.9 | all-reduce | flops 8 | bytes 64 | tf_op jit(solution)/shard_map/psum | solution.py:181
  239.2 0.8 broadcast_in_dim.148
  240.0 6.1 %all-to-all-start.7 = ((bf16[16,8,1536]{2,1,0:T(8,128)(2,1)}), bf16[16,8,1536]{2,1,0:T(8,128)(2,1)S(1)}, u32[]{:S(2)}, u32[]{:S(2)}) async-start(bf16[16,8,1536]{2,1,0:T(8,128)(2,1)} %broadcast_in_dim.148), calls=%async_computation.7 | async-start | bytes 786432 | tf_op jit(solution)/shard_map/all_to_all | solution.py:72
  246.3 17.0 %all-to-all-done.7 = bf16[16,8,1536]{2,1,0:T(8,128)(2,1)S(1)} async-done(((bf16[16,8,1536]{2,1,0:T(8,128)(2,1)}), bf16[16,8,1536]{2,1,0:T(8,128)(2,1)S(1)}, u32[]{:S(2)}, u32[]{:S(2)}) %all-to-all-start.7) | async-done | bytes 393248 | tf_op jit(solution)/shard_map/all_to_all | solution.py:72
  263.3 9.7 %collective-permute-start.6 = (bf16[128,1536]{1,0:T(8,128)(2,1)S(1)}, bf16[128,1536]{1,0:T(8,128)(2,1)S(1)}, u32[]{:S(2)}, u32[]{:S(2)}) collective-permute-start(bf16[128,1536]{1,0:T(8,128)(2,1)S(1)} %bitcast.205), channel_id=1, source_target_pairs={{0,1},{1,0},{2,3},{3,2},{4,5},{5,4},{6,7},{7,6},{8,9},{9,8},{10,11... | collective-permute-start | bytes 1179656 | tf_op jit(solution)/shard_map/ppermute | solution.py:55
  275.3 1.2 broadcast_in_dim.151
  276.5 3.7 %all-to-all-start.8 = ((bf16[16,256,128]{2,1,0:T(8,128)(2,1)}), bf16[16,256,128]{2,1,0:T(8,128)(2,1)S(1)}, u32[]{:S(2)}, u32[]{:S(2)}) async-start(bf16[16,256,128]{2,1,0:T(8,128)(2,1)} %broadcast_in_dim.151), calls=%async_computation.8 | async-start | bytes 2097152 | tf_op jit(solution)/shard_map/all_to_all | solution.py:124
  280.2 0.9 fusion.5
  282.0 1.4 maximum_select_fusion.2
  283.4 13.8 %all-to-all-done.8 = bf16[16,256,128]{2,1,0:T(8,128)(2,1)S(1)} async-done(((bf16[16,256,128]{2,1,0:T(8,128)(2,1)}), bf16[16,256,128]{2,1,0:T(8,128)(2,1)S(1)}, u32[]{:S(2)}, u32[]{:S(2)}) %all-to-all-start.8) | async-done | bytes 1048608 | tf_op jit(solution)/shard_map/all_to_all | solution.py:124
  297.9 0.9 fusion.6
  298.8 0.8 fusion.7
  (155 shorter events, 15.5 us)
Async XLA Ops:
  0.6 28.5 %copy-start = (bf16[256,3072]{1,0:T(8,128)(2,1)S(1)}, bf16[256,3072]{1,0:T(8,128)(2,1)}, u32[]{:S(2)}) copy-start(bf16[256,3072]{1,0:T(8,128)(2,1)} %param.17) | copy-start | bytes 4718596
  1.4 18.3 %copy-start.31 = (f32[2]{0:T(128)}, f32[2]{0:T(128)S(1)}, u32[]{:S(2)}) copy-start(f32[2]{0:T(128)S(1)} %get-tuple-element.54) | copy-start | bytes 28
  4.1 14.6 %copy-start.24 = (bf16[128,256]{1,0:T(8,128)(2,1)S(1)}, bf16[128,256]{1,0:T(8,128)(2,1)}, u32[]{:S(2)}) copy-start(bf16[128,256]{1,0:T(8,128)(2,1)} %param.13) | copy-start | bytes 196612
  4.1 16.3 %copy-start.10 = (bf16[128,256]{1,0:T(8,128)(2,1)S(1)}, bf16[128,256]{1,0:T(8,128)(2,1)}, u32[]{:S(2)}) copy-start(bf16[128,256]{1,0:T(8,128)(2,1)} %param.14) | copy-start | bytes 196612
  5.3 22.1 %all-to-all-start = ((bf16[16,256,128]{2,1,0:T(8,128)(2,1)}), bf16[16,256,128]{2,1,0:T(8,128)(2,1)S(1)}, u32[]{:S(2)}, u32[]{:S(2)}) async-start(bf16[16,256,128]{2,1,0:T(8,128)(2,1)} %broadcast_in_dim.136), calls=%async_computation | async-start | bytes 2097152 | tf_op jit(solution)/shard_map/all_to_all | solution.py:124
  12.9 16.0 %copy-start.4 = (bf16[128,256]{1,0:T(8,128)(2,1)S(1)}, bf16[128,256]{1,0:T(8,128)(2,1)}, u32[]{:S(2)}) copy-start(bf16[128,256]{1,0:T(8,128)(2,1)} %param.15) | copy-start | bytes 196612
  12.9 22.5 %collective-permute-start = (bf16[8,1536]{1,0:T(8,128)(2,1)S(1)}, bf16[8,1536]{1,0:T(8,128)(2,1)S(1)}, u32[]{:S(2)}, u32[]{:S(2)}) collective-permute-start(bf16[8,1536]{1,0:T(8,128)(2,1)S(1)} %constant_dynamic-slice_fusion.5), channel_id=1, source_target_pairs={{0,1},{1,0},{2,3},{3,2},{4,5},{5,4},{6,7},{7,6},{8,9},{9,8},{10,11... | collective-permute-start | bytes 73736 | tf_op jit(solution)/shard_map/ppermute | solution.py:55
  17.9 69.2 %copy-start.6 = (bf16[4,1536]{1,0:T(4,128)(2,1)}, bf16[4,1536]{1,0:T(4,128)(2,1)S(1)}, u32[]{:S(2)}) copy-start(bf16[4,1536]{1,0:T(4,128)(2,1)S(1)} %get-tuple-element.38) | copy-start | bytes 36868
  19.5 10.0 %copy-start.30 = (f32[128,2]{0,1:T(2,128)}, f32[128,2]{0,1:T(2,128)S(1)}, u32[]{:S(2)}) copy-start(f32[128,2]{0,1:T(2,128)S(1)} %get-tuple-element.49) | copy-start | bytes 3076
  20.6 15.0 %copy-start.12 = (bf16[2,128,128]{2,1,0:T(8,128)(2,1)}, bf16[2,128,128]{2,1,0:T(8,128)(2,1)S(1)}, u32[]{:S(2)}) copy-start(bf16[2,128,128]{2,1,0:T(8,128)(2,1)S(1)} %fusion.11) | copy-start | bytes 196612
  29.5 7.3 %collective-permute-start.1 = (bf16[128,1536]{1,0:T(8,128)(2,1)S(1)}, bf16[128,1536]{1,0:T(8,128)(2,1)S(1)}, u32[]{:S(2)}, u32[]{:S(2)}) collective-permute-start(bf16[128,1536]{1,0:T(8,128)(2,1)S(1)} %convolution_convert_fusion.1), channel_id=1, source_target_pairs={{0,1},{1,0},{2,3},{3,2},{4,5},{5,4},{6,7},{7,6},{8,9},{9,8},{10,11... | collective-permute-start | bytes 1179656 | tf_op jit(solution)/shard_map/ppermute | solution.py:55
  35.5 2.5 copy-start.22
  35.5 51.6 %copy-start.8 = (bf16[4,1536]{1,0:T(4,128)(2,1)}, bf16[4,1536]{1,0:T(4,128)(2,1)S(1)}, u32[]{:S(2)}) copy-start(bf16[4,1536]{1,0:T(4,128)(2,1)S(1)} %get-tuple-element.40) | copy-start | bytes 36868
  37.1 16.0 %copy-start.33 = (f32[3072]{0:T(1024)S(1)}, f32[3072]{0:T(1024)}, u32[]{:S(2)}) copy-start(f32[3072]{0:T(1024)} %param.20) | copy-start | bytes 36868
  37.1 16.1 %copy-start.37 = (s32[128,2]{0,1:T(2,128)S(1)}, s32[128,2]{0,1:T(2,128)}, u32[]{:S(2)}) copy-start(s32[128,2]{0,1:T(2,128)} %param.21) | copy-start | bytes 3076
  38.0 57.3 %copy-start.38 = (f32[128,2]{0,1:T(2,128)S(1)}, f32[128,2]{0,1:T(2,128)}, u32[]{:S(2)}) copy-start(f32[128,2]{0,1:T(2,128)} %param.22) | copy-start | bytes 3076
  38.0 40.4 %all-to-all-start.1 = ((bf16[16,8,2304]{2,1,0:T(8,128)(2,1)}), bf16[16,8,2304]{2,1,0:T(8,128)(2,1)S(1)}, u32[]{:S(2)}, u32[]{:S(2)}) async-start(bf16[16,8,2304]{2,1,0:T(8,128)(2,1)} %pad_maximum_fusion.2), calls=%async_computation.1 | async-start | bytes 1179648 | tf_op jit(solution)/shard_map/all_to_all | solution.py:175
  53.2 43.7 %copy-start.18 = (f32[1536]{0:T(1024)}, f32[1536]{0:T(1024)S(1)}, u32[]{:S(2)}) copy-start(f32[1536]{0:T(1024)S(1)} %dynamic_slice.45) | copy-start | bytes 18436
  87.1 8.1 %copy-start.34 = (f32[8]{0:T(128)}, f32[8]{0:T(128)S(1)}, u32[]{:S(2)}) copy-start(f32[8]{0:T(128)S(1)} %rsqrt_bitcast_fusion) | copy-start | bytes 100
  88.0 24.4 %all-to-all-start.3 = ((bf16[16,8,1536]{2,1,0:T(8,128)(2,1)}), bf16[16,8,1536]{2,1,0:T(8,128)(2,1)S(1)}, u32[]{:S(2)}, u32[]{:S(2)}) async-start(bf16[16,8,1536]{2,1,0:T(8,128)(2,1)} %broadcast_in_dim.146), calls=%async_computation.3 | async-start | bytes 786432 | tf_op jit(solution)/shard_map/all_to_all | solution.py:72
  95.3 17.1 %copy-start.16 = (s32[16,128]{1,0:T(8,128)}, s32[16,128]{1,0:T(8,128)S(1)}, u32[]{:S(2)}) copy-start(s32[16,128]{1,0:T(8,128)S(1)} %copy.64) | copy-start | bytes 24580
  95.3 17.1 %copy-start.27 = (pred[16,128]{1,0:T(8,128)(4,1)}, pred[16,128]{1,0:T(8,128)(4,1)S(1)}, u32[]{:S(2)}) copy-start(pred[16,128]{1,0:T(8,128)(4,1)S(1)} %convert_compare_fusion) | copy-start | bytes 6148
  112.4 18.6 %all-to-all-start.2 = ((bf16[16,32,768]{2,1,0:T(8,128)(2,1)}), bf16[16,32,768]{2,1,0:T(8,128)(2,1)S(1)}, u32[]{:S(2)}, u32[]{:S(2)}) async-start(bf16[16,32,768]{2,1,0:T(8,128)(2,1)} %bitcast.29), calls=%async_computation.2 | async-start | bytes 1572864 | tf_op jit(solution)/shard_map/all_to_all | solution.py:191
  119.6 21.2 %collective-permute-start.2 = (bf16[432,1536]{1,0:T(8,128)(2,1)}, bf16[432,1536]{1,0:T(8,128)(2,1)}, u32[]{:S(2)}, u32[]{:S(2)}) collective-permute-start(bf16[432,1536]{1,0:T(8,128)(2,1)} %get-tuple-element.34), channel_id=1, source_target_pairs={{0,1},{1,0},{2,3},{3,2},{4,5},{5,4},{6,7},{7,6},{8,9},{9,8},{10,11... | collective-permute-start | bytes 3981320 | tf_op jit(solution)/shard_map/ppermute | solution.py:55
  131.0 27.8 %all-to-all-start.4 = ((bf16[16,32,1536]{2,1,0:T(8,128)(2,1)}), bf16[16,32,1536]{2,1,0:T(8,128)(2,1)}, u32[]{:S(2)}, u32[]{:S(2)}) async-start(bf16[16,32,1536]{2,1,0:T(8,128)(2,1)} %bitcast.199), calls=%async_computation.4 | async-start | bytes 3145728 | tf_op jit(solution)/shard_map/all_to_all | solution.py:196
  137.9 19.2 %collective-permute-start.3 = (bf16[512,768]{1,0:T(8,128)(2,1)S(1)}, bf16[512,768]{1,0:T(8,128)(2,1)S(1)}, u32[]{:S(2)}, u32[]{:S(2)}) collective-permute-start(bf16[512,768]{1,0:T(8,128)(2,1)S(1)} %bitcast.196), channel_id=1, source_target_pairs={{0,2},{1,3},{2,0},{3,1},{4,6},{5,7},{6,4},{7,5},{8,10},{9,11},{10,... | collective-permute-start | bytes 2359304 | tf_op jit(solution)/shard_map/ppermute | solution.py:84
  161.1 6.0 %copy-start.1 = (bf16[432,1536]{1,0:T(8,128)(2,1)S(1)}, bf16[432,1536]{1,0:T(8,128)(2,1)}, u32[]{:S(2)}) copy-start(bf16[432,1536]{1,0:T(8,128)(2,1)} %get-tuple-element.18) | copy-start | bytes 3981316
  161.1 8.8 %collective-permute-start.4 = (f32[432,512]{1,0:T(8,128)S(1)}, f32[432,512]{1,0:T(8,128)S(1)}, u32[]{:S(2)}, u32[]{:S(2)}) collective-permute-start(f32[432,512]{1,0:T(8,128)S(1)} %pad_maximum_fusion.1), channel_id=1, source_target_pairs={{0,1},{1,0},{2,3},{3,2},{4,5},{5,4},{6,7},{7,6},{8,9},{9,8},{10,11... | collective-permute-start | bytes 2654216 | tf_op jit(solution)/shard_map/ppermute | solution.py:55
  170.3 3.5 %collective-permute-start.5 = (bf16[288,512]{1,0:T(8,128)(2,1)S(1)}, bf16[288,512]{1,0:T(8,128)(2,1)S(1)}, u32[]{:S(2)}, u32[]{:S(2)}) collective-permute-start(bf16[288,512]{1,0:T(8,128)(2,1)S(1)} %pad_maximum_fusion.3), channel_id=1, source_target_pairs={{0,1},{1,0},{2,3},{3,2},{4,5},{5,4},{6,7},{7,6},{8,9},{9,8},{10,11... | collective-permute-start | bytes 884744 | tf_op jit(solution)/shard_map/ppermute | solution.py:55
  177.0 26.3 %copy-start.17 = (s32[16,128]{1,0:T(8,128)S(1)}, s32[16,128]{1,0:T(8,128)}, u32[]{:S(2)}) copy-start(s32[16,128]{1,0:T(8,128)} %copy-done.16) | copy-start | bytes 24580
  177.0 26.3 %copy-start.28 = (pred[16,128]{1,0:T(8,128)(4,1)S(1)}, pred[16,128]{1,0:T(8,128)(4,1)}, u32[]{:S(2)}) copy-start(pred[16,128]{1,0:T(8,128)(4,1)} %copy-done.27) | copy-start | bytes 6148
  203.3 25.5 %copy-start.7 = (bf16[4,1536]{1,0:T(4,128)(2,1)S(1)}, bf16[4,1536]{1,0:T(4,128)(2,1)}, u32[]{:S(2)}) copy-start(bf16[4,1536]{1,0:T(4,128)(2,1)} %copy-done.6) | copy-start | bytes 36868
  203.3 25.5 %copy-start.9 = (bf16[4,1536]{1,0:T(4,128)(2,1)S(1)}, bf16[4,1536]{1,0:T(4,128)(2,1)}, u32[]{:S(2)}) copy-start(bf16[4,1536]{1,0:T(4,128)(2,1)} %copy-done.8) | copy-start | bytes 36868
  203.3 25.5 %copy-start.19 = (f32[1536]{0:T(1024)S(1)}, f32[1536]{0:T(1024)}, u32[]{:S(2)}) copy-start(f32[1536]{0:T(1024)} %copy-done.18) | copy-start | bytes 18436
  203.3 25.5 %copy-start.35 = (f32[8]{0:T(128)S(1)}, f32[8]{0:T(128)}, u32[]{:S(2)}) copy-start(f32[8]{0:T(128)} %copy-done.34) | copy-start | bytes 100
  203.3 35.8 %copy-start.21 = (bf16[4,1536]{1,0:T(4,128)(2,1)S(1)}, bf16[4,1536]{1,0:T(4,128)(2,1)}, u32[]{:S(2)}) copy-start(bf16[4,1536]{1,0:T(4,128)(2,1)} %copy-done.20) | copy-start | bytes 36868
  203.3 35.8 %copy-start.23 = (bf16[4,1536]{1,0:T(4,128)(2,1)S(1)}, bf16[4,1536]{1,0:T(4,128)(2,1)}, u32[]{:S(2)}) copy-start(bf16[4,1536]{1,0:T(4,128)(2,1)} %copy-done.22) | copy-start | bytes 36868
  203.8 42.4 %copy-start.29 = (f32[16,2]{1,0:T(8,128)S(1)}, f32[16,2]{1,0:T(8,128)}, u32[]{:S(2)}) copy-start(f32[16,2]{1,0:T(8,128)} %get-tuple-element.50) | copy-start | bytes 388
  240.0 23.3 %all-to-all-start.7 = ((bf16[16,8,1536]{2,1,0:T(8,128)(2,1)}), bf16[16,8,1536]{2,1,0:T(8,128)(2,1)S(1)}, u32[]{:S(2)}, u32[]{:S(2)}) async-start(bf16[16,8,1536]{2,1,0:T(8,128)(2,1)} %broadcast_in_dim.148), calls=%async_computation.7 | async-start | bytes 786432 | tf_op jit(solution)/shard_map/all_to_all | solution.py:72
  246.2 28.7 %copy-start.5 = (bf16[128,256]{1,0:T(8,128)(2,1)S(1)}, bf16[128,256]{1,0:T(8,128)(2,1)}, u32[]{:S(2)}) copy-start(bf16[128,256]{1,0:T(8,128)(2,1)} %param.15) | copy-start | bytes 196612
  246.2 28.7 %copy-start.15 = (f32[128,128]{1,0:T(8,128)S(1)}, f32[128,128]{1,0:T(8,128)}, u32[]{:S(2)}) copy-start(f32[128,128]{1,0:T(8,128)} %copy-done.14) | copy-start | bytes 196612
  246.2 28.7 %copy-start.26 = (pred[128,128]{1,0:T(8,128)(4,1)S(1)}, pred[128,128]{1,0:T(8,128)(4,1)}, u32[]{:S(2)}) copy-start(pred[128,128]{1,0:T(8,128)(4,1)} %copy-done.25) | copy-start | bytes 49156
  246.2 28.7 %copy-start.32 = (f32[2]{0:T(128)S(1)}, f32[2]{0:T(128)}, u32[]{:S(2)}) copy-start(f32[2]{0:T(128)} %copy-done.31) | copy-start | bytes 28
  263.3 11.0 %collective-permute-start.6 = (bf16[128,1536]{1,0:T(8,128)(2,1)S(1)}, bf16[128,1536]{1,0:T(8,128)(2,1)S(1)}, u32[]{:S(2)}, u32[]{:S(2)}) collective-permute-start(bf16[128,1536]{1,0:T(8,128)(2,1)S(1)} %bitcast.205), channel_id=1, source_target_pairs={{0,1},{1,0},{2,3},{3,2},{4,5},{5,4},{6,7},{7,6},{8,9},{9,8},{10,11... | collective-permute-start | bytes 1179656 | tf_op jit(solution)/shard_map/ppermute | solution.py:55
  275.3 4.9 %copy-start.3 = (bf16[256,128]{1,0:T(8,128)(2,1)S(1)}, bf16[256,128]{1,0:T(8,128)(2,1)}, u32[]{:S(2)}) copy-start(bf16[256,128]{1,0:T(8,128)(2,1)} %copy-done.2) | copy-start | bytes 196612
  275.3 5.7 %copy-start.11 = (bf16[128,256]{1,0:T(8,128)(2,1)S(1)}, bf16[128,256]{1,0:T(8,128)(2,1)}, u32[]{:S(2)}) copy-start(bf16[128,256]{1,0:T(8,128)(2,1)} %param.14) | copy-start | bytes 196612
  276.5 20.7 %all-to-all-start.8 = ((bf16[16,256,128]{2,1,0:T(8,128)(2,1)}), bf16[16,256,128]{2,1,0:T(8,128)(2,1)S(1)}, u32[]{:S(2)}, u32[]{:S(2)}) async-start(bf16[16,256,128]{2,1,0:T(8,128)(2,1)} %broadcast_in_dim.151), calls=%async_computation.8 | async-start | bytes 2097152 | tf_op jit(solution)/shard_map/all_to_all | solution.py:124
  280.2 19.5 %copy-start.13 = (bf16[2,128,128]{2,1,0:T(8,128)(2,1)S(1)}, bf16[2,128,128]{2,1,0:T(8,128)(2,1)}, u32[]{:S(2)}) copy-start(bf16[2,128,128]{2,1,0:T(8,128)(2,1)} %copy-done.12) | copy-start | bytes 196612
  (5 other events, 5.1 us)

commit v4 on v3

--- a/solution.py
+++ b/solution.py
@@ -1,6 +1,8 @@
 import jax
 import jax.numpy as jnp
 from jax import lax
+from jax.experimental import pallas as pl
+from jax.experimental.pallas import tpu as pltpu
 from jax.sharding import PartitionSpec as P
 
 EPSILON = 1e-06
@@ -18,6 +20,86 @@
 
 def heads_dot(spec, a, b):
     return jnp.einsum(spec, a, b, preferred_element_type=F32)
+
+
+LIMITS = pltpu.CompilerParams(vmem_limit_bytes=8 * 2**20)
+VMEM = pl.BlockSpec(memory_space=pltpu.VMEM)
+SMEM = pl.BlockSpec(memory_space=pltpu.SMEM)
+
+
+def rows_of(length, lanes):
+    return lax.broadcasted_iota(jnp.int32, (length, lanes), 0).astype(F32)
+
+
+def state_kernel(head_size, first_power, step, rate_ref, left_ref, right_ref, out_ref):
+    length = left_ref.shape[0]
+    for head in range(rate_ref.shape[0]):
+        columns = pl.ds(head * head_size, head_size)
+        powers = first_power + step * rows_of(length, head_size)
+        left = jnp.exp(-rate_ref[head] * powers) * left_ref[:, columns].astype(F32)
+        state = lax.dot_general(
+            left.astype(BF16),
+            right_ref[:, columns].astype(BF16),
+            (((0,), (0,)), ((), ())),
+            preferred_element_type=F32,
+        ).astype(BF16)
+        for copy in range(out_ref.shape[0]):
+            out_ref[copy, columns, :] = state
+
+
+def state_copies(rates, left, right, copies, first_power, step):
+    length, width = left.shape
+    head_size = width // rates.shape[0]
+    return pl.pallas_call(
+        lambda *refs: state_kernel(head_size, first_power, step, *refs),
+        out_shape=jax.ShapeDtypeStruct((copies, width, head_size), BF16),
+        in_specs=[SMEM, VMEM, VMEM],
+        out_specs=VMEM,
+        cost_estimate=pl.CostEstimate(
+            flops=2 * length * width * head_size,
+            bytes_accessed=2 * (copies * width * head_size + 2 * length * width),
+            transcendentals=length * width,
+        ),
+    )(rates, left, right)
+
+
+def last_kernel(
+    rate_ref, place_ref, states_ref, key_ref, value_ref, key_in_ref, value_in_ref, key_ref_out, value_ref_out
+):
+    length, width = key_ref.shape
+    peers, _, head_size = states_ref.shape
+    for head in range(rate_ref.shape[0]):
+        rate = rate_ref[head]
+        columns = pl.ds(head * head_size, head_size)
+        leaving = jnp.zeros((head_size, head_size), F32)
+        for peer in range(peers):
+            ahead = peer - 1 - place_ref[0]
+            power = jnp.full((1, head_size), rate * length * jnp.maximum(ahead, 0).astype(F32))
+            share = jnp.where(ahead >= 0, jnp.exp(-power), 0.0)
+            leaving = leaving + share * states_ref[peer, columns, :].astype(F32)
+        leaving = leaving.astype(BF16)
+        tail = jnp.exp(-rate * (length - 1.0 - rows_of(length, head_size)))
+        key_part = key_in_ref[:, columns] + tail * mm_t(value_ref[:, columns], leaving)
+        value_part = value_in_ref[:, columns] + tail * mm(key_ref[:, columns], leaving)
+        key_ref_out[:, columns] = key_part.astype(BF16)
+        value_ref_out[:, columns] = value_part.astype(BF16)
+
+
+def last_grads(rates, place, states, key_rows, value_rows, key_inside, value_inside):
+    length, width = key_rows.shape
+    out = jax.ShapeDtypeStruct((length, width), BF16)
+    return pl.pallas_call(
+        last_kernel,
+        out_shape=(out, out),
+        in_specs=[SMEM, SMEM, VMEM, VMEM, VMEM, VMEM, VMEM],
+        out_specs=(VMEM, VMEM),
+        compiler_params=LIMITS,
+        cost_estimate=pl.CostEstimate(
+            flops=4 * length * width * states.shape[2],
+            bytes_accessed=2 * states.size + 16 * length * width,
+            transcendentals=length * width,
+        ),
+    )(rates, place.reshape(1), states, key_rows, value_rows, key_inside, value_inside)
 
 
 def body(
@@ -115,12 +197,8 @@
     clipped = jnp.where(causal, offset, 0.0)
     decay_band = jnp.where(causal[None], jnp.exp(-decay_rates[:, None, None] * clipped[None]), 0.0)
     head_decay = jnp.exp(-decay_rates[:, None] * places[None, :])[:, :, None]
-    tail_decay = jnp.exp(-decay_rates[:, None] * (length - 1.0 - places)[None, :])[:, :, None]
-    step_decay = jnp.exp(-decay_rates)[:, None, None]
-
-    def exchange_states(states):
-        sent = states.astype(BF16).reshape(head_count * head_size, head_size)
-        sent = jnp.broadcast_to(sent[None], (seq_count,) + sent.shape)
+
+    def exchange_states(sent):
         return lax.all_to_all(sent, "seq", 0, 0, tiled=True)
 
     def combine_states(states, ahead):
@@ -130,12 +208,9 @@
         return jnp.sum(share.T[:, :, None, None] * states, axis=0)
 
     peers = jnp.arange(seq_count, dtype=jnp.int32)
-    local_state = heads_dot(
-        "htd,hte->hde",
-        (step_decay * tail_decay * key_heads.astype(F32)).astype(BF16),
-        value_heads,
-    )
-    local_state = local_state.astype(BF16)
+    local_state = state_copies(
+        decay_rates, key_rows, value_rows, seq_count, float(length), -1.0
+    )
 
     both = jnp.concatenate([inputs, cotangent], axis=0)
     hidden_units = w_down.shape[1]
@@ -237,20 +312,27 @@
     local_adjoint = heads_dot(
         "htd,hte->hde",
         query_heads,
-        (step_decay * head_decay * grad_heads).astype(BF16),
-    )
-    leaving = combine_states(exchange_states(local_adjoint), peers - 1 - seq_place)
-    leaving_b = leaving.astype(BF16)
+        (jnp.exp(-decay_rates[:, None] * (places + 1.0)[None, :])[:, :, None] * grad_heads).astype(BF16),
+    ).astype(BF16)
+    local_adjoint = local_adjoint.reshape(head_count * head_size, head_size)
+    local_adjoint = jnp.broadcast_to(local_adjoint[None], (seq_count,) + local_adjoint.shape)
+    adjoints = exchange_states(local_adjoint)
     grad_scores = (heads_dot("hte,hse->hts", grad_b, value_heads) * decay_band).astype(BF16)
     query_part = heads_dot("hts,hsd->htd", grad_scores, key_heads)
     query_part = query_part + head_decay * heads_dot("hte,hde->htd", grad_b, entering_b)
     key_part = heads_dot("hts,htd->hsd", grad_scores, query_heads)
-    key_part = key_part + tail_decay * heads_dot("hse,hde->hsd", value_heads, leaving_b)
     value_part = heads_dot("hts,hte->hse", scores_b, grad_b)
-    value_part = value_part + tail_decay * heads_dot("hsd,hde->hse", key_heads, leaving_b)
     query_grad = from_heads(query_part).astype(BF16)
-    key_grad = from_heads(key_part).astype(BF16)
-    value_grad = from_heads(value_part).astype(BF16)
+    key_grad, value_grad = last_grads(
+        decay_rates,
+        seq_place,
+        adjoints,
+        key_rows,
+        value_rows,
+        from_heads(key_part),
+        from_heads(value_part),
+    )
+
     def own_tokens(x):
         return lax.dynamic_slice_in_dim(x, lax.axis_index("mp") * tok_share, tok_share, 0)
 

time: 303 us -> 299 us (0.987)
  other arithmetic: 10.9 us -> 6.94 us
  Pallas kernels: 0 us -> 3.79 us
    pallas_call x0 -> x2, Pallas kernels: none -> 3.79 us  [the longest x1 2.2 us: state_copies(): pl.pallas_call(lambda *refs: state_kernel(head_size, first_power, step, *...]
where the time goes in v4:
time: 299 us; the launch traced here: 298 us
  waiting for transfers between devices  97 us (32%)
  starting transfers between devices  91.1 us (30%)
  blocking collectives  70.6 us (24%)
  matrix products  17 us (6%)
  local copies, waits for them, and re-layouts  9.56 us (3%)
  other arithmetic  6.94 us (2%)
  Pallas kernels  3.79 us (1%)
    ppermute x6, starting transfers between devices, swap(): return lax.ppermute(x, 'mp', swap_pairs)  38 us
    all_to_all x2, waiting for transfers between devices, spread_z(): lax.all_to_all(copies, 'mp', 0, 0, axis_index_groups=z_groups, tiled=True)  32.6 us
    all_to_all x1, blocking collectives, body(): returned = lax.all_to_all(slots, 'seq', 0, 0, tiled=True).reshape(-1, half)  27 us
    all_to_all x1, blocking collectives, sum_z(): lax.all_to_all(parts, 'mp', 0, 0, axis_index_groups=z_groups, tiled=True)  25 us
    all_to_all x1, waiting for transfers between devices, body(): lax.all_to_all(sent, 'mp', 0, 0, axis_index_groups=z_groups, tiled=True)  24.9 us
    all_to_all x2, waiting for transfers between devices, exchange_states(): return lax.all_to_all(sent, 'seq', 0, 0, tiled=True)  20.6 us
    psum x2, blocking collectives, over_features(): return lax.psum(total, 'mp', axis_index_groups=core_groups) / width  18.7 us
    all_to_all x1, starting transfers between devices, body(): lax.all_to_all(sent, 'mp', 0, 0, axis_index_groups=z_groups, tiled=True)  15.1 us
  transfers between devices with their start and end apart: 14, of which 10 were waited for; matrix products, arithmetic and copies ran while one was open for 7% of the time, Pallas kernels for 0%

profile of v4, /device:TPU:1, one launch (start us, length us, event | category | flops | bytes accessed | tf_op | source)
XLA Modules:
  0.0 297.6 jit_solution(11560051886685969697)
XLA Ops:
  0.6 0.9 pad_maximum_fusion.4
  1.6 2.2 shard_map.156
  3.8 7.6 %all-to-all-start = ((bf16[16,256,128]{2,1,0:T(8,128)(2,1)}), bf16[16,256,128]{2,1,0:T(8,128)(2,1)S(1)}, u32[]{:S(2)}, u32[]{:S(2)}) async-start(bf16[16,256,128]{2,1,0:T(8,128)(2,1)} %shard_map.156), calls=%async_computation | async-start | bytes 2097152 | tf_op jit(solution)/shard_map/all_to_all | solution.py:202
  11.4 4.9 %collective-permute-start = (bf16[8,1536]{1,0:T(8,128)(2,1)S(1)}, bf16[8,1536]{1,0:T(8,128)(2,1)S(1)}, u32[]{:S(2)}, u32[]{:S(2)}) collective-permute-start(bf16[8,1536]{1,0:T(8,128)(2,1)S(1)} %constant_dynamic-slice_fusion.5), channel_id=1, source_target_pairs={{0,1},{1,0},{2,3},{3,2},{4,5},{5,4},{6,7},{7,6},{8,9},{9,8},{10,11... | collective-permute-start | bytes 73736 | tf_op jit(solution)/shard_map/ppermute | solution.py:137
  17.9 7.9 %all-to-all-done = bf16[16,256,128]{2,1,0:T(8,128)(2,1)S(1)} async-done(((bf16[16,256,128]{2,1,0:T(8,128)(2,1)}), bf16[16,256,128]{2,1,0:T(8,128)(2,1)S(1)}, u32[]{:S(2)}, u32[]{:S(2)}) %all-to-all-start) | async-done | bytes 1048608 | tf_op jit(solution)/shard_map/all_to_all | solution.py:202
  27.4 6.0 %collective-permute-start.1 = (bf16[128,1536]{1,0:T(8,128)(2,1)S(1)}, bf16[128,1536]{1,0:T(8,128)(2,1)S(1)}, u32[]{:S(2)}, u32[]{:S(2)}) collective-permute-start(bf16[128,1536]{1,0:T(8,128)(2,1)S(1)} %convolution_convert_fusion.1), channel_id=1, source_target_pairs={{0,1},{1,0},{2,3},{3,2},{4,5},{5,4},{6,7},{7,6},{8,9},{9,8},{10,11... | collective-permute-start | bytes 1179656 | tf_op jit(solution)/shard_map/ppermute | solution.py:137
  33.5 1.2 collective-permute-done.1
  35.0 0.9 pad_maximum_fusion.2
  35.9 15.1 %all-to-all-start.1 = ((bf16[16,8,2304]{2,1,0:T(8,128)(2,1)}), bf16[16,8,2304]{2,1,0:T(8,128)(2,1)S(1)}, u32[]{:S(2)}, u32[]{:S(2)}) async-start(bf16[16,8,2304]{2,1,0:T(8,128)(2,1)} %pad_maximum_fusion.2), calls=%async_computation.1 | async-start | bytes 1179648 | tf_op jit(solution)/shard_map/all_to_all | solution.py:250
  51.4 24.9 %all-to-all-done.1 = bf16[16,8,2304]{2,1,0:T(8,128)(2,1)S(1)} async-done(((bf16[16,8,2304]{2,1,0:T(8,128)(2,1)}), bf16[16,8,2304]{2,1,0:T(8,128)(2,1)S(1)}, u32[]{:S(2)}, u32[]{:S(2)}) %all-to-all-start.1) | async-done | bytes 589856 | tf_op jit(solution)/shard_map/all_to_all | solution.py:250
  76.5 8.5 %psum.14 = f32[8,1]{0,1:T(1,128)S(1)} all-reduce(f32[8,1]{0,1:T(1,128)S(1)} %bitcast.170), channel_id=1, replica_groups={{0,1},{2,3},{4,5},{6,7},{8,9},{10,11},{12,13},{14,15},{16,17},{18,19},{..., use_global_device_ids=true, to_apply=%region_3.4 | all-reduce | flops 8 | bytes 64 | tf_op jit(solution)/shard_map/psum | solution.py:256
  85.1 0.8 broadcast_in_dim.126
  85.9 7.2 %all-to-all-start.3 = ((bf16[16,8,1536]{2,1,0:T(8,128)(2,1)}), bf16[16,8,1536]{2,1,0:T(8,128)(2,1)S(1)}, u32[]{:S(2)}, u32[]{:S(2)}) async-start(bf16[16,8,1536]{2,1,0:T(8,128)(2,1)} %broadcast_in_dim.126), calls=%async_computation.3 | async-start | bytes 786432 | tf_op jit(solution)/shard_map/all_to_all | solution.py:154
  93.5 1.3 multiply_convert_fusion
  94.8 15.5 %all-to-all-done.3 = bf16[16,8,1536]{2,1,0:T(8,128)(2,1)S(1)} async-done(((bf16[16,8,1536]{2,1,0:T(8,128)(2,1)}), bf16[16,8,1536]{2,1,0:T(8,128)(2,1)S(1)}, u32[]{:S(2)}, u32[]{:S(2)}) %all-to-all-start.3) | async-done | bytes 393248 | tf_op jit(solution)/shard_map/all_to_all | solution.py:154
  110.3 3.6 %all-to-all-start.2 = ((bf16[16,32,768]{2,1,0:T(8,128)(2,1)}), bf16[16,32,768]{2,1,0:T(8,128)(2,1)S(1)}, u32[]{:S(2)}, u32[]{:S(2)}) async-start(bf16[16,32,768]{2,1,0:T(8,128)(2,1)} %bitcast.29), calls=%async_computation.2 | async-start | bytes 1572864 | tf_op jit(solution)/shard_map/all_to_all | solution.py:266
  113.9 1.9 pad_maximum_fusion
  115.8 1.7 constant_dynamic-slice_fusion.3
  117.5 9.7 %collective-permute-start.2 = (bf16[432,1536]{1,0:T(8,128)(2,1)}, bf16[432,1536]{1,0:T(8,128)(2,1)}, u32[]{:S(2)}, u32[]{:S(2)}) collective-permute-start(bf16[432,1536]{1,0:T(8,128)(2,1)} %get-tuple-element.30), channel_id=1, source_target_pairs={{0,1},{1,0},{2,3},{3,2},{4,5},{5,4},{6,7},{7,6},{8,9},{9,8},{10,11... | collective-permute-start | bytes 3981320 | tf_op jit(solution)/shard_map/ppermute | solution.py:137
  127.1 1.7 convolution_convert_fusion
  128.8 6.9 %all-to-all-start.4 = ((bf16[16,32,1536]{2,1,0:T(8,128)(2,1)}), bf16[16,32,1536]{2,1,0:T(8,128)(2,1)}, u32[]{:S(2)}, u32[]{:S(2)}) async-start(bf16[16,32,1536]{2,1,0:T(8,128)(2,1)} %bitcast.140), calls=%async_computation.4 | async-start | bytes 3145728 | tf_op jit(solution)/shard_map/all_to_all | solution.py:271
  135.8 2.9 collective-permute-start.3
  138.7 1.0 slice.66
  140.1 14.8 %collective-permute-done.3 = bf16[512,768]{1,0:T(8,128)(2,1)S(1)} collective-permute-done((bf16[512,768]{1,0:T(8,128)(2,1)S(1)}, bf16[512,768]{1,0:T(8,128)(2,1)S(1)}, u32[]{:S(2)}, u32[]{:S(2)}) %collective-permute-start.3) | collective-permute-done | bytes 786464 | tf_op jit(solution)/shard_map/ppermute | solution.py:166
  155.0 1.1 convolution_add_fusion.1
  156.6 2.4 fusion.13
  159.0 5.9 %collective-permute-start.4 = (f32[432,512]{1,0:T(8,128)S(1)}, f32[432,512]{1,0:T(8,128)S(1)}, u32[]{:S(2)}, u32[]{:S(2)}) collective-permute-start(f32[432,512]{1,0:T(8,128)S(1)} %pad_maximum_fusion.1), channel_id=1, source_target_pairs={{0,1},{1,0},{2,3},{3,2},{4,5},{5,4},{6,7},{7,6},{8,9},{9,8},{10,11... | collective-permute-start | bytes 2654216 | tf_op jit(solution)/shard_map/ppermute | solution.py:137
  165.8 2.1 fusion.16
  168.2 1.9 collective-permute-start.5
  170.2 1.5 collective-permute-done.5
  171.7 2.2 fusion.11
  173.9 1.0 fusion
  174.9 27.0 %all_to_all.45 = bf16[16,32,1536]{2,1,0:T(8,128)(2,1)S(1)} all-to-all(bf16[16,32,1536]{2,1,0:T(8,128)(2,1)S(1)} %bitcast.141), channel_id=1, replica_groups=mesh['seq'=16,'mp'=32] {'seq'}, dimensions={0} | all-to-all | bytes 3145728 | tf_op jit(solution)/shard_map/all_to_all | solution.py:298
  202.4 25.0 %all_to_all.46 = bf16[16,8,1536]{2,1,0:T(8,128)(2,1)S(1)} all-to-all(bf16[16,8,1536]{2,1,0:T(8,128)(2,1)S(1)} %fusion.2), channel_id=1, replica_groups={{0,2,4,6,8,10,12,14,16,18,20,22,24,26,28,30},{1,3,5,7,9,11,13,15,17,19,..., dimensions={0} | all-to-all | bytes 786432 | tf_op jit(solution)/shard_map/all_to_all | solution.py:170
  227.6 10.1 %psum.15 = f32[8,1]{0,1:T(1,128)S(1)} all-reduce(f32[8,1]{0,1:T(1,128)S(1)} %bitcast.171), channel_id=1, replica_groups={{0,1},{2,3},{4,5},{6,7},{8,9},{10,11},{12,13},{14,15},{16,17},{18,19},{..., use_global_device_ids=true, to_apply=%region_8.9 | all-reduce | flops 8 | bytes 64 | tf_op jit(solution)/shard_map/psum | solution.py:256
  237.8 0.8 broadcast_in_dim.128
  238.6 6.1 %all-to-all-start.7 = ((bf16[16,8,1536]{2,1,0:T(8,128)(2,1)}), bf16[16,8,1536]{2,1,0:T(8,128)(2,1)S(1)}, u32[]{:S(2)}, u32[]{:S(2)}) async-start(bf16[16,8,1536]{2,1,0:T(8,128)(2,1)} %broadcast_in_dim.128), calls=%async_computation.7 | async-start | bytes 786432 | tf_op jit(solution)/shard_map/all_to_all | solution.py:154
  244.8 17.1 %all-to-all-done.7 = bf16[16,8,1536]{2,1,0:T(8,128)(2,1)S(1)} async-done(((bf16[16,8,1536]{2,1,0:T(8,128)(2,1)}), bf16[16,8,1536]{2,1,0:T(8,128)(2,1)S(1)}, u32[]{:S(2)}, u32[]{:S(2)}) %all-to-all-start.7) | async-done | bytes 393248 | tf_op jit(solution)/shard_map/all_to_all | solution.py:154
  261.9 9.7 %collective-permute-start.6 = (bf16[128,1536]{1,0:T(8,128)(2,1)S(1)}, bf16[128,1536]{1,0:T(8,128)(2,1)S(1)}, u32[]{:S(2)}, u32[]{:S(2)}) collective-permute-start(bf16[128,1536]{1,0:T(8,128)(2,1)S(1)} %bitcast.146), channel_id=1, source_target_pairs={{0,1},{1,0},{2,3},{3,2},{4,5},{5,4},{6,7},{7,6},{8,9},{9,8},{10,11... | collective-permute-start | bytes 1179656 | tf_op jit(solution)/shard_map/ppermute | solution.py:137
  272.1 0.9 collective-permute-done.6
  274.0 1.2 broadcast_in_dim.130
  275.2 3.8 %all-to-all-start.8 = ((bf16[16,256,128]{2,1,0:T(8,128)(2,1)}), bf16[16,256,128]{2,1,0:T(8,128)(2,1)S(1)}, u32[]{:S(2)}, u32[]{:S(2)}) async-start(bf16[16,256,128]{2,1,0:T(8,128)(2,1)} %broadcast_in_dim.130), calls=%async_computation.8 | async-start | bytes 2097152 | tf_op jit(solution)/shard_map/all_to_all | solution.py:202
  279.1 0.8 fusion.64
  279.9 1.0 copy.47.key_in_ref
  281.2 0.7 copy.33
  282.0 0.7 constant_dynamic-slice_fusion.1
  283.4 12.7 %all-to-all-done.8.states_ref = bf16[16,256,128]{2,1,0:T(8,128)(2,1)S(1)} async-done(((bf16[16,256,128]{2,1,0:T(8,128)(2,1)}), bf16[16,256,128]{2,1,0:T(8,128)(2,1)S(1)}, u32[]{:S(2)}, u32[]{:S(2)}) %all-to-all-start.8) | async-done | bytes 1048608 | tf_op jit(solution)/shard_map/all_to_all | solution.py:202
  296.0 1.6 shard_map.157
  (135 shorter events, 9.9 us)
Async XLA Ops:
  0.6 26.4 %copy-start = (bf16[256,3072]{1,0:T(8,128)(2,1)S(1)}, bf16[256,3072]{1,0:T(8,128)(2,1)}, u32[]{:S(2)}) copy-start(bf16[256,3072]{1,0:T(8,128)(2,1)} %param.17) | copy-start | bytes 4718596
  1.5 14.8 %copy-start.3 = (f32[2]{0:T(128)S(1)}, f32[2]{0:T(128)}, u32[]{:S(2)}) copy-start(f32[2]{0:T(128)} %rate_ref.1) | copy-start | bytes 28
  1.6 14.8 %copy-start.2 = (bf16[128,256]{1,0:T(8,128)(2,1)S(1)}, bf16[128,256]{1,0:T(8,128)(2,1)}, u32[]{:S(2)}) copy-start(bf16[128,256]{1,0:T(8,128)(2,1)} %key_ref.1) | copy-start | bytes 196612
  1.6 15.1 %copy-start.19 = (bf16[128,256]{1,0:T(8,128)(2,1)S(1)}, bf16[128,256]{1,0:T(8,128)(2,1)}, u32[]{:S(2)}) copy-start(bf16[128,256]{1,0:T(8,128)(2,1)} %param.13) | copy-start | bytes 196612
  3.8 22.1 %all-to-all-start = ((bf16[16,256,128]{2,1,0:T(8,128)(2,1)}), bf16[16,256,128]{2,1,0:T(8,128)(2,1)S(1)}, u32[]{:S(2)}, u32[]{:S(2)}) async-start(bf16[16,256,128]{2,1,0:T(8,128)(2,1)} %shard_map.156), calls=%async_computation | async-start | bytes 2097152 | tf_op jit(solution)/shard_map/all_to_all | solution.py:202
  11.4 15.4 %copy-start.1 = (bf16[128,256]{1,0:T(8,128)(2,1)S(1)}, bf16[128,256]{1,0:T(8,128)(2,1)}, u32[]{:S(2)}) copy-start(bf16[128,256]{1,0:T(8,128)(2,1)} %value_ref.1) | copy-start | bytes 196612
  11.4 22.0 %collective-permute-start = (bf16[8,1536]{1,0:T(8,128)(2,1)S(1)}, bf16[8,1536]{1,0:T(8,128)(2,1)S(1)}, u32[]{:S(2)}, u32[]{:S(2)}) collective-permute-start(bf16[8,1536]{1,0:T(8,128)(2,1)S(1)} %constant_dynamic-slice_fusion.5), channel_id=1, source_target_pairs={{0,1},{1,0},{2,3},{3,2},{4,5},{5,4},{6,7},{7,6},{8,9},{9,8},{10,11... | collective-permute-start | bytes 73736 | tf_op jit(solution)/shard_map/ppermute | solution.py:137
  16.3 11.0 %copy-start.27 = (f32[2]{0:T(128)}, f32[2]{0:T(128)S(1)}, u32[]{:S(2)}) copy-start(f32[2]{0:T(128)S(1)} %get-tuple-element.42) | copy-start | bytes 28
  16.5 10.9 %copy-start.7 = (bf16[128,256]{0,1:T(8,128)(2,1)}, bf16[128,256]{0,1:T(8,128)(2,1)S(1)}, u32[]{:S(2)}) copy-start(bf16[128,256]{0,1:T(8,128)(2,1)S(1)} %copy.43) | copy-start | bytes 196612
  16.9 0.6 copy-start.15
  17.5 9.9 %copy-start.22 = (f32[128,2]{0,1:T(2,128)}, f32[128,2]{0,1:T(2,128)S(1)}, u32[]{:S(2)}) copy-start(f32[128,2]{0,1:T(2,128)S(1)} %multiply_exponential_fusion.1) | copy-start | bytes 3076
  17.6 9.8 %copy-start.20 = (pred[128,128]{1,0:T(8,128)(4,1)}, pred[128,128]{1,0:T(8,128)(4,1)S(1)}, u32[]{:S(2)}) copy-start(pred[128,128]{1,0:T(8,128)(4,1)S(1)} %subtract_compare_fusion) | copy-start | bytes 49156
  17.7 9.7 %copy-start.9 = (f32[128,128]{1,0:T(8,128)}, f32[128,128]{1,0:T(8,128)S(1)}, u32[]{:S(2)}) copy-start(f32[128,128]{1,0:T(8,128)S(1)} %subtract_select_fusion) | copy-start | bytes 196612
  27.4 7.3 %collective-permute-start.1 = (bf16[128,1536]{1,0:T(8,128)(2,1)S(1)}, bf16[128,1536]{1,0:T(8,128)(2,1)S(1)}, u32[]{:S(2)}, u32[]{:S(2)}) collective-permute-start(bf16[128,1536]{1,0:T(8,128)(2,1)S(1)} %convolution_convert_fusion.1), channel_id=1, source_target_pairs={{0,1},{1,0},{2,3},{3,2},{4,5},{5,4},{6,7},{7,6},{8,9},{9,8},{10,11... | collective-permute-start | bytes 1179656 | tf_op jit(solution)/shard_map/ppermute | solution.py:137
  33.4 2.5 copy-start.17
  35.0 16.0 %copy-start.24 = (f32[3072]{0:T(1024)S(1)}, f32[3072]{0:T(1024)}, u32[]{:S(2)}) copy-start(f32[3072]{0:T(1024)} %param.20) | copy-start | bytes 36868
  35.0 16.1 %copy-start.29 = (s32[128,2]{0,1:T(2,128)S(1)}, s32[128,2]{0,1:T(2,128)}, u32[]{:S(2)}) copy-start(s32[128,2]{0,1:T(2,128)} %param.21) | copy-start | bytes 3076
  35.9 57.3 %copy-start.30 = (f32[128,2]{0,1:T(2,128)S(1)}, f32[128,2]{0,1:T(2,128)}, u32[]{:S(2)}) copy-start(f32[128,2]{0,1:T(2,128)} %param.22) | copy-start | bytes 3076
  35.9 40.4 %all-to-all-start.1 = ((bf16[16,8,2304]{2,1,0:T(8,128)(2,1)}), bf16[16,8,2304]{2,1,0:T(8,128)(2,1)S(1)}, u32[]{:S(2)}, u32[]{:S(2)}) async-start(bf16[16,8,2304]{2,1,0:T(8,128)(2,1)} %pad_maximum_fusion.2), calls=%async_computation.1 | async-start | bytes 1179648 | tf_op jit(solution)/shard_map/all_to_all | solution.py:250
  51.1 43.7 %copy-start.13 = (f32[1536]{0:T(1024)}, f32[1536]{0:T(1024)S(1)}, u32[]{:S(2)}) copy-start(f32[1536]{0:T(1024)S(1)} %dynamic_slice.45) | copy-start | bytes 18436
  85.0 8.2 %copy-start.25 = (f32[8]{0:T(128)}, f32[8]{0:T(128)S(1)}, u32[]{:S(2)}) copy-start(f32[8]{0:T(128)S(1)} %rsqrt_bitcast_fusion) | copy-start | bytes 100
  85.9 24.4 %all-to-all-start.3 = ((bf16[16,8,1536]{2,1,0:T(8,128)(2,1)}), bf16[16,8,1536]{2,1,0:T(8,128)(2,1)S(1)}, u32[]{:S(2)}, u32[]{:S(2)}) async-start(bf16[16,8,1536]{2,1,0:T(8,128)(2,1)} %broadcast_in_dim.126), calls=%async_computation.3 | async-start | bytes 786432 | tf_op jit(solution)/shard_map/all_to_all | solution.py:154
  93.2 17.1 %copy-start.11 = (s32[16,128]{1,0:T(8,128)}, s32[16,128]{1,0:T(8,128)S(1)}, u32[]{:S(2)}) copy-start(s32[16,128]{1,0:T(8,128)S(1)} %copy.26) | copy-start | bytes 24580
  110.3 18.6 %all-to-all-start.2 = ((bf16[16,32,768]{2,1,0:T(8,128)(2,1)}), bf16[16,32,768]{2,1,0:T(8,128)(2,1)S(1)}, u32[]{:S(2)}, u32[]{:S(2)}) async-start(bf16[16,32,768]{2,1,0:T(8,128)(2,1)} %bitcast.29), calls=%async_computation.2 | async-start | bytes 1572864 | tf_op jit(solution)/shard_map/all_to_all | solution.py:266
  117.5 21.2 %collective-permute-start.2 = (bf16[432,1536]{1,0:T(8,128)(2,1)}, bf16[432,1536]{1,0:T(8,128)(2,1)}, u32[]{:S(2)}, u32[]{:S(2)}) collective-permute-start(bf16[432,1536]{1,0:T(8,128)(2,1)} %get-tuple-element.30), channel_id=1, source_target_pairs={{0,1},{1,0},{2,3},{3,2},{4,5},{5,4},{6,7},{7,6},{8,9},{9,8},{10,11... | collective-permute-start | bytes 3981320 | tf_op jit(solution)/shard_map/ppermute | solution.py:137
  128.8 27.7 %all-to-all-start.4 = ((bf16[16,32,1536]{2,1,0:T(8,128)(2,1)}), bf16[16,32,1536]{2,1,0:T(8,128)(2,1)}, u32[]{:S(2)}, u32[]{:S(2)}) async-start(bf16[16,32,1536]{2,1,0:T(8,128)(2,1)} %bitcast.140), calls=%async_computation.4 | async-start | bytes 3145728 | tf_op jit(solution)/shard_map/all_to_all | solution.py:271
  135.8 19.2 %collective-permute-start.3 = (bf16[512,768]{1,0:T(8,128)(2,1)S(1)}, bf16[512,768]{1,0:T(8,128)(2,1)S(1)}, u32[]{:S(2)}, u32[]{:S(2)}) collective-permute-start(bf16[512,768]{1,0:T(8,128)(2,1)S(1)} %bitcast.137), channel_id=1, source_target_pairs={{0,2},{1,3},{2,0},{3,1},{4,6},{5,7},{6,4},{7,5},{8,10},{9,11},{10,... | collective-permute-start | bytes 2359304 | tf_op jit(solution)/shard_map/ppermute | solution.py:166
  156.6 2.4 copy-start.5
  159.0 6.0 %copy-start.4 = (bf16[432,1536]{1,0:T(8,128)(2,1)S(1)}, bf16[432,1536]{1,0:T(8,128)(2,1)}, u32[]{:S(2)}) copy-start(bf16[432,1536]{1,0:T(8,128)(2,1)} %get-tuple-element.20) | copy-start | bytes 3981316
  159.0 8.8 %collective-permute-start.4 = (f32[432,512]{1,0:T(8,128)S(1)}, f32[432,512]{1,0:T(8,128)S(1)}, u32[]{:S(2)}, u32[]{:S(2)}) collective-permute-start(f32[432,512]{1,0:T(8,128)S(1)} %pad_maximum_fusion.1), channel_id=1, source_target_pairs={{0,1},{1,0},{2,3},{3,2},{4,5},{5,4},{6,7},{7,6},{8,9},{9,8},{10,11... | collective-permute-start | bytes 2654216 | tf_op jit(solution)/shard_map/ppermute | solution.py:137
  168.2 3.5 %collective-permute-start.5 = (bf16[288,512]{1,0:T(8,128)(2,1)S(1)}, bf16[288,512]{1,0:T(8,128)(2,1)S(1)}, u32[]{:S(2)}, u32[]{:S(2)}) collective-permute-start(bf16[288,512]{1,0:T(8,128)(2,1)S(1)} %pad_maximum_fusion.3), channel_id=1, source_target_pairs={{0,1},{1,0},{2,3},{3,2},{4,5},{5,4},{6,7},{7,6},{8,9},{9,8},{10,11... | collective-permute-start | bytes 884744 | tf_op jit(solution)/shard_map/ppermute | solution.py:137
  174.9 27.0 %copy-start.12 = (s32[16,128]{1,0:T(8,128)S(1)}, s32[16,128]{1,0:T(8,128)}, u32[]{:S(2)}) copy-start(s32[16,128]{1,0:T(8,128)} %copy-done.11) | copy-start | bytes 24580
  201.9 25.5 %copy-start.14 = (f32[1536]{0:T(1024)S(1)}, f32[1536]{0:T(1024)}, u32[]{:S(2)}) copy-start(f32[1536]{0:T(1024)} %copy-done.13) | copy-start | bytes 18436
  201.9 25.5 %copy-start.26 = (f32[8]{0:T(128)S(1)}, f32[8]{0:T(128)}, u32[]{:S(2)}) copy-start(f32[8]{0:T(128)} %copy-done.25) | copy-start | bytes 100
  201.9 35.8 %copy-start.16 = (bf16[4,1536]{1,0:T(4,128)(2,1)S(1)}, bf16[4,1536]{1,0:T(4,128)(2,1)}, u32[]{:S(2)}) copy-start(bf16[4,1536]{1,0:T(4,128)(2,1)} %copy-done.15) | copy-start | bytes 36868
  201.9 35.8 %copy-start.18 = (bf16[4,1536]{1,0:T(4,128)(2,1)S(1)}, bf16[4,1536]{1,0:T(4,128)(2,1)}, u32[]{:S(2)}) copy-start(bf16[4,1536]{1,0:T(4,128)(2,1)} %copy-done.17) | copy-start | bytes 36868
  202.3 42.4 %copy-start.28 = (f32[2]{0:T(128)S(1)}, f32[2]{0:T(128)}, u32[]{:S(2)}) copy-start(f32[2]{0:T(128)} %copy-done.27) | copy-start | bytes 28
  238.6 23.3 %all-to-all-start.7 = ((bf16[16,8,1536]{2,1,0:T(8,128)(2,1)}), bf16[16,8,1536]{2,1,0:T(8,128)(2,1)S(1)}, u32[]{:S(2)}, u32[]{:S(2)}) async-start(bf16[16,8,1536]{2,1,0:T(8,128)(2,1)} %broadcast_in_dim.128), calls=%async_computation.7 | async-start | bytes 786432 | tf_op jit(solution)/shard_map/all_to_all | solution.py:154
  261.9 11.0 %collective-permute-start.6 = (bf16[128,1536]{1,0:T(8,128)(2,1)S(1)}, bf16[128,1536]{1,0:T(8,128)(2,1)S(1)}, u32[]{:S(2)}, u32[]{:S(2)}) collective-permute-start(bf16[128,1536]{1,0:T(8,128)(2,1)S(1)} %bitcast.146), channel_id=1, source_target_pairs={{0,1},{1,0},{2,3},{3,2},{4,5},{5,4},{6,7},{7,6},{8,9},{9,8},{10,11... | collective-permute-start | bytes 1179656 | tf_op jit(solution)/shard_map/ppermute | solution.py:137
  271.6 2.0 copy-start.10
  271.6 2.0 copy-start.21
  272.9 2.3 copy-start.6
  275.2 5.7 %copy-start.23 = (f32[128,2]{0,1:T(2,128)S(1)}, f32[128,2]{0,1:T(2,128)}, u32[]{:S(2)}) copy-start(f32[128,2]{0,1:T(2,128)} %copy-done.22) | copy-start | bytes 3076
  275.2 5.9 %copy-start.8 = (bf16[128,256]{0,1:T(8,128)(2,1)S(1)}, bf16[128,256]{0,1:T(8,128)(2,1)}, u32[]{:S(2)}) copy-start(bf16[128,256]{0,1:T(8,128)(2,1)} %copy-done.7) | copy-start | bytes 196612
  275.2 20.8 %all-to-all-start.8 = ((bf16[16,256,128]{2,1,0:T(8,128)(2,1)}), bf16[16,256,128]{2,1,0:T(8,128)(2,1)S(1)}, u32[]{:S(2)}, u32[]{:S(2)}) async-start(bf16[16,256,128]{2,1,0:T(8,128)(2,1)} %broadcast_in_dim.130), calls=%async_computation.8 | async-start | bytes 2097152 | tf_op jit(solution)/shard_map/all_to_all | solution.py:202

commit v5 on v4

--- a/solution.py
+++ b/solution.py
@@ -255,12 +255,21 @@
         total = jnp.sum(x, axis=1, keepdims=True)
         return lax.psum(total, "mp", axis_index_groups=core_groups) / width
 
-    inverse = lax.rsqrt(over_features(stream * stream) + EPSILON)
+
+    stream_b = stream.astype(BF16)
+    weights_kept, weights_got, stream_b = lax.optimization_barrier(
+        (weights_kept, weights_got, stream_b)
+    )
+    both_weights = jnp.concatenate(
+        [weights_kept[: 2 * hidden_units], weights_got[: 2 * hidden_units]], axis=0
+    )
+    block_stream = spread_z(stream_b).astype(F32)
+    block_inverse = lax.rsqrt(over_features(block_stream * block_stream) + EPSILON)
+    group_in = (block_stream * block_inverse * gain).astype(BF16)
+    inverse = lax.dynamic_slice_in_dim(
+        block_inverse, lax.axis_index("mp") // 2 * pair_share, pair_share, 0
+    )
     normed = stream * inverse
-    expert_in = (normed * gain).astype(BF16)
-
-
-    group_in = spread_z(expert_in)
     outgoing = mm(placing, group_in).astype(BF16).reshape(seq_count, capacity, half)
     weighted = (slot_weight.reshape(-1, 1) * mm(placing, block_cot)).astype(BF16)
     cot_own = lax.all_to_all(
@@ -286,13 +295,12 @@
     grads = jnp.concatenate([gate_grad, up_grad], axis=0)
     grads_got = swap(grads)
 
-    def units_part(units, part):
-        return lax.dot_general(
-            units, part, (((0,), (0,)), ((), ())), preferred_element_type=F32
-        )
-
-    slots = units_part(grads, weights_kept[: 2 * hidden_units])
-    slots = slots + units_part(grads_got, weights_got[: 2 * hidden_units])
+    slots = lax.dot_general(
+        jnp.concatenate([grads, grads_got], axis=0),
+        both_weights,
+        (((0,), (0,)), ((), ())),
+        preferred_element_type=F32,
+    )
     slots = slots.astype(BF16).reshape(seq_count, capacity, half)
 
     returned = lax.all_to_all(slots, "seq", 0, 0, tiled=True).reshape(-1, half)

time: 299 us -> 295 us (0.987)
  blocking collectives: 70.6 us -> 47.4 us
  starting transfers between devices: 91.1 us -> 102 us
  waiting for transfers between devices: 97 us -> 105 us
    all_to_all x1 -> x0, blocking collectives: 25 us -> none  [sum_z(): lax.all_to_all(parts, 'mp', 0, 0, axis_index_groups=z_groups, tiled=True)]
    all_to_all x0 -> x1, waiting for transfers between devices: none -> 16.2 us  [sum_z(): lax.all_to_all(parts, 'mp', 0, 0, axis_index_groups=z_groups, tiled=True)]
    all_to_all x0 -> x1, starting transfers between devices: none -> 9.78 us  [sum_z(): lax.all_to_all(parts, 'mp', 0, 0, axis_index_groups=z_groups, tiled=True)]
    all_to_all x1, waiting for transfers between devices: 24.9 us -> 16.2 us  [body(): lax.all_to_all(sent, 'mp', 0, 0, axis_index_groups=z_groups, tiled=True)]
    ppermute x6, starting transfers between devices: 38 us -> 31.2 us  [swap(): return lax.ppermute(x, 'mp', swap_pairs)]
    all_to_all x2, starting transfers between devices: 13.3 us -> 19.2 us  [spread_z(): lax.all_to_all(copies, 'mp', 0, 0, axis_index_groups=z_groups, tiled=True)]
  transfers between devices with their start and end apart: 14 -> 15, of which waited for: 10 -> 11; matrix products, arithmetic and copies ran while one was open for 7% -> 8% of each run, Pallas kernels for 0% -> 0%
where the time goes in v5:
time: 295 us; the launch traced here: 294 us
  waiting for transfers between devices  105 us (36%)
  starting transfers between devices  102 us (35%)
  blocking collectives  47.4 us (16%)
  matrix products  16.1 us (5%)
  local copies, waits for them, and re-layouts  10.9 us (4%)
  other arithmetic  7.3 us (2%)
  Pallas kernels  3.79 us (1%)
    all_to_all x2, waiting for transfers between devices, spread_z(): lax.all_to_all(copies, 'mp', 0, 0, axis_index_groups=z_groups, tiled=True)  33 us
    ppermute x6, starting transfers between devices, swap(): return lax.ppermute(x, 'mp', swap_pairs)  31.2 us
    all_to_all x1, blocking collectives, body(): returned = lax.all_to_all(slots, 'seq', 0, 0, tiled=True).reshape(-1, half)  27.8 us
    all_to_all x2, waiting for transfers between devices, exchange_states(): return lax.all_to_all(sent, 'seq', 0, 0, tiled=True)  20.8 us
    psum x2, blocking collectives, over_features(): return lax.psum(total, 'mp', axis_index_groups=core_groups) / width  19.6 us
    all_to_all x2, starting transfers between devices, spread_z(): lax.all_to_all(copies, 'mp', 0, 0, axis_index_groups=z_groups, tiled=True)  19.2 us
    all_to_all x1, waiting for transfers between devices, body(): lax.all_to_all(sent, 'mp', 0, 0, axis_index_groups=z_groups, tiled=True)  16.2 us
    all_to_all x1, waiting for transfers between devices, sum_z(): lax.all_to_all(parts, 'mp', 0, 0, axis_index_groups=z_groups, tiled=True)  16.2 us
  transfers between devices with their start and end apart: 15, of which 11 were waited for; matrix products, arithmetic and copies ran while one was open for 8% of the time, Pallas kernels for 0%

profile of v5, /device:TPU:1, one launch (start us, length us, event | category | flops | bytes accessed | tf_op | source)
XLA Modules:
  0.0 293.6 jit_solution(8043576779792453743)
XLA Ops:
  0.6 0.9 pad_maximum_fusion.4
  1.6 2.2 shard_map.156
  3.8 7.6 %all-to-all-start = ((bf16[16,256,128]{2,1,0:T(8,128)(2,1)}), bf16[16,256,128]{2,1,0:T(8,128)(2,1)S(1)}, u32[]{:S(2)}, u32[]{:S(2)}) async-start(bf16[16,256,128]{2,1,0:T(8,128)(2,1)} %shard_map.156), calls=%async_computation | async-start | bytes 2097152 | tf_op jit(solution)/shard_map/all_to_all | solution.py:202
  11.4 4.9 %collective-permute-start.1 = (bf16[8,1536]{1,0:T(8,128)(2,1)S(1)}, bf16[8,1536]{1,0:T(8,128)(2,1)S(1)}, u32[]{:S(2)}, u32[]{:S(2)}) collective-permute-start(bf16[8,1536]{1,0:T(8,128)(2,1)S(1)} %constant_dynamic-slice_fusion.4), channel_id=1, source_target_pairs={{0,1},{1,0},{2,3},{3,2},{4,5},{5,4},{6,7},{7,6},{8,9},{9,8},{10,11... | collective-permute-start | bytes 73736 | tf_op jit(solution)/shard_map/ppermute | solution.py:137
  17.7 8.1 %all-to-all-done = bf16[16,256,128]{2,1,0:T(8,128)(2,1)S(1)} async-done(((bf16[16,256,128]{2,1,0:T(8,128)(2,1)}), bf16[16,256,128]{2,1,0:T(8,128)(2,1)S(1)}, u32[]{:S(2)}, u32[]{:S(2)}) %all-to-all-start) | async-done | bytes 1048608 | tf_op jit(solution)/shard_map/all_to_all | solution.py:202
  27.4 6.0 %collective-permute-start.2 = (bf16[128,1536]{1,0:T(8,128)(2,1)S(1)}, bf16[128,1536]{1,0:T(8,128)(2,1)S(1)}, u32[]{:S(2)}, u32[]{:S(2)}) collective-permute-start(bf16[128,1536]{1,0:T(8,128)(2,1)S(1)} %convolution_convert_fusion.2), channel_id=1, source_target_pairs={{0,1},{1,0},{2,3},{3,2},{4,5},{5,4},{6,7},{7,6},{8,9},{9,8},{10,11... | collective-permute-start | bytes 1179656 | tf_op jit(solution)/shard_map/ppermute | solution.py:137
  33.5 1.2 collective-permute-done.2
  35.0 0.9 pad_maximum_fusion.2
  35.9 15.0 %all-to-all-start.1 = ((bf16[16,8,2304]{2,1,0:T(8,128)(2,1)}), bf16[16,8,2304]{2,1,0:T(8,128)(2,1)S(1)}, u32[]{:S(2)}, u32[]{:S(2)}) async-start(bf16[16,8,2304]{2,1,0:T(8,128)(2,1)} %pad_maximum_fusion.2), calls=%async_computation.1 | async-start | bytes 1179648 | tf_op jit(solution)/shard_map/all_to_all | solution.py:250
  50.9 1.7 pad_maximum_fusion
  52.6 1.7 constant_dynamic-slice_fusion.5
  54.3 2.7 collective-permute-start
  57.3 2.7 collective-permute-done
  60.0 16.2 %all-to-all-done.1 = bf16[16,8,2304]{2,1,0:T(8,128)(2,1)S(1)} async-done(((bf16[16,8,2304]{2,1,0:T(8,128)(2,1)}), bf16[16,8,2304]{2,1,0:T(8,128)(2,1)S(1)}, u32[]{:S(2)}, u32[]{:S(2)}) %all-to-all-start.1) | async-done | bytes 589856 | tf_op jit(solution)/shard_map/all_to_all | solution.py:250
  76.3 0.8 broadcast_in_dim.118
  77.1 13.1 %all-to-all-start.2 = ((bf16[16,8,1536]{2,1,0:T(8,128)(2,1)}), bf16[16,8,1536]{2,1,0:T(8,128)(2,1)S(1)}, u32[]{:S(2)}, u32[]{:S(2)}) async-start(bf16[16,8,1536]{2,1,0:T(8,128)(2,1)} %broadcast_in_dim.118), calls=%async_computation.2 | async-start | bytes 786432 | tf_op jit(solution)/shard_map/all_to_all | solution.py:154
  90.6 1.3 multiply_convert_fusion
  91.8 15.9 %all-to-all-done.2 = bf16[16,8,1536]{2,1,0:T(8,128)(2,1)S(1)} async-done(((bf16[16,8,1536]{2,1,0:T(8,128)(2,1)}), bf16[16,8,1536]{2,1,0:T(8,128)(2,1)S(1)}, u32[]{:S(2)}, u32[]{:S(2)}) %all-to-all-start.2) | async-done | bytes 393248 | tf_op jit(solution)/shard_map/all_to_all | solution.py:154
  107.8 3.6 %all-to-all-start.3 = ((bf16[16,32,768]{2,1,0:T(8,128)(2,1)}), bf16[16,32,768]{2,1,0:T(8,128)(2,1)S(1)}, u32[]{:S(2)}, u32[]{:S(2)}) async-start(bf16[16,32,768]{2,1,0:T(8,128)(2,1)} %bitcast.143), calls=%async_computation.3 | async-start | bytes 1572864 | tf_op jit(solution)/shard_map/all_to_all | solution.py:275
  111.7 9.5 %psum.14 = f32[128,1]{0,1:T(1,128)S(1)} all-reduce(f32[128,1]{0,1:T(1,128)S(1)} %broadcast_in_dim.119), channel_id=1, replica_groups={{0,1},{2,3},{4,5},{6,7},{8,9},{10,11},{12,13},{14,15},{16,17},{18,19},{..., use_global_device_ids=true, to_apply=%region_3.4 | all-reduce | flops 128 | bytes 1024 | tf_op jit(solution)/shard_map/psum | solution.py:256
  121.8 1.8 convolution_convert_fusion.1
  123.6 6.9 %all-to-all-start.4 = ((bf16[16,32,1536]{2,1,0:T(8,128)(2,1)}), bf16[16,32,1536]{2,1,0:T(8,128)(2,1)}, u32[]{:S(2)}, u32[]{:S(2)}) async-start(bf16[16,32,1536]{2,1,0:T(8,128)(2,1)} %bitcast.138), calls=%async_computation.4 | async-start | bytes 3145728 | tf_op jit(solution)/shard_map/all_to_all | solution.py:280
  130.5 4.9 %collective-permute-start.3 = (bf16[512,768]{1,0:T(8,128)(2,1)S(1)}, bf16[512,768]{1,0:T(8,128)(2,1)S(1)}, u32[]{:S(2)}, u32[]{:S(2)}) collective-permute-start(bf16[512,768]{1,0:T(8,128)(2,1)S(1)} %bitcast.135), channel_id=1, source_target_pairs={{0,2},{1,3},{2,0},{3,1},{4,6},{5,7},{6,4},{7,5},{8,10},{9,11},{10,... | collective-permute-start | bytes 2359304 | tf_op jit(solution)/shard_map/ppermute | solution.py:166
  135.4 1.0 slice.66
  136.9 13.5 %collective-permute-done.3 = bf16[512,768]{1,0:T(8,128)(2,1)S(1)} collective-permute-done((bf16[512,768]{1,0:T(8,128)(2,1)S(1)}, bf16[512,768]{1,0:T(8,128)(2,1)S(1)}, u32[]{:S(2)}, u32[]{:S(2)}) %collective-permute-start.3) | collective-permute-done | bytes 786464 | tf_op jit(solution)/shard_map/ppermute | solution.py:166
  150.4 1.1 convolution_add_fusion
  151.5 2.4 fusion.71
  154.0 6.1 %collective-permute-start.4 = (f32[432,512]{1,0:T(8,128)S(1)}, f32[432,512]{1,0:T(8,128)S(1)}, u32[]{:S(2)}, u32[]{:S(2)}) collective-permute-start(f32[432,512]{1,0:T(8,128)S(1)} %pad_maximum_fusion.1), channel_id=1, source_target_pairs={{0,1},{1,0},{2,3},{3,2},{4,5},{5,4},{6,7},{7,6},{8,9},{9,8},{10,11... | collective-permute-start | bytes 2654216 | tf_op jit(solution)/shard_map/ppermute | solution.py:137
  160.9 2.1 fusion.73
  163.4 1.9 collective-permute-start.5
  165.4 1.2 slice.65
  166.8 1.4 convolution_convert_fusion
  168.3 27.8 %all_to_all.45 = bf16[16,32,1536]{2,1,0:T(8,128)(2,1)S(1)} all-to-all(bf16[16,32,1536]{2,1,0:T(8,128)(2,1)S(1)} %bitcast.146), channel_id=1, replica_groups=mesh['seq'=16,'mp'=32] {'seq'}, dimensions={0} | all-to-all | bytes 3145728 | tf_op jit(solution)/shard_map/all_to_all | solution.py:306
  196.1 1.2 fusion.1
  197.3 9.8 %all-to-all-start.6 = ((bf16[16,8,1536]{2,1,0:T(8,128)(2,1)}), bf16[16,8,1536]{2,1,0:T(8,128)(2,1)S(1)}, u32[]{:S(2)}, u32[]{:S(2)}) async-start(bf16[16,8,1536]{2,1,0:T(8,128)(2,1)} %fusion.1), calls=%async_computation.6 | async-start | bytes 786432 | tf_op jit(solution)/shard_map/all_to_all | solution.py:170
  207.2 16.2 %all-to-all-done.6 = bf16[16,8,1536]{2,1,0:T(8,128)(2,1)S(1)} async-done(((bf16[16,8,1536]{2,1,0:T(8,128)(2,1)}), bf16[16,8,1536]{2,1,0:T(8,128)(2,1)S(1)}, u32[]{:S(2)}, u32[]{:S(2)}) %all-to-all-start.6) | async-done | bytes 393248 | tf_op jit(solution)/shard_map/all_to_all | solution.py:170
  223.6 10.2 %psum.15 = f32[8,1]{0,1:T(1,128)S(1)} all-reduce(f32[8,1]{0,1:T(1,128)S(1)} %bitcast.169), channel_id=1, replica_groups={{0,1},{2,3},{4,5},{6,7},{8,9},{10,11},{12,13},{14,15},{16,17},{18,19},{..., use_global_device_ids=true, to_apply=%region_8.9 | all-reduce | flops 8 | bytes 64 | tf_op jit(solution)/shard_map/psum | solution.py:256
  233.9 0.8 broadcast_in_dim.128
  234.6 6.1 %all-to-all-start.7 = ((bf16[16,8,1536]{2,1,0:T(8,128)(2,1)}), bf16[16,8,1536]{2,1,0:T(8,128)(2,1)S(1)}, u32[]{:S(2)}, u32[]{:S(2)}) async-start(bf16[16,8,1536]{2,1,0:T(8,128)(2,1)} %broadcast_in_dim.128), calls=%async_computation.7 | async-start | bytes 786432 | tf_op jit(solution)/shard_map/all_to_all | solution.py:154
  240.9 17.1 %all-to-all-done.7 = bf16[16,8,1536]{2,1,0:T(8,128)(2,1)S(1)} async-done(((bf16[16,8,1536]{2,1,0:T(8,128)(2,1)}), bf16[16,8,1536]{2,1,0:T(8,128)(2,1)S(1)}, u32[]{:S(2)}, u32[]{:S(2)}) %all-to-all-start.7) | async-done | bytes 393248 | tf_op jit(solution)/shard_map/all_to_all | solution.py:154
  258.0 9.7 %collective-permute-start.6 = (bf16[128,1536]{1,0:T(8,128)(2,1)S(1)}, bf16[128,1536]{1,0:T(8,128)(2,1)S(1)}, u32[]{:S(2)}, u32[]{:S(2)}) collective-permute-start(bf16[128,1536]{1,0:T(8,128)(2,1)S(1)} %bitcast.144), channel_id=1, source_target_pairs={{0,1},{1,0},{2,3},{3,2},{4,5},{5,4},{6,7},{7,6},{8,9},{9,8},{10,11... | collective-permute-start | bytes 1179656 | tf_op jit(solution)/shard_map/ppermute | solution.py:137
  268.1 0.9 collective-permute-done.6
  270.0 1.2 broadcast_in_dim.130
  271.2 3.8 %all-to-all-start.8 = ((bf16[16,256,128]{2,1,0:T(8,128)(2,1)}), bf16[16,256,128]{2,1,0:T(8,128)(2,1)S(1)}, u32[]{:S(2)}, u32[]{:S(2)}) async-start(bf16[16,256,128]{2,1,0:T(8,128)(2,1)} %broadcast_in_dim.130), calls=%async_computation.8 | async-start | bytes 2097152 | tf_op jit(solution)/shard_map/all_to_all | solution.py:202
  275.1 0.8 fusion.78
  275.9 1.0 copy.81.key_in_ref
  279.4 12.7 %all-to-all-done.8.states_ref = bf16[16,256,128]{2,1,0:T(8,128)(2,1)S(1)} async-done(((bf16[16,256,128]{2,1,0:T(8,128)(2,1)}), bf16[16,256,128]{2,1,0:T(8,128)(2,1)S(1)}, u32[]{:S(2)}, u32[]{:S(2)}) %all-to-all-start.8) | async-done | bytes 1048608 | tf_op jit(solution)/shard_map/all_to_all | solution.py:202
  292.0 1.6 shard_map.157
  (140 shorter events, 11.3 us)
Async XLA Ops:
  0.6 26.4 %copy-start = (bf16[256,3072]{1,0:T(8,128)(2,1)S(1)}, bf16[256,3072]{1,0:T(8,128)(2,1)}, u32[]{:S(2)}) copy-start(bf16[256,3072]{1,0:T(8,128)(2,1)} %param.17) | copy-start | bytes 4718596
  1.5 14.8 %copy-start.3 = (f32[2]{0:T(128)S(1)}, f32[2]{0:T(128)}, u32[]{:S(2)}) copy-start(f32[2]{0:T(128)} %rate_ref.1) | copy-start | bytes 28
  1.6 14.8 %copy-start.2 = (bf16[128,256]{1,0:T(8,128)(2,1)S(1)}, bf16[128,256]{1,0:T(8,128)(2,1)}, u32[]{:S(2)}) copy-start(bf16[128,256]{1,0:T(8,128)(2,1)} %key_ref.1) | copy-start | bytes 196612
  1.6 15.1 %copy-start.20 = (bf16[128,256]{1,0:T(8,128)(2,1)S(1)}, bf16[128,256]{1,0:T(8,128)(2,1)}, u32[]{:S(2)}) copy-start(bf16[128,256]{1,0:T(8,128)(2,1)} %param.13) | copy-start | bytes 196612
  3.8 22.1 %all-to-all-start = ((bf16[16,256,128]{2,1,0:T(8,128)(2,1)}), bf16[16,256,128]{2,1,0:T(8,128)(2,1)S(1)}, u32[]{:S(2)}, u32[]{:S(2)}) async-start(bf16[16,256,128]{2,1,0:T(8,128)(2,1)} %shard_map.156), calls=%async_computation | async-start | bytes 2097152 | tf_op jit(solution)/shard_map/all_to_all | solution.py:202
  11.4 15.4 %copy-start.1 = (bf16[128,256]{1,0:T(8,128)(2,1)S(1)}, bf16[128,256]{1,0:T(8,128)(2,1)}, u32[]{:S(2)}) copy-start(bf16[128,256]{1,0:T(8,128)(2,1)} %value_ref.1) | copy-start | bytes 196612
  11.4 21.9 %collective-permute-start.1 = (bf16[8,1536]{1,0:T(8,128)(2,1)S(1)}, bf16[8,1536]{1,0:T(8,128)(2,1)S(1)}, u32[]{:S(2)}, u32[]{:S(2)}) collective-permute-start(bf16[8,1536]{1,0:T(8,128)(2,1)S(1)} %constant_dynamic-slice_fusion.4), channel_id=1, source_target_pairs={{0,1},{1,0},{2,3},{3,2},{4,5},{5,4},{6,7},{7,6},{8,9},{9,8},{10,11... | collective-permute-start | bytes 73736 | tf_op jit(solution)/shard_map/ppermute | solution.py:137
  16.3 11.0 %copy-start.26 = (f32[2]{0:T(128)}, f32[2]{0:T(128)S(1)}, u32[]{:S(2)}) copy-start(f32[2]{0:T(128)S(1)} %get-tuple-element.58) | copy-start | bytes 28
  16.5 9.4 %copy-start.8 = (bf16[128,256]{0,1:T(8,128)(2,1)}, bf16[128,256]{0,1:T(8,128)(2,1)S(1)}, u32[]{:S(2)}) copy-start(bf16[128,256]{0,1:T(8,128)(2,1)S(1)} %copy.77) | copy-start | bytes 196612
  16.9 0.6 copy-start.16
  17.0 10.4 %copy-start.23 = (f32[128,2]{0,1:T(2,128)}, f32[128,2]{0,1:T(2,128)S(1)}, u32[]{:S(2)}) copy-start(f32[128,2]{0,1:T(2,128)S(1)} %multiply_exponential_fusion.1) | copy-start | bytes 3076
  17.1 8.8 %copy-start.21 = (pred[128,128]{1,0:T(8,128)(4,1)}, pred[128,128]{1,0:T(8,128)(4,1)S(1)}, u32[]{:S(2)}) copy-start(pred[128,128]{1,0:T(8,128)(4,1)S(1)} %subtract_compare_fusion) | copy-start | bytes 49156
  17.2 10.2 %copy-start.10 = (f32[128,128]{1,0:T(8,128)}, f32[128,128]{1,0:T(8,128)S(1)}, u32[]{:S(2)}) copy-start(f32[128,128]{1,0:T(8,128)S(1)} %subtract_select_fusion) | copy-start | bytes 196612
  27.4 7.3 %collective-permute-start.2 = (bf16[128,1536]{1,0:T(8,128)(2,1)S(1)}, bf16[128,1536]{1,0:T(8,128)(2,1)S(1)}, u32[]{:S(2)}, u32[]{:S(2)}) collective-permute-start(bf16[128,1536]{1,0:T(8,128)(2,1)S(1)} %convolution_convert_fusion.2), channel_id=1, source_target_pairs={{0,1},{1,0},{2,3},{3,2},{4,5},{5,4},{6,7},{7,6},{8,9},{9,8},{10,11... | collective-permute-start | bytes 1179656 | tf_op jit(solution)/shard_map/ppermute | solution.py:137
  33.4 2.5 copy-start.18
  35.0 15.9 %copy-start.6 = (bf16[1,144,3072]{2,1,0:T(8,128)(2,1)S(1)}, bf16[1,144,3072]{2,1,0:T(8,128)(2,1)}, u32[]{:S(2)}) copy-start(bf16[1,144,3072]{2,1,0:T(8,128)(2,1)} %param.25) | copy-start | bytes 2654212
  35.9 40.3 %all-to-all-start.1 = ((bf16[16,8,2304]{2,1,0:T(8,128)(2,1)}), bf16[16,8,2304]{2,1,0:T(8,128)(2,1)S(1)}, u32[]{:S(2)}, u32[]{:S(2)}) async-start(bf16[16,8,2304]{2,1,0:T(8,128)(2,1)} %pad_maximum_fusion.2), calls=%async_computation.1 | async-start | bytes 1179648 | tf_op jit(solution)/shard_map/all_to_all | solution.py:250
  52.6 4.4 %copy-start.28 = (s32[128,2]{0,1:T(2,128)S(1)}, s32[128,2]{0,1:T(2,128)}, u32[]{:S(2)}) copy-start(s32[128,2]{0,1:T(2,128)} %param.21) | copy-start | bytes 3076
  54.3 35.9 %copy-start.29 = (f32[128,2]{0,1:T(2,128)S(1)}, f32[128,2]{0,1:T(2,128)}, u32[]{:S(2)}) copy-start(f32[128,2]{0,1:T(2,128)} %param.22) | copy-start | bytes 3076
  54.3 5.7 %collective-permute-start = (bf16[432,1536]{1,0:T(8,128)(2,1)}, bf16[432,1536]{1,0:T(8,128)(2,1)}, u32[]{:S(2)}, u32[]{:S(2)}) collective-permute-start(bf16[432,1536]{1,0:T(8,128)(2,1)} %get-tuple-element.44), channel_id=1, source_target_pairs={{0,1},{1,0},{2,3},{3,2},{4,5},{5,4},{6,7},{7,6},{8,9},{9,8},{10,11... | collective-permute-start | bytes 3981320 | tf_op jit(solution)/shard_map/ppermute | solution.py:137
  77.1 30.7 %all-to-all-start.2 = ((bf16[16,8,1536]{2,1,0:T(8,128)(2,1)}), bf16[16,8,1536]{2,1,0:T(8,128)(2,1)S(1)}, u32[]{:S(2)}, u32[]{:S(2)}) async-start(bf16[16,8,1536]{2,1,0:T(8,128)(2,1)} %broadcast_in_dim.118), calls=%async_computation.2 | async-start | bytes 786432 | tf_op jit(solution)/shard_map/all_to_all | solution.py:154
  90.1 21.3 %copy-start.25 = (f32[3072]{0:T(1024)S(1)}, f32[3072]{0:T(1024)}, u32[]{:S(2)}) copy-start(f32[3072]{0:T(1024)} %param.20) | copy-start | bytes 36868
  90.2 17.5 %copy-start.14 = (s32[16,128]{1,0:T(8,128)}, s32[16,128]{1,0:T(8,128)S(1)}, u32[]{:S(2)}) copy-start(s32[16,128]{1,0:T(8,128)S(1)} %copy.60) | copy-start | bytes 24580
  107.8 15.8 %all-to-all-start.3 = ((bf16[16,32,768]{2,1,0:T(8,128)(2,1)}), bf16[16,32,768]{2,1,0:T(8,128)(2,1)S(1)}, u32[]{:S(2)}, u32[]{:S(2)}) async-start(bf16[16,32,768]{2,1,0:T(8,128)(2,1)} %bitcast.143), calls=%async_computation.3 | async-start | bytes 1572864 | tf_op jit(solution)/shard_map/all_to_all | solution.py:275
  111.5 12.1 %copy-start.12 = (f32[1536]{0:T(1024)}, f32[1536]{0:T(1024)S(1)}, u32[]{:S(2)}) copy-start(f32[1536]{0:T(1024)S(1)} %dynamic_slice.49) | copy-start | bytes 18436
  123.6 27.9 %all-to-all-start.4 = ((bf16[16,32,1536]{2,1,0:T(8,128)(2,1)}), bf16[16,32,1536]{2,1,0:T(8,128)(2,1)}, u32[]{:S(2)}, u32[]{:S(2)}) async-start(bf16[16,32,1536]{2,1,0:T(8,128)(2,1)} %bitcast.138), calls=%async_computation.4 | async-start | bytes 3145728 | tf_op jit(solution)/shard_map/all_to_all | solution.py:280
  130.5 19.9 %collective-permute-start.3 = (bf16[512,768]{1,0:T(8,128)(2,1)S(1)}, bf16[512,768]{1,0:T(8,128)(2,1)S(1)}, u32[]{:S(2)}, u32[]{:S(2)}) collective-permute-start(bf16[512,768]{1,0:T(8,128)(2,1)S(1)} %bitcast.135), channel_id=1, source_target_pairs={{0,2},{1,3},{2,0},{3,1},{4,6},{5,7},{6,4},{7,5},{8,10},{9,11},{10,... | collective-permute-start | bytes 2359304 | tf_op jit(solution)/shard_map/ppermute | solution.py:166
  151.5 2.4 copy-start.5
  153.9 6.2 %copy-start.4 = (bf16[432,1536]{1,0:T(8,128)(2,1)S(1)}, bf16[432,1536]{1,0:T(8,128)(2,1)}, u32[]{:S(2)}) copy-start(bf16[432,1536]{1,0:T(8,128)(2,1)} %get-tuple-element.26) | copy-start | bytes 3981316
  154.0 9.0 %collective-permute-start.4 = (f32[432,512]{1,0:T(8,128)S(1)}, f32[432,512]{1,0:T(8,128)S(1)}, u32[]{:S(2)}, u32[]{:S(2)}) collective-permute-start(f32[432,512]{1,0:T(8,128)S(1)} %pad_maximum_fusion.1), channel_id=1, source_target_pairs={{0,1},{1,0},{2,3},{3,2},{4,5},{5,4},{6,7},{7,6},{8,9},{9,8},{10,11... | collective-permute-start | bytes 2654216 | tf_op jit(solution)/shard_map/ppermute | solution.py:137
  163.4 3.5 %collective-permute-start.5 = (bf16[288,512]{1,0:T(8,128)(2,1)S(1)}, bf16[288,512]{1,0:T(8,128)(2,1)S(1)}, u32[]{:S(2)}, u32[]{:S(2)}) collective-permute-start(bf16[288,512]{1,0:T(8,128)(2,1)S(1)} %pad_maximum_fusion.3), channel_id=1, source_target_pairs={{0,1},{1,0},{2,3},{3,2},{4,5},{5,4},{6,7},{7,6},{8,9},{9,8},{10,11... | collective-permute-start | bytes 884744 | tf_op jit(solution)/shard_map/ppermute | solution.py:137
  168.3 27.9 %copy-start.15 = (s32[16,128]{1,0:T(8,128)S(1)}, s32[16,128]{1,0:T(8,128)}, u32[]{:S(2)}) copy-start(s32[16,128]{1,0:T(8,128)} %copy-done.14) | copy-start | bytes 24580
  196.1 11.0 %copy-start.30 = (f32[128,1]{0,1:T(1,128)S(1)}, f32[128,1]{0,1:T(1,128)}, u32[]{:S(2)}) copy-start(f32[128,1]{0,1:T(1,128)} %get-tuple-element.56) | copy-start | bytes 1540
  196.1 27.3 %copy-start.13 = (f32[1536]{0:T(1024)S(1)}, f32[1536]{0:T(1024)}, u32[]{:S(2)}) copy-start(f32[1536]{0:T(1024)} %copy-done.12) | copy-start | bytes 18436
  196.1 37.7 %copy-start.17 = (bf16[4,1536]{1,0:T(4,128)(2,1)S(1)}, bf16[4,1536]{1,0:T(4,128)(2,1)}, u32[]{:S(2)}) copy-start(bf16[4,1536]{1,0:T(4,128)(2,1)} %copy-done.16) | copy-start | bytes 36868
  196.1 37.7 %copy-start.19 = (bf16[4,1536]{1,0:T(4,128)(2,1)S(1)}, bf16[4,1536]{1,0:T(4,128)(2,1)}, u32[]{:S(2)}) copy-start(bf16[4,1536]{1,0:T(4,128)(2,1)} %copy-done.18) | copy-start | bytes 36868
  197.3 43.5 %copy-start.27 = (f32[2]{0:T(128)S(1)}, f32[2]{0:T(128)}, u32[]{:S(2)}) copy-start(f32[2]{0:T(128)} %copy-done.26) | copy-start | bytes 28
  197.3 26.1 %all-to-all-start.6 = ((bf16[16,8,1536]{2,1,0:T(8,128)(2,1)}), bf16[16,8,1536]{2,1,0:T(8,128)(2,1)S(1)}, u32[]{:S(2)}, u32[]{:S(2)}) async-start(bf16[16,8,1536]{2,1,0:T(8,128)(2,1)} %fusion.1), calls=%async_computation.6 | async-start | bytes 786432 | tf_op jit(solution)/shard_map/all_to_all | solution.py:170
  234.6 23.3 %all-to-all-start.7 = ((bf16[16,8,1536]{2,1,0:T(8,128)(2,1)}), bf16[16,8,1536]{2,1,0:T(8,128)(2,1)S(1)}, u32[]{:S(2)}, u32[]{:S(2)}) async-start(bf16[16,8,1536]{2,1,0:T(8,128)(2,1)} %broadcast_in_dim.128), calls=%async_computation.7 | async-start | bytes 786432 | tf_op jit(solution)/shard_map/all_to_all | solution.py:154
  258.0 11.0 %collective-permute-start.6 = (bf16[128,1536]{1,0:T(8,128)(2,1)S(1)}, bf16[128,1536]{1,0:T(8,128)(2,1)S(1)}, u32[]{:S(2)}, u32[]{:S(2)}) collective-permute-start(bf16[128,1536]{1,0:T(8,128)(2,1)S(1)} %bitcast.144), channel_id=1, source_target_pairs={{0,1},{1,0},{2,3},{3,2},{4,5},{5,4},{6,7},{7,6},{8,9},{9,8},{10,11... | collective-permute-start | bytes 1179656 | tf_op jit(solution)/shard_map/ppermute | solution.py:137
  267.7 2.0 copy-start.11
  267.7 2.0 copy-start.22
  269.0 2.3 copy-start.7
  271.2 5.7 %copy-start.24 = (f32[128,2]{0,1:T(2,128)S(1)}, f32[128,2]{0,1:T(2,128)}, u32[]{:S(2)}) copy-start(f32[128,2]{0,1:T(2,128)} %copy-done.23) | copy-start | bytes 3076
  271.2 5.9 %copy-start.9 = (bf16[128,256]{0,1:T(8,128)(2,1)S(1)}, bf16[128,256]{0,1:T(8,128)(2,1)}, u32[]{:S(2)}) copy-start(bf16[128,256]{0,1:T(8,128)(2,1)} %copy-done.8) | copy-start | bytes 196612
  271.2 20.8 %all-to-all-start.8 = ((bf16[16,256,128]{2,1,0:T(8,128)(2,1)}), bf16[16,256,128]{2,1,0:T(8,128)(2,1)S(1)}, u32[]{:S(2)}, u32[]{:S(2)}) async-start(bf16[16,256,128]{2,1,0:T(8,128)(2,1)} %broadcast_in_dim.130), calls=%async_computation.8 | async-start | bytes 2097152 | tf_op jit(solution)/shard_map/all_to_all | solution.py:202

commit v6 on v5

--- a/solution.py
+++ b/solution.py
@@ -271,6 +271,11 @@
     )
     normed = stream * inverse
     outgoing = mm(placing, group_in).astype(BF16).reshape(seq_count, capacity, half)
+    adjoint_decay = jnp.exp(-decay_rates[:, None] * (places + 1.0)[None, :])[:, :, None]
+    first_token = lax.axis_index("mp") * tok_share
+    outgoing, inverse, normed, adjoint_decay, first_token = lax.optimization_barrier(
+        (outgoing, inverse, normed, adjoint_decay, first_token)
+    )
     weighted = (slot_weight.reshape(-1, 1) * mm(placing, block_cot)).astype(BF16)
     cot_own = lax.all_to_all(
         weighted.reshape(seq_count, capacity, half // 2), "seq", 0, 0, tiled=True
@@ -320,7 +325,7 @@
     local_adjoint = heads_dot(
         "htd,hte->hde",
         query_heads,
-        (jnp.exp(-decay_rates[:, None] * (places + 1.0)[None, :])[:, :, None] * grad_heads).astype(BF16),
+        (adjoint_decay * grad_heads).astype(BF16),
     ).astype(BF16)
     local_adjoint = local_adjoint.reshape(head_count * head_size, head_size)
     local_adjoint = jnp.broadcast_to(local_adjoint[None], (seq_count,) + local_adjoint.shape)
@@ -342,7 +347,9 @@
     )
 
     def own_tokens(x):
-        return lax.dynamic_slice_in_dim(x, lax.axis_index("mp") * tok_share, tok_share, 0)
+        return lax.dynamic_slice(
+            x, (first_token, 0), (tok_share, half), allow_negative_indices=False
+        )
 
     input_grad = by_core(own_tokens(block_own), own_tokens(block_other), 1)
     return (query_grad, key_grad, value_grad, input_grad)

time: 295 us -> 293 us (level)
  blocking collectives: 47.4 us -> 96.2 us
  waiting for transfers between devices: 105 us -> 70.9 us
  starting transfers between devices: 102 us -> 85.9 us
    all_to_all x0 -> x2, blocking collectives: none -> 48.9 us  [the longest x1 25.8 us: sum_z(): lax.all_to_all(parts, 'mp', 0, 0, axis_index_groups=z_groups, tiled=True)]
    all_to_all x2 -> x1, waiting for transfers between devices: 33 us -> 15.2 us  [spread_z(): lax.all_to_all(copies, 'mp', 0, 0, axis_index_groups=z_groups, tiled=True)]
    all_to_all x1 -> x0, waiting for transfers between devices: 16.2 us -> none  [sum_z(): lax.all_to_all(parts, 'mp', 0, 0, axis_index_groups=z_groups, tiled=True)]
    all_to_all x1 -> x0, starting transfers between devices: 9.78 us -> none  [sum_z(): lax.all_to_all(parts, 'mp', 0, 0, axis_index_groups=z_groups, tiled=True)]
    all_to_all x2 -> x1, starting transfers between devices: 19.2 us -> 13.1 us  [spread_z(): lax.all_to_all(copies, 'mp', 0, 0, axis_index_groups=z_groups, tiled=True)]
  transfers between devices with their start and end apart: 15 -> 13, of which waited for: 11 -> 9; matrix products, arithmetic and copies ran while one was open for 8% -> 8% of each run, Pallas kernels for 0% -> 0%
where the time goes in v6:
time: 293 us; the launch traced here: 291 us
  blocking collectives  96.2 us (33%)
  starting transfers between devices  85.9 us (29%)
  waiting for transfers between devices  70.9 us (24%)
  matrix products  16.1 us (5%)
  local copies, waits for them, and re-layouts  9.63 us (3%)
  other arithmetic  7.37 us (3%)
  Pallas kernels  3.8 us (1%)
    ppermute x6, starting transfers between devices, swap(): return lax.ppermute(x, 'mp', swap_pairs)  31.3 us
    all_to_all x1, blocking collectives, body(): returned = lax.all_to_all(slots, 'seq', 0, 0, tiled=True).reshape(-1, half)  27.7 us
    all_to_all x1, blocking collectives, sum_z(): lax.all_to_all(parts, 'mp', 0, 0, axis_index_groups=z_groups, tiled=True)  25.8 us
    all_to_all x1, blocking collectives, spread_z(): lax.all_to_all(copies, 'mp', 0, 0, axis_index_groups=z_groups, tiled=True)  23.1 us
    all_to_all x2, waiting for transfers between devices, exchange_states(): return lax.all_to_all(sent, 'seq', 0, 0, tiled=True)  21.1 us
    psum x2, blocking collectives, over_features(): return lax.psum(total, 'mp', axis_index_groups=core_groups) / width  19.6 us
    all_to_all x1, waiting for transfers between devices, body(): lax.all_to_all(sent, 'mp', 0, 0, axis_index_groups=z_groups, tiled=True)  16.1 us
    all_to_all x1, waiting for transfers between devices, spread_z(): lax.all_to_all(copies, 'mp', 0, 0, axis_index_groups=z_groups, tiled=True)  15.2 us
  transfers between devices with their start and end apart: 13, of which 9 were waited for; matrix products, arithmetic and copies ran while one was open for 8% of the time, Pallas kernels for 0%

profile of v6, /device:TPU:1, one launch (start us, length us, event | category | flops | bytes accessed | tf_op | source)
XLA Modules:
  0.0 291.4 jit_solution(18215836633732806000)
XLA Ops:
  0.6 0.9 pad_maximum_fusion.4
  1.6 2.2 shard_map.156
  3.8 7.6 %all-to-all-start = ((bf16[16,256,128]{2,1,0:T(8,128)(2,1)}), bf16[16,256,128]{2,1,0:T(8,128)(2,1)S(1)}, u32[]{:S(2)}, u32[]{:S(2)}) async-start(bf16[16,256,128]{2,1,0:T(8,128)(2,1)} %shard_map.156), calls=%async_computation | async-start | bytes 2097152 | tf_op jit(solution)/shard_map/all_to_all | solution.py:202
  11.4 4.9 %collective-permute-start.1 = (bf16[8,1536]{1,0:T(8,128)(2,1)S(1)}, bf16[8,1536]{1,0:T(8,128)(2,1)S(1)}, u32[]{:S(2)}, u32[]{:S(2)}) collective-permute-start(bf16[8,1536]{1,0:T(8,128)(2,1)S(1)} %constant_dynamic-slice_fusion.4), channel_id=1, source_target_pairs={{0,1},{1,0},{2,3},{3,2},{4,5},{5,4},{6,7},{7,6},{8,9},{9,8},{10,11... | collective-permute-start | bytes 73736 | tf_op jit(solution)/shard_map/ppermute | solution.py:137
  17.4 8.4 %all-to-all-done = bf16[16,256,128]{2,1,0:T(8,128)(2,1)S(1)} async-done(((bf16[16,256,128]{2,1,0:T(8,128)(2,1)}), bf16[16,256,128]{2,1,0:T(8,128)(2,1)S(1)}, u32[]{:S(2)}, u32[]{:S(2)}) %all-to-all-start) | async-done | bytes 1048608 | tf_op jit(solution)/shard_map/all_to_all | solution.py:202
  25.9 0.7 multiply_reduce_fusion
  27.4 6.0 %collective-permute-start.2 = (bf16[128,1536]{1,0:T(8,128)(2,1)S(1)}, bf16[128,1536]{1,0:T(8,128)(2,1)S(1)}, u32[]{:S(2)}, u32[]{:S(2)}) collective-permute-start(bf16[128,1536]{1,0:T(8,128)(2,1)S(1)} %convolution_convert_fusion.2), channel_id=1, source_target_pairs={{0,1},{1,0},{2,3},{3,2},{4,5},{5,4},{6,7},{7,6},{8,9},{9,8},{10,11... | collective-permute-start | bytes 1179656 | tf_op jit(solution)/shard_map/ppermute | solution.py:137
  33.5 1.2 collective-permute-done.2
  35.0 0.9 pad_maximum_fusion.2
  35.9 15.0 %all-to-all-start.1 = ((bf16[16,8,2304]{2,1,0:T(8,128)(2,1)}), bf16[16,8,2304]{2,1,0:T(8,128)(2,1)S(1)}, u32[]{:S(2)}, u32[]{:S(2)}) async-start(bf16[16,8,2304]{2,1,0:T(8,128)(2,1)} %pad_maximum_fusion.2), calls=%async_computation.1 | async-start | bytes 1179648 | tf_op jit(solution)/shard_map/all_to_all | solution.py:250
  50.9 1.7 pad_maximum_fusion
  52.6 1.7 constant_dynamic-slice_fusion.5
  54.3 2.7 collective-permute-start
  57.3 2.7 collective-permute-done
  60.0 16.1 %all-to-all-done.1 = bf16[16,8,2304]{2,1,0:T(8,128)(2,1)S(1)} async-done(((bf16[16,8,2304]{2,1,0:T(8,128)(2,1)}), bf16[16,8,2304]{2,1,0:T(8,128)(2,1)S(1)}, u32[]{:S(2)}, u32[]{:S(2)}) %all-to-all-start.1) | async-done | bytes 589856 | tf_op jit(solution)/shard_map/all_to_all | solution.py:250
  76.3 0.8 broadcast_in_dim.118
  77.1 13.1 %all-to-all-start.2 = ((bf16[16,8,1536]{2,1,0:T(8,128)(2,1)}), bf16[16,8,1536]{2,1,0:T(8,128)(2,1)S(1)}, u32[]{:S(2)}, u32[]{:S(2)}) async-start(bf16[16,8,1536]{2,1,0:T(8,128)(2,1)} %broadcast_in_dim.118), calls=%async_computation.2 | async-start | bytes 786432 | tf_op jit(solution)/shard_map/all_to_all | solution.py:154
  90.6 0.7 multiply_exponential_fusion
  91.3 1.2 multiply_convert_fusion
  92.6 15.2 %all-to-all-done.2 = bf16[16,8,1536]{2,1,0:T(8,128)(2,1)S(1)} async-done(((bf16[16,8,1536]{2,1,0:T(8,128)(2,1)}), bf16[16,8,1536]{2,1,0:T(8,128)(2,1)S(1)}, u32[]{:S(2)}, u32[]{:S(2)}) %all-to-all-start.2) | async-done | bytes 393248 | tf_op jit(solution)/shard_map/all_to_all | solution.py:154
  107.8 3.6 %all-to-all-start.3 = ((bf16[16,32,768]{2,1,0:T(8,128)(2,1)}), bf16[16,32,768]{2,1,0:T(8,128)(2,1)S(1)}, u32[]{:S(2)}, u32[]{:S(2)}) async-start(bf16[16,32,768]{2,1,0:T(8,128)(2,1)} %bitcast.145), calls=%async_computation.3 | async-start | bytes 1572864 | tf_op jit(solution)/shard_map/all_to_all | solution.py:280
  111.6 9.5 %psum.14 = f32[128,1]{0,1:T(1,128)S(1)} all-reduce(f32[128,1]{0,1:T(1,128)S(1)} %broadcast_in_dim.119), channel_id=1, replica_groups={{0,1},{2,3},{4,5},{6,7},{8,9},{10,11},{12,13},{14,15},{16,17},{18,19},{..., use_global_device_ids=true, to_apply=%region_4.5 | all-reduce | flops 128 | bytes 1024 | tf_op jit(solution)/shard_map/psum | solution.py:256
  121.8 1.8 convolution_convert_fusion.1
  123.7 6.9 %all-to-all-start.4 = ((bf16[16,32,1536]{2,1,0:T(8,128)(2,1)}), bf16[16,32,1536]{2,1,0:T(8,128)(2,1)}, u32[]{:S(2)}, u32[]{:S(2)}) async-start(bf16[16,32,1536]{2,1,0:T(8,128)(2,1)} %bitcast.140), calls=%async_computation.4 | async-start | bytes 3145728 | tf_op jit(solution)/shard_map/all_to_all | solution.py:285
  130.7 4.7 %collective-permute-start.3 = (bf16[512,768]{1,0:T(8,128)(2,1)S(1)}, bf16[512,768]{1,0:T(8,128)(2,1)S(1)}, u32[]{:S(2)}, u32[]{:S(2)}) collective-permute-start(bf16[512,768]{1,0:T(8,128)(2,1)S(1)} %bitcast.137), channel_id=1, source_target_pairs={{0,2},{1,3},{2,0},{3,1},{4,6},{5,7},{6,4},{7,5},{8,10},{9,11},{10,... | collective-permute-start | bytes 2359304 | tf_op jit(solution)/shard_map/ppermute | solution.py:166
  135.4 1.0 slice.66
  136.8 13.5 %collective-permute-done.3 = bf16[512,768]{1,0:T(8,128)(2,1)S(1)} collective-permute-done((bf16[512,768]{1,0:T(8,128)(2,1)S(1)}, bf16[512,768]{1,0:T(8,128)(2,1)S(1)}, u32[]{:S(2)}, u32[]{:S(2)}) %collective-permute-start.3) | collective-permute-done | bytes 786464 | tf_op jit(solution)/shard_map/ppermute | solution.py:166
  150.4 1.1 convolution_add_fusion
  151.5 2.4 fusion.71
  154.0 6.2 %collective-permute-start.4 = (f32[432,512]{1,0:T(8,128)S(1)}, f32[432,512]{1,0:T(8,128)S(1)}, u32[]{:S(2)}, u32[]{:S(2)}) collective-permute-start(f32[432,512]{1,0:T(8,128)S(1)} %pad_maximum_fusion.1), channel_id=1, source_target_pairs={{0,1},{1,0},{2,3},{3,2},{4,5},{5,4},{6,7},{7,6},{8,9},{9,8},{10,11... | collective-permute-start | bytes 2654216 | tf_op jit(solution)/shard_map/ppermute | solution.py:137
  161.1 2.1 fusion.73
  163.5 1.9 collective-permute-start.5
  165.5 1.2 slice.65
  167.0 1.4 convolution_convert_fusion
  168.4 27.7 %all_to_all.45 = bf16[16,32,1536]{2,1,0:T(8,128)(2,1)S(1)} all-to-all(bf16[16,32,1536]{2,1,0:T(8,128)(2,1)S(1)} %bitcast.148), channel_id=1, replica_groups=mesh['seq'=16,'mp'=32] {'seq'}, dimensions={0} | all-to-all | bytes 3145728 | tf_op jit(solution)/shard_map/all_to_all | solution.py:311
  196.5 25.8 %all_to_all.46 = bf16[16,8,1536]{2,1,0:T(8,128)(2,1)S(1)} all-to-all(bf16[16,8,1536]{2,1,0:T(8,128)(2,1)S(1)} %fusion.1), channel_id=1, replica_groups={{0,2,4,6,8,10,12,14,16,18,20,22,24,26,28,30},{1,3,5,7,9,11,13,15,17,19,..., dimensions={0} | all-to-all | bytes 786432 | tf_op jit(solution)/shard_map/all_to_all | solution.py:170
  222.5 10.1 %psum.15 = f32[8,1]{0,1:T(1,128)S(1)} all-reduce(f32[8,1]{0,1:T(1,128)S(1)} %bitcast.173), channel_id=1, replica_groups={{0,1},{2,3},{4,5},{6,7},{8,9},{10,11},{12,13},{14,15},{16,17},{18,19},{..., use_global_device_ids=true, to_apply=%region_8.9 | all-reduce | flops 8 | bytes 64 | tf_op jit(solution)/shard_map/psum | solution.py:256
  232.7 23.1 %all_to_all.47 = bf16[16,8,1536]{2,1,0:T(8,128)(2,1)S(1)} all-to-all(bf16[16,8,1536]{2,1,0:T(8,128)(2,1)S(1)} %broadcast_in_dim.128), channel_id=1, replica_groups={{0,2,4,6,8,10,12,14,16,18,20,22,24,26,28,30},{1,3,5,7,9,11,13,15,17,19,..., dimensions={0} | all-to-all | bytes 786432 | tf_op jit(solution)/shard_map/all_to_all | solution.py:154
  255.8 9.7 %collective-permute-start.6 = (bf16[128,1536]{1,0:T(8,128)(2,1)S(1)}, bf16[128,1536]{1,0:T(8,128)(2,1)S(1)}, u32[]{:S(2)}, u32[]{:S(2)}) collective-permute-start(bf16[128,1536]{1,0:T(8,128)(2,1)S(1)} %bitcast.146), channel_id=1, source_target_pairs={{0,1},{1,0},{2,3},{3,2},{4,5},{5,4},{6,7},{7,6},{8,9},{9,8},{10,11... | collective-permute-start | bytes 1179656 | tf_op jit(solution)/shard_map/ppermute | solution.py:137
  266.0 0.8 collective-permute-done.6
  267.9 1.2 broadcast_in_dim.130
  269.1 3.7 %all-to-all-start.8 = ((bf16[16,256,128]{2,1,0:T(8,128)(2,1)}), bf16[16,256,128]{2,1,0:T(8,128)(2,1)S(1)}, u32[]{:S(2)}, u32[]{:S(2)}) async-start(bf16[16,256,128]{2,1,0:T(8,128)(2,1)} %broadcast_in_dim.130), calls=%async_computation.8 | async-start | bytes 2097152 | tf_op jit(solution)/shard_map/all_to_all | solution.py:202
  273.2 0.8 fusion.5
  274.0 1.0 fusion.12
  275.0 0.7 copy.67
  275.8 0.8 constant_dynamic-slice_fusion.1
  277.2 12.6 %all-to-all-done.8.states_ref = bf16[16,256,128]{2,1,0:T(8,128)(2,1)S(1)} async-done(((bf16[16,256,128]{2,1,0:T(8,128)(2,1)}), bf16[16,256,128]{2,1,0:T(8,128)(2,1)S(1)}, u32[]{:S(2)}, u32[]{:S(2)}) %all-to-all-start.8) | async-done | bytes 1048608 | tf_op jit(solution)/shard_map/all_to_all | solution.py:202
  289.8 1.6 shard_map.157
  (130 shorter events, 9.2 us)
Async XLA Ops:
  0.6 26.4 %copy-start = (bf16[256,3072]{1,0:T(8,128)(2,1)S(1)}, bf16[256,3072]{1,0:T(8,128)(2,1)}, u32[]{:S(2)}) copy-start(bf16[256,3072]{1,0:T(8,128)(2,1)} %param.17) | copy-start | bytes 4718596
  1.5 14.8 %copy-start.3 = (f32[2]{0:T(128)S(1)}, f32[2]{0:T(128)}, u32[]{:S(2)}) copy-start(f32[2]{0:T(128)} %rate_ref.1) | copy-start | bytes 28
  1.6 14.8 %copy-start.2 = (bf16[128,256]{1,0:T(8,128)(2,1)S(1)}, bf16[128,256]{1,0:T(8,128)(2,1)}, u32[]{:S(2)}) copy-start(bf16[128,256]{1,0:T(8,128)(2,1)} %key_ref.1) | copy-start | bytes 196612
  1.6 15.1 %copy-start.13 = (bf16[128,256]{1,0:T(8,128)(2,1)S(1)}, bf16[128,256]{1,0:T(8,128)(2,1)}, u32[]{:S(2)}) copy-start(bf16[128,256]{1,0:T(8,128)(2,1)} %param.13) | copy-start | bytes 196612
  3.8 22.1 %all-to-all-start = ((bf16[16,256,128]{2,1,0:T(8,128)(2,1)}), bf16[16,256,128]{2,1,0:T(8,128)(2,1)S(1)}, u32[]{:S(2)}, u32[]{:S(2)}) async-start(bf16[16,256,128]{2,1,0:T(8,128)(2,1)} %shard_map.156), calls=%async_computation | async-start | bytes 2097152 | tf_op jit(solution)/shard_map/all_to_all | solution.py:202
  11.4 15.4 %copy-start.1 = (bf16[128,256]{1,0:T(8,128)(2,1)S(1)}, bf16[128,256]{1,0:T(8,128)(2,1)}, u32[]{:S(2)}) copy-start(bf16[128,256]{1,0:T(8,128)(2,1)} %value_ref.1) | copy-start | bytes 196612
  11.4 21.9 %collective-permute-start.1 = (bf16[8,1536]{1,0:T(8,128)(2,1)S(1)}, bf16[8,1536]{1,0:T(8,128)(2,1)S(1)}, u32[]{:S(2)}, u32[]{:S(2)}) collective-permute-start(bf16[8,1536]{1,0:T(8,128)(2,1)S(1)} %constant_dynamic-slice_fusion.4), channel_id=1, source_target_pairs={{0,1},{1,0},{2,3},{3,2},{4,5},{5,4},{6,7},{7,6},{8,9},{9,8},{10,11... | collective-permute-start | bytes 73736 | tf_op jit(solution)/shard_map/ppermute | solution.py:137
  16.4 74.2 %copy-start.20 = (f32[2]{0:T(128)}, f32[2]{0:T(128)S(1)}, u32[]{:S(2)}) copy-start(f32[2]{0:T(128)S(1)} %get-tuple-element.68) | copy-start | bytes 28
  16.5 9.4 %copy-start.8 = (bf16[128,256]{0,1:T(8,128)(2,1)}, bf16[128,256]{0,1:T(8,128)(2,1)S(1)}, u32[]{:S(2)}) copy-start(bf16[128,256]{0,1:T(8,128)(2,1)S(1)} %copy.77) | copy-start | bytes 196612
  17.0 10.4 %copy-start.18 = (f32[128,2]{0,1:T(2,128)}, f32[128,2]{0,1:T(2,128)S(1)}, u32[]{:S(2)}) copy-start(f32[128,2]{0,1:T(2,128)S(1)} %multiply_exponential_fusion.1) | copy-start | bytes 3076
  17.1 10.3 %copy-start.14 = (pred[128,128]{1,0:T(8,128)(4,1)}, pred[128,128]{1,0:T(8,128)(4,1)S(1)}, u32[]{:S(2)}) copy-start(pred[128,128]{1,0:T(8,128)(4,1)S(1)} %subtract_compare_fusion) | copy-start | bytes 49156
  17.2 10.2 %copy-start.9 = (f32[128,128]{1,0:T(8,128)}, f32[128,128]{1,0:T(8,128)S(1)}, u32[]{:S(2)}) copy-start(f32[128,128]{1,0:T(8,128)S(1)} %subtract_select_fusion) | copy-start | bytes 196612
  27.4 7.3 %collective-permute-start.2 = (bf16[128,1536]{1,0:T(8,128)(2,1)S(1)}, bf16[128,1536]{1,0:T(8,128)(2,1)S(1)}, u32[]{:S(2)}, u32[]{:S(2)}) collective-permute-start(bf16[128,1536]{1,0:T(8,128)(2,1)S(1)} %convolution_convert_fusion.2), channel_id=1, source_target_pairs={{0,1},{1,0},{2,3},{3,2},{4,5},{5,4},{6,7},{7,6},{8,9},{9,8},{10,11... | collective-permute-start | bytes 1179656 | tf_op jit(solution)/shard_map/ppermute | solution.py:137
  33.4 2.5 copy-start.11
  35.0 15.9 %copy-start.6 = (bf16[1,144,3072]{2,1,0:T(8,128)(2,1)S(1)}, bf16[1,144,3072]{2,1,0:T(8,128)(2,1)}, u32[]{:S(2)}) copy-start(bf16[1,144,3072]{2,1,0:T(8,128)(2,1)} %param.25) | copy-start | bytes 2654212
  35.9 40.3 %all-to-all-start.1 = ((bf16[16,8,2304]{2,1,0:T(8,128)(2,1)}), bf16[16,8,2304]{2,1,0:T(8,128)(2,1)S(1)}, u32[]{:S(2)}, u32[]{:S(2)}) async-start(bf16[16,8,2304]{2,1,0:T(8,128)(2,1)} %pad_maximum_fusion.2), calls=%async_computation.1 | async-start | bytes 1179648 | tf_op jit(solution)/shard_map/all_to_all | solution.py:250
  52.6 4.4 %copy-start.23 = (s32[128,2]{0,1:T(2,128)S(1)}, s32[128,2]{0,1:T(2,128)}, u32[]{:S(2)}) copy-start(s32[128,2]{0,1:T(2,128)} %param.21) | copy-start | bytes 3076
  54.3 35.8 %copy-start.24 = (f32[128,2]{0,1:T(2,128)S(1)}, f32[128,2]{0,1:T(2,128)}, u32[]{:S(2)}) copy-start(f32[128,2]{0,1:T(2,128)} %param.22) | copy-start | bytes 3076
  54.3 35.9 %copy-start.19 = (f32[3072]{0:T(1024)S(1)}, f32[3072]{0:T(1024)}, u32[]{:S(2)}) copy-start(f32[3072]{0:T(1024)} %param.20) | copy-start | bytes 36868
  54.3 5.7 %collective-permute-start = (bf16[432,1536]{1,0:T(8,128)(2,1)}, bf16[432,1536]{1,0:T(8,128)(2,1)}, u32[]{:S(2)}, u32[]{:S(2)}) collective-permute-start(bf16[432,1536]{1,0:T(8,128)(2,1)} %get-tuple-element.54), channel_id=1, source_target_pairs={{0,1},{1,0},{2,3},{3,2},{4,5},{5,4},{6,7},{7,6},{8,9},{9,8},{10,11... | collective-permute-start | bytes 3981320 | tf_op jit(solution)/shard_map/ppermute | solution.py:137
  77.1 30.7 %all-to-all-start.2 = ((bf16[16,8,1536]{2,1,0:T(8,128)(2,1)}), bf16[16,8,1536]{2,1,0:T(8,128)(2,1)S(1)}, u32[]{:S(2)}, u32[]{:S(2)}) async-start(bf16[16,8,1536]{2,1,0:T(8,128)(2,1)} %broadcast_in_dim.118), calls=%async_computation.2 | async-start | bytes 786432 | tf_op jit(solution)/shard_map/all_to_all | solution.py:154
  90.3 21.2 %copy-start.16 = (pred[16,128]{1,0:T(8,128)(4,1)}, pred[16,128]{1,0:T(8,128)(4,1)S(1)}, u32[]{:S(2)}) copy-start(pred[16,128]{1,0:T(8,128)(4,1)S(1)} %convert_compare_fusion) | copy-start | bytes 6148
  107.8 16.0 %all-to-all-start.3 = ((bf16[16,32,768]{2,1,0:T(8,128)(2,1)}), bf16[16,32,768]{2,1,0:T(8,128)(2,1)S(1)}, u32[]{:S(2)}, u32[]{:S(2)}) async-start(bf16[16,32,768]{2,1,0:T(8,128)(2,1)} %bitcast.145), calls=%async_computation.3 | async-start | bytes 1572864 | tf_op jit(solution)/shard_map/all_to_all | solution.py:280
  123.7 27.8 %all-to-all-start.4 = ((bf16[16,32,1536]{2,1,0:T(8,128)(2,1)}), bf16[16,32,1536]{2,1,0:T(8,128)(2,1)}, u32[]{:S(2)}, u32[]{:S(2)}) async-start(bf16[16,32,1536]{2,1,0:T(8,128)(2,1)} %bitcast.140), calls=%async_computation.4 | async-start | bytes 3145728 | tf_op jit(solution)/shard_map/all_to_all | solution.py:285
  130.7 19.7 %collective-permute-start.3 = (bf16[512,768]{1,0:T(8,128)(2,1)S(1)}, bf16[512,768]{1,0:T(8,128)(2,1)S(1)}, u32[]{:S(2)}, u32[]{:S(2)}) collective-permute-start(bf16[512,768]{1,0:T(8,128)(2,1)S(1)} %bitcast.137), channel_id=1, source_target_pairs={{0,2},{1,3},{2,0},{3,1},{4,6},{5,7},{6,4},{7,5},{8,10},{9,11},{10,... | collective-permute-start | bytes 2359304 | tf_op jit(solution)/shard_map/ppermute | solution.py:166
  151.5 2.4 copy-start.5
  153.9 6.3 %copy-start.4 = (bf16[432,1536]{1,0:T(8,128)(2,1)S(1)}, bf16[432,1536]{1,0:T(8,128)(2,1)}, u32[]{:S(2)}) copy-start(bf16[432,1536]{1,0:T(8,128)(2,1)} %get-tuple-element.32) | copy-start | bytes 3981316
  154.0 9.2 %collective-permute-start.4 = (f32[432,512]{1,0:T(8,128)S(1)}, f32[432,512]{1,0:T(8,128)S(1)}, u32[]{:S(2)}, u32[]{:S(2)}) collective-permute-start(f32[432,512]{1,0:T(8,128)S(1)} %pad_maximum_fusion.1), channel_id=1, source_target_pairs={{0,1},{1,0},{2,3},{3,2},{4,5},{5,4},{6,7},{7,6},{8,9},{9,8},{10,11... | collective-permute-start | bytes 2654216 | tf_op jit(solution)/shard_map/ppermute | solution.py:137
  163.5 3.5 %collective-permute-start.5 = (bf16[288,512]{1,0:T(8,128)(2,1)S(1)}, bf16[288,512]{1,0:T(8,128)(2,1)S(1)}, u32[]{:S(2)}, u32[]{:S(2)}) collective-permute-start(bf16[288,512]{1,0:T(8,128)(2,1)S(1)} %pad_maximum_fusion.3), channel_id=1, source_target_pairs={{0,1},{1,0},{2,3},{3,2},{4,5},{5,4},{6,7},{7,6},{8,9},{9,8},{10,11... | collective-permute-start | bytes 884744 | tf_op jit(solution)/shard_map/ppermute | solution.py:137
  168.4 27.7 %copy-start.17 = (pred[16,128]{1,0:T(8,128)(4,1)S(1)}, pred[16,128]{1,0:T(8,128)(4,1)}, u32[]{:S(2)}) copy-start(pred[16,128]{1,0:T(8,128)(4,1)} %copy-done.16) | copy-start | bytes 6148
  196.1 36.5 %copy-start.12 = (bf16[4,1536]{1,0:T(4,128)(2,1)S(1)}, bf16[4,1536]{1,0:T(4,128)(2,1)}, u32[]{:S(2)}) copy-start(bf16[4,1536]{1,0:T(4,128)(2,1)} %copy-done.11) | copy-start | bytes 36868
  196.1 36.5 %copy-start.25 = (f32[8,1]{0,1:T(1,128)S(1)}, f32[8,1]{0,1:T(1,128)}, u32[]{:S(2)}) copy-start(f32[8,1]{0,1:T(1,128)} %constant_dynamic-slice_fusion.3) | copy-start | bytes 100
  255.8 11.0 %collective-permute-start.6 = (bf16[128,1536]{1,0:T(8,128)(2,1)S(1)}, bf16[128,1536]{1,0:T(8,128)(2,1)S(1)}, u32[]{:S(2)}, u32[]{:S(2)}) collective-permute-start(bf16[128,1536]{1,0:T(8,128)(2,1)S(1)} %bitcast.146), channel_id=1, source_target_pairs={{0,1},{1,0},{2,3},{3,2},{4,5},{5,4},{6,7},{7,6},{8,9},{9,8},{10,11... | collective-permute-start | bytes 1179656 | tf_op jit(solution)/shard_map/ppermute | solution.py:137
  265.6 1.9 copy-start.10
  265.6 1.9 copy-start.15
  265.6 1.9 copy-start.21
  265.6 2.2 copy-start.22
  266.8 2.3 copy-start.7
  269.1 20.7 %all-to-all-start.8 = ((bf16[16,256,128]{2,1,0:T(8,128)(2,1)}), bf16[16,256,128]{2,1,0:T(8,128)(2,1)S(1)}, u32[]{:S(2)}, u32[]{:S(2)}) async-start(bf16[16,256,128]{2,1,0:T(8,128)(2,1)} %broadcast_in_dim.130), calls=%async_computation.8 | async-start | bytes 2097152 | tf_op jit(solution)/shard_map/all_to_all | solution.py:202

commit v7 on v6

--- a/solution.py
+++ b/solution.py
@@ -212,22 +212,23 @@
         decay_rates, key_rows, value_rows, seq_count, float(length), -1.0
     )
 
-    both = jnp.concatenate([inputs, cotangent], axis=0)
     hidden_units = w_down.shape[1]
-    both, gate_in, up_in, down_in, local_state = lax.optimization_barrier(
-        (both, w_gate[0], w_up[0], w_down[0], local_state)
+    inputs, cotangent, gate_in, up_in, down_in, local_state = lax.optimization_barrier(
+        (inputs, cotangent, w_gate[0], w_up[0], w_down[0], local_state)
     )
     weights = jnp.concatenate([gate_in.T, up_in.T, down_in], axis=0)
-    both_kept, both_got = own_half(both, 1), swap(other_half(both, 1))
     weights_kept, weights_got = lax.optimization_barrier(
         (own_half(weights, 1), swap(other_half(weights, 1)))
     )
-    pair_inputs = by_core(both_kept[:tok_share], both_got[:tok_share], 0).astype(F32)
-    pair_cot_b = by_core(both_kept[tok_share:], both_got[tok_share:], 0)
+    pair_inputs = by_core(own_half(inputs, 1), swap(other_half(inputs, 1)), 0).astype(F32)
+    pair_cot_b = by_core(own_half(cotangent, 1), swap(other_half(cotangent, 1)), 0)
+    gain = own_half(norm_gain, 0)[None, :]
+
+    states, pair_inputs, pair_cot_b = lax.optimization_barrier(
+        (exchange_states(local_state), pair_inputs, pair_cot_b)
+    )
     pair_cot = pair_cot_b.astype(F32)
-    gain = own_half(norm_gain, 0)[None, :]
-
-    entering = combine_states(exchange_states(local_state), seq_place - 1 - peers)
+    entering = combine_states(states, seq_place - 1 - peers)
     entering_b = entering.astype(BF16)
     scores = heads_dot("htd,hsd->hts", query_heads, key_heads) * decay_band
     scores_b = scores.astype(BF16)

time: 293 us -> 298 us (1.017)
  waiting for transfers between devices: 70.9 us -> 78 us
    all_to_all x2, waiting for transfers between devices: 21.1 us -> 28 us  [exchange_states(): return lax.all_to_all(sent, 'seq', 0, 0, tiled=True)]
    all_to_all x2, starting transfers between devices: 11.2 us -> 7.32 us  [exchange_states(): return lax.all_to_all(sent, 'seq', 0, 0, tiled=True)]
    ppermute x6 -> x7, starting transfers between devices: 31.3 us -> 35.1 us  [swap(): return lax.ppermute(x, 'mp', swap_pairs)]
  transfers between devices with their start and end apart: 13 -> 14, of which waited for: 9 -> 9; matrix products, arithmetic and copies ran while one was open for 8% -> 7% of each run, Pallas kernels for 0% -> 0%
where the time goes in v7:
time: 298 us; the launch traced here: 297 us
  blocking collectives  96.1 us (32%)
  starting transfers between devices  83.5 us (28%)
  waiting for transfers between devices  78 us (26%)
  matrix products  16.1 us (5%)
  local copies, waits for them, and re-layouts  11 us (4%)
  other arithmetic  6.49 us (2%)
  Pallas kernels  3.9 us (1%)
    ppermute x7, starting transfers between devices, swap(): return lax.ppermute(x, 'mp', swap_pairs)  35.1 us
    all_to_all x2, waiting for transfers between devices, exchange_states(): return lax.all_to_all(sent, 'seq', 0, 0, tiled=True)  28 us
    all_to_all x1, blocking collectives, body(): returned = lax.all_to_all(slots, 'seq', 0, 0, tiled=True).reshape(-1, half)  27.6 us
    all_to_all x1, blocking collectives, sum_z(): lax.all_to_all(parts, 'mp', 0, 0, axis_index_groups=z_groups, tiled=True)  25.8 us
    all_to_all x1, blocking collectives, spread_z(): lax.all_to_all(copies, 'mp', 0, 0, axis_index_groups=z_groups, tiled=True)  23.1 us
    psum x2, blocking collectives, over_features(): return lax.psum(total, 'mp', axis_index_groups=core_groups) / width  19.6 us
    all_to_all x1, waiting for transfers between devices, body(): lax.all_to_all(sent, 'mp', 0, 0, axis_index_groups=z_groups, tiled=True)  16.1 us
    all_to_all x1, waiting for transfers between devices, spread_z(): lax.all_to_all(copies, 'mp', 0, 0, axis_index_groups=z_groups, tiled=True)  15.2 us
  transfers between devices with their start and end apart: 14, of which 9 were waited for; matrix products, arithmetic and copies ran while one was open for 7% of the time, Pallas kernels for 0%

profile of v7, /device:TPU:1, one launch (start us, length us, event | category | flops | bytes accessed | tf_op | source)
XLA Modules:
  0.0 296.6 jit_solution(2401302420254795500)
XLA Ops:
  0.7 2.3 shard_map.156
  3.0 0.7 constant_dynamic-slice_fusion.4
  3.7 8.8 %collective-permute-start.2 = (bf16[4,1536]{1,0:T(4,128)(2,1)S(1)}, bf16[4,1536]{1,0:T(4,128)(2,1)S(1)}, u32[]{:S(2)}, u32[]{:S(2)}) collective-permute-start(bf16[4,1536]{1,0:T(4,128)(2,1)S(1)} %get-tuple-element.69), channel_id=1, source_target_pairs={{0,1},{1,0},{2,3},{3,2},{4,5},{5,4},{6,7},{7,6},{8,9},{9,8},{10,11... | collective-permute-start | bytes 36872 | tf_op jit(solution)/shard_map/ppermute | solution.py:137
  12.5 0.7 constant_dynamic-slice_fusion.6
  13.3 1.9 collective-permute-start.1
  15.2 3.7 %all-to-all-start = ((bf16[16,256,128]{2,1,0:T(8,128)(2,1)}), bf16[16,256,128]{2,1,0:T(8,128)(2,1)S(1)}, u32[]{:S(2)}, u32[]{:S(2)}) async-start(bf16[16,256,128]{2,1,0:T(8,128)(2,1)} %shard_map.156), calls=%async_computation | async-start | bytes 2097152 | tf_op jit(solution)/shard_map/all_to_all | solution.py:202
  20.0 15.4 %all-to-all-done = bf16[16,256,128]{2,1,0:T(8,128)(2,1)S(1)} async-done(((bf16[16,256,128]{2,1,0:T(8,128)(2,1)}), bf16[16,256,128]{2,1,0:T(8,128)(2,1)S(1)}, u32[]{:S(2)}, u32[]{:S(2)}) %all-to-all-start) | async-done | bytes 1048608 | tf_op jit(solution)/shard_map/all_to_all | solution.py:202
  36.9 3.8 %collective-permute-start.3 = (bf16[128,1536]{1,0:T(8,128)(2,1)S(1)}, bf16[128,1536]{1,0:T(8,128)(2,1)S(1)}, u32[]{:S(2)}, u32[]{:S(2)}) collective-permute-start(bf16[128,1536]{1,0:T(8,128)(2,1)S(1)} %convolution_convert_fusion.2), channel_id=1, source_target_pairs={{0,1},{1,0},{2,3},{3,2},{4,5},{5,4},{6,7},{7,6},{8,9},{9,8},{10,11... | collective-permute-start | bytes 1179656 | tf_op jit(solution)/shard_map/ppermute | solution.py:137
  40.7 1.3 collective-permute-done.3
  42.4 0.9 pad_maximum_fusion.2
  43.3 12.8 %all-to-all-start.1 = ((bf16[16,8,2304]{2,1,0:T(8,128)(2,1)}), bf16[16,8,2304]{2,1,0:T(8,128)(2,1)S(1)}, u32[]{:S(2)}, u32[]{:S(2)}) async-start(bf16[16,8,2304]{2,1,0:T(8,128)(2,1)} %pad_maximum_fusion.2), calls=%async_computation.1 | async-start | bytes 1179648 | tf_op jit(solution)/shard_map/all_to_all | solution.py:251
  56.1 1.7 pad_maximum_fusion
  57.8 1.7 constant_dynamic-slice_fusion.7
  59.5 2.7 collective-permute-start
  62.5 2.7 collective-permute-done
  65.2 16.1 %all-to-all-done.1 = bf16[16,8,2304]{2,1,0:T(8,128)(2,1)S(1)} async-done(((bf16[16,8,2304]{2,1,0:T(8,128)(2,1)}), bf16[16,8,2304]{2,1,0:T(8,128)(2,1)S(1)}, u32[]{:S(2)}, u32[]{:S(2)}) %all-to-all-start.1) | async-done | bytes 589856 | tf_op jit(solution)/shard_map/all_to_all | solution.py:251
  81.4 0.8 broadcast_in_dim.118
  82.2 13.1 %all-to-all-start.2 = ((bf16[16,8,1536]{2,1,0:T(8,128)(2,1)}), bf16[16,8,1536]{2,1,0:T(8,128)(2,1)S(1)}, u32[]{:S(2)}, u32[]{:S(2)}) async-start(bf16[16,8,1536]{2,1,0:T(8,128)(2,1)} %broadcast_in_dim.118), calls=%async_computation.2 | async-start | bytes 786432 | tf_op jit(solution)/shard_map/all_to_all | solution.py:154
  96.5 1.2 multiply_convert_fusion
  97.7 15.2 %all-to-all-done.2 = bf16[16,8,1536]{2,1,0:T(8,128)(2,1)S(1)} async-done(((bf16[16,8,1536]{2,1,0:T(8,128)(2,1)}), bf16[16,8,1536]{2,1,0:T(8,128)(2,1)S(1)}, u32[]{:S(2)}, u32[]{:S(2)}) %all-to-all-start.2) | async-done | bytes 393248 | tf_op jit(solution)/shard_map/all_to_all | solution.py:154
  113.0 3.6 %all-to-all-start.3 = ((bf16[16,32,768]{2,1,0:T(8,128)(2,1)}), bf16[16,32,768]{2,1,0:T(8,128)(2,1)S(1)}, u32[]{:S(2)}, u32[]{:S(2)}) async-start(bf16[16,32,768]{2,1,0:T(8,128)(2,1)} %bitcast.146), calls=%async_computation.3 | async-start | bytes 1572864 | tf_op jit(solution)/shard_map/all_to_all | solution.py:281
  116.8 9.5 %psum.14 = f32[128,1]{0,1:T(1,128)S(1)} all-reduce(f32[128,1]{0,1:T(1,128)S(1)} %broadcast_in_dim.119), channel_id=1, replica_groups={{0,1},{2,3},{4,5},{6,7},{8,9},{10,11},{12,13},{14,15},{16,17},{18,19},{..., use_global_device_ids=true, to_apply=%region_4.5 | all-reduce | flops 128 | bytes 1024 | tf_op jit(solution)/shard_map/psum | solution.py:257
  127.1 1.8 convolution_convert_fusion.1
  129.0 6.9 %all-to-all-start.4 = ((bf16[16,32,1536]{2,1,0:T(8,128)(2,1)}), bf16[16,32,1536]{2,1,0:T(8,128)(2,1)}, u32[]{:S(2)}, u32[]{:S(2)}) async-start(bf16[16,32,1536]{2,1,0:T(8,128)(2,1)} %bitcast.141), calls=%async_computation.4 | async-start | bytes 3145728 | tf_op jit(solution)/shard_map/all_to_all | solution.py:286
  135.9 4.7 %collective-permute-start.4 = (bf16[512,768]{1,0:T(8,128)(2,1)S(1)}, bf16[512,768]{1,0:T(8,128)(2,1)S(1)}, u32[]{:S(2)}, u32[]{:S(2)}) collective-permute-start(bf16[512,768]{1,0:T(8,128)(2,1)S(1)} %bitcast.138), channel_id=1, source_target_pairs={{0,2},{1,3},{2,0},{3,1},{4,6},{5,7},{6,4},{7,5},{8,10},{9,11},{10,... | collective-permute-start | bytes 2359304 | tf_op jit(solution)/shard_map/ppermute | solution.py:166
  140.6 1.0 slice.50
  142.0 13.5 %collective-permute-done.4 = bf16[512,768]{1,0:T(8,128)(2,1)S(1)} collective-permute-done((bf16[512,768]{1,0:T(8,128)(2,1)S(1)}, bf16[512,768]{1,0:T(8,128)(2,1)S(1)}, u32[]{:S(2)}, u32[]{:S(2)}) %collective-permute-start.4) | collective-permute-done | bytes 786464 | tf_op jit(solution)/shard_map/ppermute | solution.py:166
  155.6 1.1 convolution_add_fusion
  156.7 2.4 fusion.69
  159.2 6.3 %collective-permute-start.5 = (f32[432,512]{1,0:T(8,128)S(1)}, f32[432,512]{1,0:T(8,128)S(1)}, u32[]{:S(2)}, u32[]{:S(2)}) collective-permute-start(f32[432,512]{1,0:T(8,128)S(1)} %pad_maximum_fusion.1), channel_id=1, source_target_pairs={{0,1},{1,0},{2,3},{3,2},{4,5},{5,4},{6,7},{7,6},{8,9},{9,8},{10,11... | collective-permute-start | bytes 2654216 | tf_op jit(solution)/shard_map/ppermute | solution.py:137
  166.3 2.1 fusion.71
  168.7 1.9 collective-permute-start.6
  170.7 1.2 slice.49
  172.2 1.4 convolution_convert_fusion
  173.6 27.6 %all_to_all.45 = bf16[16,32,1536]{2,1,0:T(8,128)(2,1)S(1)} all-to-all(bf16[16,32,1536]{2,1,0:T(8,128)(2,1)S(1)} %bitcast.149), channel_id=1, replica_groups=mesh['seq'=16,'mp'=32] {'seq'}, dimensions={0} | all-to-all | bytes 3145728 | tf_op jit(solution)/shard_map/all_to_all | solution.py:312
  201.7 25.8 %all_to_all.46 = bf16[16,8,1536]{2,1,0:T(8,128)(2,1)S(1)} all-to-all(bf16[16,8,1536]{2,1,0:T(8,128)(2,1)S(1)} %fusion.1), channel_id=1, replica_groups={{0,2,4,6,8,10,12,14,16,18,20,22,24,26,28,30},{1,3,5,7,9,11,13,15,17,19,..., dimensions={0} | all-to-all | bytes 786432 | tf_op jit(solution)/shard_map/all_to_all | solution.py:170
  227.7 10.1 %psum.15 = f32[8,1]{0,1:T(1,128)S(1)} all-reduce(f32[8,1]{0,1:T(1,128)S(1)} %bitcast.175), channel_id=1, replica_groups={{0,1},{2,3},{4,5},{6,7},{8,9},{10,11},{12,13},{14,15},{16,17},{18,19},{..., use_global_device_ids=true, to_apply=%region_8.9 | all-reduce | flops 8 | bytes 64 | tf_op jit(solution)/shard_map/psum | solution.py:257
  237.9 23.1 %all_to_all.47 = bf16[16,8,1536]{2,1,0:T(8,128)(2,1)S(1)} all-to-all(bf16[16,8,1536]{2,1,0:T(8,128)(2,1)S(1)} %broadcast_in_dim.128), channel_id=1, replica_groups={{0,2,4,6,8,10,12,14,16,18,20,22,24,26,28,30},{1,3,5,7,9,11,13,15,17,19,..., dimensions={0} | all-to-all | bytes 786432 | tf_op jit(solution)/shard_map/all_to_all | solution.py:154
  261.1 9.7 %collective-permute-start.7 = (bf16[128,1536]{1,0:T(8,128)(2,1)S(1)}, bf16[128,1536]{1,0:T(8,128)(2,1)S(1)}, u32[]{:S(2)}, u32[]{:S(2)}) collective-permute-start(bf16[128,1536]{1,0:T(8,128)(2,1)S(1)} %bitcast.147), channel_id=1, source_target_pairs={{0,1},{1,0},{2,3},{3,2},{4,5},{5,4},{6,7},{7,6},{8,9},{9,8},{10,11... | collective-permute-start | bytes 1179656 | tf_op jit(solution)/shard_map/ppermute | solution.py:137
  271.2 0.8 collective-permute-done.7
  273.1 1.2 broadcast_in_dim.130
  274.4 3.7 %all-to-all-start.8 = ((bf16[16,256,128]{2,1,0:T(8,128)(2,1)}), bf16[16,256,128]{2,1,0:T(8,128)(2,1)S(1)}, u32[]{:S(2)}, u32[]{:S(2)}) async-start(bf16[16,256,128]{2,1,0:T(8,128)(2,1)} %broadcast_in_dim.130), calls=%async_computation.8 | async-start | bytes 2097152 | tf_op jit(solution)/shard_map/all_to_all | solution.py:202
  278.4 0.8 fusion.5
  279.2 1.0 fusion.12
  280.2 0.7 copy.64
  281.0 0.8 constant_dynamic-slice_fusion
  282.4 12.6 %all-to-all-done.8.states_ref = bf16[16,256,128]{2,1,0:T(8,128)(2,1)S(1)} async-done(((bf16[16,256,128]{2,1,0:T(8,128)(2,1)}), bf16[16,256,128]{2,1,0:T(8,128)(2,1)S(1)}, u32[]{:S(2)}, u32[]{:S(2)}) %all-to-all-start.8) | async-done | bytes 1048608 | tf_op jit(solution)/shard_map/all_to_all | solution.py:202
  295.0 1.6 shard_map.157
  (130 shorter events, 10.4 us)
Async XLA Ops:
  0.6 35.9 %copy-start = (bf16[256,3072]{1,0:T(8,128)(2,1)S(1)}, bf16[256,3072]{1,0:T(8,128)(2,1)}, u32[]{:S(2)}) copy-start(bf16[256,3072]{1,0:T(8,128)(2,1)} %param.17) | copy-start | bytes 4718596
  0.7 18.3 %copy-start.3 = (f32[2]{0:T(128)S(1)}, f32[2]{0:T(128)}, u32[]{:S(2)}) copy-start(f32[2]{0:T(128)} %rate_ref.1) | copy-start | bytes 28
  0.7 18.6 %copy-start.2 = (bf16[128,256]{1,0:T(8,128)(2,1)S(1)}, bf16[128,256]{1,0:T(8,128)(2,1)}, u32[]{:S(2)}) copy-start(bf16[128,256]{1,0:T(8,128)(2,1)} %key_ref.1) | copy-start | bytes 196612
  0.7 18.7 %copy-start.15 = (bf16[128,256]{1,0:T(8,128)(2,1)S(1)}, bf16[128,256]{1,0:T(8,128)(2,1)}, u32[]{:S(2)}) copy-start(bf16[128,256]{1,0:T(8,128)(2,1)} %param.13) | copy-start | bytes 196612
  3.7 16.2 %collective-permute-start.2 = (bf16[4,1536]{1,0:T(4,128)(2,1)S(1)}, bf16[4,1536]{1,0:T(4,128)(2,1)S(1)}, u32[]{:S(2)}, u32[]{:S(2)}) collective-permute-start(bf16[4,1536]{1,0:T(4,128)(2,1)S(1)} %get-tuple-element.69), channel_id=1, source_target_pairs={{0,1},{1,0},{2,3},{3,2},{4,5},{5,4},{6,7},{7,6},{8,9},{9,8},{10,11... | collective-permute-start | bytes 36872 | tf_op jit(solution)/shard_map/ppermute | solution.py:137
  13.3 6.7 %collective-permute-start.1 = (bf16[4,1536]{1,0:T(4,128)(2,1)S(1)}, bf16[4,1536]{1,0:T(4,128)(2,1)S(1)}, u32[]{:S(2)}, u32[]{:S(2)}) collective-permute-start(bf16[4,1536]{1,0:T(4,128)(2,1)S(1)} %get-tuple-element.71), channel_id=1, source_target_pairs={{0,1},{1,0},{2,3},{3,2},{4,5},{5,4},{6,7},{7,6},{8,9},{9,8},{10,11... | collective-permute-start | bytes 36872 | tf_op jit(solution)/shard_map/ppermute | solution.py:137
  15.2 20.2 %all-to-all-start = ((bf16[16,256,128]{2,1,0:T(8,128)(2,1)}), bf16[16,256,128]{2,1,0:T(8,128)(2,1)S(1)}, u32[]{:S(2)}, u32[]{:S(2)}) async-start(bf16[16,256,128]{2,1,0:T(8,128)(2,1)} %shard_map.156), calls=%async_computation | async-start | bytes 2097152 | tf_op jit(solution)/shard_map/all_to_all | solution.py:202
  18.9 17.4 %copy-start.1 = (bf16[128,256]{1,0:T(8,128)(2,1)S(1)}, bf16[128,256]{1,0:T(8,128)(2,1)}, u32[]{:S(2)}) copy-start(bf16[128,256]{1,0:T(8,128)(2,1)} %value_ref.1) | copy-start | bytes 196612
  18.9 17.9 %copy-start.20 = (f32[2]{0:T(128)}, f32[2]{0:T(128)S(1)}, u32[]{:S(2)}) copy-start(f32[2]{0:T(128)S(1)} %get-tuple-element.78) | copy-start | bytes 28
  19.1 17.8 %copy-start.9 = (f32[128,128]{1,0:T(8,128)}, f32[128,128]{1,0:T(8,128)S(1)}, u32[]{:S(2)}) copy-start(f32[128,128]{1,0:T(8,128)S(1)} %subtract_select_fusion) | copy-start | bytes 196612
  19.2 17.7 %copy-start.16 = (pred[128,128]{1,0:T(8,128)(4,1)}, pred[128,128]{1,0:T(8,128)(4,1)S(1)}, u32[]{:S(2)}) copy-start(pred[128,128]{1,0:T(8,128)(4,1)S(1)} %subtract_compare_fusion) | copy-start | bytes 49156
  19.4 16.0 %copy-start.8 = (bf16[128,256]{0,1:T(8,128)(2,1)}, bf16[128,256]{0,1:T(8,128)(2,1)S(1)}, u32[]{:S(2)}) copy-start(bf16[128,256]{0,1:T(8,128)(2,1)S(1)} %copy.74) | copy-start | bytes 196612
  19.8 17.1 %copy-start.18 = (f32[128,2]{0,1:T(2,128)}, f32[128,2]{0,1:T(2,128)S(1)}, u32[]{:S(2)}) copy-start(f32[128,2]{0,1:T(2,128)S(1)} %multiply_exponential_fusion.1) | copy-start | bytes 3076
  36.9 5.1 %collective-permute-start.3 = (bf16[128,1536]{1,0:T(8,128)(2,1)S(1)}, bf16[128,1536]{1,0:T(8,128)(2,1)S(1)}, u32[]{:S(2)}, u32[]{:S(2)}) collective-permute-start(bf16[128,1536]{1,0:T(8,128)(2,1)S(1)} %convolution_convert_fusion.2), channel_id=1, source_target_pairs={{0,1},{1,0},{2,3},{3,2},{4,5},{5,4},{6,7},{7,6},{8,9},{9,8},{10,11... | collective-permute-start | bytes 1179656 | tf_op jit(solution)/shard_map/ppermute | solution.py:137
  42.3 13.7 %copy-start.6 = (bf16[1,144,3072]{2,1,0:T(8,128)(2,1)S(1)}, bf16[1,144,3072]{2,1,0:T(8,128)(2,1)}, u32[]{:S(2)}) copy-start(bf16[1,144,3072]{2,1,0:T(8,128)(2,1)} %param.25) | copy-start | bytes 2654212
  43.3 38.1 %all-to-all-start.1 = ((bf16[16,8,2304]{2,1,0:T(8,128)(2,1)}), bf16[16,8,2304]{2,1,0:T(8,128)(2,1)S(1)}, u32[]{:S(2)}, u32[]{:S(2)}) async-start(bf16[16,8,2304]{2,1,0:T(8,128)(2,1)} %pad_maximum_fusion.2), calls=%async_computation.1 | async-start | bytes 1179648 | tf_op jit(solution)/shard_map/all_to_all | solution.py:251
  57.8 4.4 %copy-start.24 = (s32[128,2]{0,1:T(2,128)S(1)}, s32[128,2]{0,1:T(2,128)}, u32[]{:S(2)}) copy-start(s32[128,2]{0,1:T(2,128)} %param.21) | copy-start | bytes 3076
  59.5 35.8 %copy-start.25 = (f32[128,2]{0,1:T(2,128)S(1)}, f32[128,2]{0,1:T(2,128)}, u32[]{:S(2)}) copy-start(f32[128,2]{0,1:T(2,128)} %param.22) | copy-start | bytes 3076
  59.5 35.8 %copy-start.19 = (f32[3072]{0:T(1024)S(1)}, f32[3072]{0:T(1024)}, u32[]{:S(2)}) copy-start(f32[3072]{0:T(1024)} %param.20) | copy-start | bytes 36868
  59.5 36.3 %copy-start.21 = (f32[2]{0:T(128)S(1)}, f32[2]{0:T(128)}, u32[]{:S(2)}) copy-start(f32[2]{0:T(128)} %copy-done.20) | copy-start | bytes 28
  59.5 5.7 %collective-permute-start = (bf16[432,1536]{1,0:T(8,128)(2,1)}, bf16[432,1536]{1,0:T(8,128)(2,1)}, u32[]{:S(2)}, u32[]{:S(2)}) collective-permute-start(bf16[432,1536]{1,0:T(8,128)(2,1)} %get-tuple-element.64), channel_id=1, source_target_pairs={{0,1},{1,0},{2,3},{3,2},{4,5},{5,4},{6,7},{7,6},{8,9},{9,8},{10,11... | collective-permute-start | bytes 3981320 | tf_op jit(solution)/shard_map/ppermute | solution.py:137
  82.2 30.7 %all-to-all-start.2 = ((bf16[16,8,1536]{2,1,0:T(8,128)(2,1)}), bf16[16,8,1536]{2,1,0:T(8,128)(2,1)S(1)}, u32[]{:S(2)}, u32[]{:S(2)}) async-start(bf16[16,8,1536]{2,1,0:T(8,128)(2,1)} %broadcast_in_dim.118), calls=%async_computation.2 | async-start | bytes 786432 | tf_op jit(solution)/shard_map/all_to_all | solution.py:154
  95.5 31.6 %copy-start.13 = (f32[1536]{0:T(1024)}, f32[1536]{0:T(1024)S(1)}, u32[]{:S(2)}) copy-start(f32[1536]{0:T(1024)S(1)} %dynamic_slice.56) | copy-start | bytes 18436
  95.5 21.2 %copy-start.11 = (s32[16,128]{1,0:T(8,128)}, s32[16,128]{1,0:T(8,128)S(1)}, u32[]{:S(2)}) copy-start(s32[16,128]{1,0:T(8,128)S(1)} %copy.49) | copy-start | bytes 24580
  113.0 16.0 %all-to-all-start.3 = ((bf16[16,32,768]{2,1,0:T(8,128)(2,1)}), bf16[16,32,768]{2,1,0:T(8,128)(2,1)S(1)}, u32[]{:S(2)}, u32[]{:S(2)}) async-start(bf16[16,32,768]{2,1,0:T(8,128)(2,1)} %bitcast.146), calls=%async_computation.3 | async-start | bytes 1572864 | tf_op jit(solution)/shard_map/all_to_all | solution.py:281
  129.0 27.7 %all-to-all-start.4 = ((bf16[16,32,1536]{2,1,0:T(8,128)(2,1)}), bf16[16,32,1536]{2,1,0:T(8,128)(2,1)}, u32[]{:S(2)}, u32[]{:S(2)}) async-start(bf16[16,32,1536]{2,1,0:T(8,128)(2,1)} %bitcast.141), calls=%async_computation.4 | async-start | bytes 3145728 | tf_op jit(solution)/shard_map/all_to_all | solution.py:286
  135.9 19.7 %collective-permute-start.4 = (bf16[512,768]{1,0:T(8,128)(2,1)S(1)}, bf16[512,768]{1,0:T(8,128)(2,1)S(1)}, u32[]{:S(2)}, u32[]{:S(2)}) collective-permute-start(bf16[512,768]{1,0:T(8,128)(2,1)S(1)} %bitcast.138), channel_id=1, source_target_pairs={{0,2},{1,3},{2,0},{3,1},{4,6},{5,7},{6,4},{7,5},{8,10},{9,11},{10,... | collective-permute-start | bytes 2359304 | tf_op jit(solution)/shard_map/ppermute | solution.py:166
  156.7 2.4 copy-start.5
  159.1 6.3 %copy-start.4 = (bf16[432,1536]{1,0:T(8,128)(2,1)S(1)}, bf16[432,1536]{1,0:T(8,128)(2,1)}, u32[]{:S(2)}) copy-start(bf16[432,1536]{1,0:T(8,128)(2,1)} %get-tuple-element.40) | copy-start | bytes 3981316
  159.2 9.2 %collective-permute-start.5 = (f32[432,512]{1,0:T(8,128)S(1)}, f32[432,512]{1,0:T(8,128)S(1)}, u32[]{:S(2)}, u32[]{:S(2)}) collective-permute-start(f32[432,512]{1,0:T(8,128)S(1)} %pad_maximum_fusion.1), channel_id=1, source_target_pairs={{0,1},{1,0},{2,3},{3,2},{4,5},{5,4},{6,7},{7,6},{8,9},{9,8},{10,11... | collective-permute-start | bytes 2654216 | tf_op jit(solution)/shard_map/ppermute | solution.py:137
  168.7 3.5 %collective-permute-start.6 = (bf16[288,512]{1,0:T(8,128)(2,1)S(1)}, bf16[288,512]{1,0:T(8,128)(2,1)S(1)}, u32[]{:S(2)}, u32[]{:S(2)}) collective-permute-start(bf16[288,512]{1,0:T(8,128)(2,1)S(1)} %pad_maximum_fusion.3), channel_id=1, source_target_pairs={{0,1},{1,0},{2,3},{3,2},{4,5},{5,4},{6,7},{7,6},{8,9},{9,8},{10,11... | collective-permute-start | bytes 884744 | tf_op jit(solution)/shard_map/ppermute | solution.py:137
  173.6 27.7 %copy-start.12 = (s32[16,128]{1,0:T(8,128)S(1)}, s32[16,128]{1,0:T(8,128)}, u32[]{:S(2)}) copy-start(s32[16,128]{1,0:T(8,128)} %copy-done.11) | copy-start | bytes 24580
  201.3 26.2 %copy-start.14 = (f32[1536]{0:T(1024)S(1)}, f32[1536]{0:T(1024)}, u32[]{:S(2)}) copy-start(f32[1536]{0:T(1024)} %copy-done.13) | copy-start | bytes 18436
  201.3 36.5 %copy-start.26 = (f32[8,1]{0,1:T(1,128)S(1)}, f32[8,1]{0,1:T(1,128)}, u32[]{:S(2)}) copy-start(f32[8,1]{0,1:T(1,128)} %constant_dynamic-slice_fusion.2) | copy-start | bytes 100
  261.1 11.0 %collective-permute-start.7 = (bf16[128,1536]{1,0:T(8,128)(2,1)S(1)}, bf16[128,1536]{1,0:T(8,128)(2,1)S(1)}, u32[]{:S(2)}, u32[]{:S(2)}) collective-permute-start(bf16[128,1536]{1,0:T(8,128)(2,1)S(1)} %bitcast.147), channel_id=1, source_target_pairs={{0,1},{1,0},{2,3},{3,2},{4,5},{5,4},{6,7},{7,6},{8,9},{9,8},{10,11... | collective-permute-start | bytes 1179656 | tf_op jit(solution)/shard_map/ppermute | solution.py:137
  270.8 1.9 copy-start.10
  270.8 1.9 copy-start.17
  270.8 1.9 copy-start.22
  270.8 2.2 copy-start.23
  272.1 2.3 copy-start.7
  274.4 20.7 %all-to-all-start.8 = ((bf16[16,256,128]{2,1,0:T(8,128)(2,1)}), bf16[16,256,128]{2,1,0:T(8,128)(2,1)S(1)}, u32[]{:S(2)}, u32[]{:S(2)}) async-start(bf16[16,256,128]{2,1,0:T(8,128)(2,1)} %broadcast_in_dim.130), calls=%async_computation.8 | async-start | bytes 2097152 | tf_op jit(solution)/shard_map/all_to_all | solution.py:202
